TPU v7x, 32 devices: a whole 2x2x4 slice. The times are simulated.
32 devices in a mesh: dp: 16 (over z, x, core), tensor: 2 (over y).
Axes of the slice: x: 2, y: 2, z: 4, core: 2. Of those that a mesh axis runs over, the one named last changes fastest.
Arguments:
- frames: bfloat16 [128, 16, 1024], P('dp'), may hold values from -6 to 6
- cotangent: bfloat16 [128, 16, 1024], P('dp'), may hold values from -8 to 8
- dialogue: int32 [128], P('dp'), may hold values from 0 to 15, never falling along the last dimension, each value on 1 to 32 neighbouring positions
- padding: int32 [128], P('dp'), may hold values 0 or 1
- position_set: int32 [16], replicated, may hold values from 0 to 1, as said below
- query_weight: bfloat16 [2, 1024, 1024], P(None, 'dp', 'tensor'), may hold values from -0.1875 to 0.1875
- key_weight: bfloat16 [2, 1024, 1024], P(None, 'dp', 'tensor'), may hold values from -0.1875 to 0.1875
- value_weight: bfloat16 [2, 1024, 1024], P(None, 'dp', 'tensor'), may hold values from -0.1875 to 0.1875
- output_weight: bfloat16 [2, 1024, 1024], P(None, 'tensor', 'dp'), may hold values from -0.375 to 0.375
- gate_weight: bfloat16 [2, 1024, 2816], P(None, 'dp', 'tensor'), may hold values from -0.1875 to 0.1875
- up_weight: bfloat16 [2, 1024, 2816], P(None, 'dp', 'tensor'), may hold values from -0.1875 to 0.1875
- down_weight: bfloat16 [2, 2816, 1024], P(None, 'tensor', 'dp'), may hold values from -0.109375 to 0.109375
- attention_gain: float32 [2, 1024], replicated, may hold values from 0.25 to 1.75
- feedforward_gain: float32 [2, 1024], replicated, may hold values from 0.25 to 1.75
Outputs:
- mixed: bfloat16 [128, 16, 1024], P('dp')
- frames_grad: bfloat16 [128, 16, 1024], P('dp')
- query_grad: float32 [2, 1024, 1024], P(None, 'dp', 'tensor')
- key_grad: float32 [2, 1024, 1024], P(None, 'dp', 'tensor')
- value_grad: float32 [2, 1024, 1024], P(None, 'dp', 'tensor')
- output_grad: float32 [2, 1024, 1024], P(None, 'tensor', 'dp')
- gate_grad: float32 [2, 1024, 2816], P(None, 'dp', 'tensor')
- up_grad: float32 [2, 1024, 2816], P(None, 'dp', 'tensor')
- down_grad: float32 [2, 2816, 1024], P(None, 'tensor', 'dp')
- attention_gain_grad: float32 [2, 1024], P(None, 'dp')
- feedforward_gain_grad: float32 [2, 1024], P(None, 'dp')
Inputs may be any that keep to these rules, and one draw needn't show every extreme that they name: `position_set`: never falls along the positions; each of the 2 sets holds some position. `dialogue`: never falls along the frames; each dialogue holds 1 to 32 frames, and at least one dialogue holds exactly 32.
All inputs are finite; a program needn't handle non-finite values. No bound on the sum of `padding` on one device may be relied on, other than what follows from the above.
Results may differ from a plain program's by a relative error of at most 0.013.
Values may be sent and summed in bfloat16 or wider, within the bound.
A program may use at most 192 MiB of HBM per device.

v0:
```python
import jax
import jax.numpy as jnp
from jax import lax
from jax.sharding import PartitionSpec as P

HDIM = 64


epsilon = 1e-05


def select_masks(position_set, set_count):
    return [(position_set == set_index)[None, :, None] for set_index in range(set_count)]


def project(values, weight, set_masks):
    summed = None
    for set_index in range(weight.shape[0]):
        product_rows = jnp.einsum(
            "fpk,ke->fpe", values, weight[set_index], preferred_element_type=jnp.float32
        )
        product_rows = jnp.where(set_masks[set_index], product_rows, 0.0)
        summed = product_rows if summed is None else summed + product_rows
    return summed


def project_back(gradient, weight, set_masks):
    summed = None
    for set_index in range(weight.shape[0]):
        product_rows = jnp.einsum(
            "fpe,ke->fpk", gradient, weight[set_index], preferred_element_type=jnp.float32
        )
        product_rows = jnp.where(set_masks[set_index], product_rows, 0.0)
        summed = product_rows if summed is None else summed + product_rows
    return summed


def weight_gradient(values, gradient, set_masks):
    zero_low = jnp.zeros((), values.dtype)
    return jnp.stack(
        [
            jnp.einsum(
                "fpk,fpe->ke",
                jnp.where(set_mask, values, zero_low),
                gradient,
                preferred_element_type=jnp.float32,
            )
            for set_mask in set_masks
        ]
    )


def gain_gradient(gradient, unit_rows, set_masks):
    return jnp.stack(
        [
            jnp.sum(jnp.where(set_mask, gradient * unit_rows, 0.0), axis=(0, 1))
            for set_mask in set_masks
        ]
    )


def gain_rows(gain, set_masks):
    summed = None
    for set_index in range(gain.shape[0]):
        chosen = jnp.where(set_masks[set_index], gain[set_index][None, None, :], 0.0)
        summed = chosen if summed is None else summed + chosen
    return summed


def normalize(values, gain_full):
    inverse = lax.rsqrt(jnp.mean(values * values, axis=-1, keepdims=True) + epsilon)
    unit_rows = values * inverse
    return (unit_rows, inverse, (unit_rows * gain_full).astype(jnp.bfloat16))


def norm_back(gradient, gain_full, unit_rows, inverse):
    scaled = gradient * gain_full
    return inverse * (scaled - unit_rows * jnp.mean(scaled * unit_rows, axis=-1, keepdims=True))


def forward_pass(
    block_rows,
    set_masks,
    query_weight,
    key_weight,
    value_weight,
    output_weight,
    gate_weight,
    up_weight,
    down_weight,
    attention_gain,
    feedforward_gain,
):
    frame_count, positions, width = block_rows.shape
    local_heads = query_weight.shape[2] // HDIM
    head_shape = (frame_count, positions, local_heads, HDIM)
    scale = HDIM ** (-0.5)
    first_gain = gain_rows(attention_gain, set_masks)
    unit_one, inverse_one, normed_one = normalize(block_rows, first_gain)
    queries = project(normed_one, query_weight, set_masks).astype(jnp.bfloat16).reshape(head_shape)
    key_rows = project(normed_one, key_weight, set_masks).astype(jnp.bfloat16).reshape(head_shape)
    value_rows = (
        project(normed_one, value_weight, set_masks).astype(jnp.bfloat16).reshape(head_shape)
    )
    scores = (
        jnp.einsum("fphd,fqhd->fhpq", queries, key_rows, preferred_element_type=jnp.float32) * scale
    )
    causal = jnp.arange(positions)[:, None] >= jnp.arange(positions)[None, :]
    masked = jnp.where(causal, scores, -1e30)
    row_top = jnp.max(masked, axis=-1, keepdims=True)
    expo = jnp.exp(masked - row_top)
    probs = expo / jnp.sum(expo, axis=-1, keepdims=True)
    probs_low = probs.astype(jnp.bfloat16)
    attended = jnp.einsum(
        "fhpq,fqhd->fphd", probs_low, value_rows, preferred_element_type=jnp.float32
    )
    attended = attended.reshape(frame_count, positions, local_heads * HDIM).astype(jnp.bfloat16)
    attention = lax.psum(project(attended, output_weight, set_masks), "tensor")
    hidden = block_rows + attention
    second_gain = gain_rows(feedforward_gain, set_masks)
    unit_two, inverse_two, normed_two = normalize(hidden, second_gain)
    gated = project(normed_two, gate_weight, set_masks)
    upward = project(normed_two, up_weight, set_masks)
    active = (jax.nn.silu(gated) * upward).astype(jnp.bfloat16)
    branch = lax.psum(
        project(active, down_weight, set_masks).astype(jnp.bfloat16), "tensor"
    ).astype(jnp.float32)
    output = hidden + branch
    return (
        output,
        first_gain,
        unit_one,
        inverse_one,
        normed_one,
        queries,
        key_rows,
        value_rows,
        probs,
        probs_low,
        attended,
        second_gain,
        unit_two,
        inverse_two,
        normed_two,
        gated,
        upward,
        active,
    )


def per_device(
    frames,
    cotangent,
    dialogue,
    padding,
    position_set,
    query_weight,
    key_weight,
    value_weight,
    output_weight,
    gate_weight,
    up_weight,
    down_weight,
    attention_gain,
    feedforward_gain,
):
    query_weight, key_weight, value_weight, output_weight, gate_weight, up_weight, down_weight = (
        lax.all_gather(query_weight, "dp", axis=1, tiled=True),
        lax.all_gather(key_weight, "dp", axis=1, tiled=True),
        lax.all_gather(value_weight, "dp", axis=1, tiled=True),
        lax.all_gather(output_weight, "dp", axis=2, tiled=True),
        lax.all_gather(gate_weight, "dp", axis=1, tiled=True),
        lax.all_gather(up_weight, "dp", axis=1, tiled=True),
        lax.all_gather(down_weight, "dp", axis=2, tiled=True),
    )
    set_masks = select_masks(position_set, query_weight.shape[0])
    unpadded = padding.astype(jnp.float32)
    dialogue_total = lax.axis_size("dp")
    dialogue_table = (
        dialogue[:, None] == jnp.arange(dialogue_total, dtype=jnp.int32)[None, :]
    ).astype(jnp.float32)
    counts = lax.psum(jnp.sum(dialogue_table * unpadded[:, None], axis=0), "dp")
    loss_weight = (
        unpadded
        * (frames.shape[0] * 1.0)
        / (jnp.sum(dialogue_table * counts[None, :], axis=1) + 1.0)
    )
    weights = (
        query_weight,
        key_weight,
        value_weight,
        output_weight,
        gate_weight,
        up_weight,
        down_weight,
        attention_gain,
        feedforward_gain,
    )
    block_rows = frames.astype(jnp.float32)
    first = forward_pass(block_rows, set_masks, *weights)
    saved = forward_pass(block_rows, set_masks, *weights)
    (
        output,
        first_gain,
        unit_one,
        inverse_one,
        normed_one,
        queries,
        key_rows,
        value_rows,
        probs,
        probs_low,
        attended,
        second_gain,
        unit_two,
        inverse_two,
        normed_two,
        gated,
        upward,
        active,
    ) = saved
    frame_count, positions, width = block_rows.shape
    local_heads = query_weight.shape[2] // HDIM
    head_shape = (frame_count, positions, local_heads, HDIM)
    scale = HDIM ** (-0.5)
    seed = cotangent.astype(jnp.float32) * loss_weight[:, None, None]
    seed_low = seed.astype(jnp.bfloat16)
    down_grad = weight_gradient(active, seed_low, set_masks)
    active_grad = project_back(seed_low, down_weight, set_masks)
    sigmoid_gate = jax.nn.sigmoid(gated)
    gate_low_grad = (
        active_grad * upward * sigmoid_gate * (1.0 + gated * (1.0 - sigmoid_gate))
    ).astype(jnp.bfloat16)
    upward_low_grad = (active_grad * gated * sigmoid_gate).astype(jnp.bfloat16)
    gate_grad = weight_gradient(normed_two, gate_low_grad, set_masks)
    up_grad = weight_gradient(normed_two, upward_low_grad, set_masks)
    normed_two_part = project_back(gate_low_grad, gate_weight, set_masks) + project_back(
        upward_low_grad, up_weight, set_masks
    )
    normed_two_grad = lax.psum(normed_two_part, "tensor")
    feedforward_gain_grad = gain_gradient(normed_two_grad, unit_two, set_masks)
    hidden_grad = seed + norm_back(normed_two_grad, second_gain, unit_two, inverse_two)
    hidden_low = hidden_grad.astype(jnp.bfloat16)
    output_grad = weight_gradient(attended, hidden_low, set_masks)
    attended_grad = (
        project_back(hidden_low, output_weight, set_masks).astype(jnp.bfloat16).reshape(head_shape)
    )
    probs_grad = jnp.einsum(
        "fphd,fqhd->fhpq", attended_grad, value_rows, preferred_element_type=jnp.float32
    )
    values_low_grad = jnp.einsum(
        "fhpq,fphd->fqhd", probs_low, attended_grad, preferred_element_type=jnp.float32
    ).astype(jnp.bfloat16)
    scores_grad = (
        probs * (probs_grad - jnp.sum(probs_grad * probs, axis=-1, keepdims=True))
    ).astype(jnp.bfloat16)
    queries_low_grad = (
        jnp.einsum("fhpq,fqhd->fphd", scores_grad, key_rows, preferred_element_type=jnp.float32)
        * scale
    ).astype(jnp.bfloat16)
    keys_low_grad = (
        jnp.einsum("fhpq,fphd->fqhd", scores_grad, queries, preferred_element_type=jnp.float32)
        * scale
    ).astype(jnp.bfloat16)
    flat_shape = (frame_count, positions, local_heads * HDIM)
    queries_low_grad = queries_low_grad.reshape(flat_shape)
    keys_low_grad = keys_low_grad.reshape(flat_shape)
    values_low_grad = values_low_grad.reshape(flat_shape)
    query_grad = weight_gradient(normed_one, queries_low_grad, set_masks)
    key_grad = weight_gradient(normed_one, keys_low_grad, set_masks)
    value_grad = weight_gradient(normed_one, values_low_grad, set_masks)
    normed_one_part = (
        project_back(queries_low_grad, query_weight, set_masks)
        + project_back(keys_low_grad, key_weight, set_masks)
        + project_back(values_low_grad, value_weight, set_masks)
    )
    normed_one_grad = lax.psum(normed_one_part.astype(jnp.bfloat16), "tensor").astype(jnp.float32)
    attention_gain_grad = gain_gradient(normed_one_grad, unit_one, set_masks)
    frames_grad = (
        hidden_grad + norm_back(normed_one_grad, first_gain, unit_one, inverse_one)
    ).astype(jnp.bfloat16)
    summed_all = (
        lax.psum_scatter(query_grad, "dp", scatter_dimension=1, tiled=True),
        lax.psum_scatter(key_grad, "dp", scatter_dimension=1, tiled=True),
        lax.psum_scatter(value_grad, "dp", scatter_dimension=1, tiled=True),
        lax.psum_scatter(output_grad, "dp", scatter_dimension=2, tiled=True),
        lax.psum_scatter(gate_grad, "dp", scatter_dimension=1, tiled=True),
        lax.psum_scatter(up_grad, "dp", scatter_dimension=1, tiled=True),
        lax.psum_scatter(down_grad, "dp", scatter_dimension=2, tiled=True),
        lax.psum_scatter(attention_gain_grad, "dp", scatter_dimension=1, tiled=True),
        lax.psum_scatter(feedforward_gain_grad, "dp", scatter_dimension=1, tiled=True),
    )
    (
        query_sum,
        key_sum,
        value_sum,
        output_sum,
        gate_sum,
        up_sum,
        down_sum,
        attention_gain_sum,
        feedforward_gain_sum,
    ) = summed_all
    mixed = first[0].astype(jnp.bfloat16)
    return (
        mixed,
        frames_grad,
        query_sum,
        key_sum,
        value_sum,
        output_sum,
        gate_sum,
        up_sum,
        down_sum,
        attention_gain_sum,
        feedforward_gain_sum,
    )


def solution(mesh):
    in_specs = (
        P("dp", None, None),
        P("dp", None, None),
        P("dp"),
        P("dp"),
        P(),
        P(None, "dp", "tensor"),
        P(None, "dp", "tensor"),
        P(None, "dp", "tensor"),
        P(None, "tensor", "dp"),
        P(None, "dp", "tensor"),
        P(None, "dp", "tensor"),
        P(None, "tensor", "dp"),
        P(),
        P(),
    )
    out_specs = (
        P("dp", None, None),
        P("dp", None, None),
        P(None, "dp", "tensor"),
        P(None, "dp", "tensor"),
        P(None, "dp", "tensor"),
        P(None, "tensor", "dp"),
        P(None, "dp", "tensor"),
        P(None, "dp", "tensor"),
        P(None, "tensor", "dp"),
        P(None, "dp"),
        P(None, "dp"),
    )
    return jax.shard_map(
        per_device, mesh=mesh, in_specs=in_specs, out_specs=out_specs, check_vma=False
    )
```

profile of v0, /device:TPU:0, one launch (start us, length us, event | category | flops | bytes accessed | tf_op | source)
XLA Modules:
  0.0 1408.3 jit_solution(11464318121716572430)
XLA Ops:
  15.7 38.6 %all-gather.8.cloned.1.call-done = bf16[2,1024,512]{2,1,0:T(8,128)(2,1)} async-done(((bf16[2,64,512]{2,1,0:T(8,128)(2,1)}), bf16[2,1024,512]{2,1,0:T(8,128)(2,1)}) %all-gather.8.cloned.1.call-update) | async-done | bytes 2097168 | tf_op jit(solution)/shard_map/all_gather | solution.py:170
  57.6 39.1 %all-gather.12.cloned.1.call-done = bf16[2,1024,512]{2,1,0:T(8,128)(2,1)} async-done(((bf16[2,64,512]{2,1,0:T(8,128)(2,1)}), bf16[2,1024,512]{2,1,0:T(8,128)(2,1)}) %all-gather.12.cloned.1.call-update) | async-done | bytes 2097168 | tf_op jit(solution)/shard_map/all_gather | solution.py:169
  99.9 39.1 %all-gather.10.cloned.1.call-done = bf16[2,1024,512]{2,1,0:T(8,128)(2,1)} async-done(((bf16[2,64,512]{2,1,0:T(8,128)(2,1)}), bf16[2,1024,512]{2,1,0:T(8,128)(2,1)}) %all-gather.10.cloned.1.call-update) | async-done | bytes 2097168 | tf_op jit(solution)/shard_map/all_gather | solution.py:168
  144.3 37.6 %all-gather.14.cloned.1.call-done = bf16[2,512,1024]{1,0,2:T(2,128)(2,1)} async-done(((bf16[2,512,64]{1,0,2:T(2,128)(2,1)}), bf16[2,512,1024]{1,0,2:T(2,128)(2,1)}) %all-gather.14.cloned.1.call-update) | async-done | bytes 2097168 | tf_op jit(solution)/shard_map/all_gather | solution.py:171
  200.2 31.6 %psum.40 = f32[16]{0:T(128)S(1)} all-reduce(f32[16]{0:T(128)S(1)} %select_reduce_fusion.5), channel_id=1, replica_groups=mesh['dp'=16,'tensor'=2] {'dp'}, use_global_device_ids=true, to_apply=%region_7.8 | all-reduce | flops 16 | bytes 128 | tf_op jit(solution)/shard_map/psum | solution.py:182
  234.6 52.4 %all-gather.20.cloned.1.call-done = bf16[2,1408,1024]{1,0,2:T(2,128)(2,1)} async-done(((bf16[2,1408,64]{1,0,2:T(2,128)(2,1)}), bf16[2,1408,1024]{1,0,2:T(2,128)(2,1)}) %all-gather.20.cloned.1.call-update) | async-done | bytes 5767184 | tf_op jit(solution)/shard_map/all_gather | solution.py:174
  286.9 12.4 fusion.127
  299.3 12.3 copy.114
  311.7 14.2 %copy.115 = bf16[1,1408,1024]{2,1,0:T(8,128)(2,1)} copy(bf16[1,1408,1024]{1,0,2:T(2,128)(2,1)} %get-tuple-element.67) | data formatting | bytes 5767168
  325.9 21.1 %all-gather.16.cloned.1.call-done = bf16[2,1024,1408]{2,1,0:T(8,128)(2,1)} async-done(((bf16[2,64,1408]{2,1,0:T(8,128)(2,1)}), bf16[2,1024,1408]{2,1,0:T(8,128)(2,1)}) %all-gather.16.cloned.1.call-update) | async-done | bytes 5767184 | tf_op jit(solution)/shard_map/all_gather | solution.py:172
  353.0 54.2 %all-gather.18.cloned.1.call-done = bf16[2,1024,1408]{2,1,0:T(8,128)(2,1)} async-done(((bf16[2,64,1408]{2,1,0:T(8,128)(2,1)}), bf16[2,1024,1408]{2,1,0:T(8,128)(2,1)}) %all-gather.18.cloned.1.call-update) | async-done | bytes 5767184 | tf_op jit(solution)/shard_map/all_gather | solution.py:173
  427.5 11.2 pad_maximum_fusion.2
  438.7 17.8 %copy.103 = f32[2,1408,1024]{1,0,2:T(2,128)} copy(f32[2,1408,1024]{2,1,0:T(8,128)} %pad_maximum_fusion.2) | data formatting | bytes 23068672 | tf_op jit(solution)/shard_map/stack | solution.py:40
  483.7 23.5 %all-reduce.15.cloned.1.call-done = (bf16[8,16,1024]{2,1,0:T(8,128)(2,1)}, bf16[8,16,1024]{2,1,0:T(8,128)(2,1)}) async-done(((bf16[8,16,1024]{2,1,0:T(8,128)(2,1)}, bf16[8,16,1024]{2,1,0:T(8,128)(2,1)}), (bf16[8,16,1024]{2,1,0:T(8,128)(2,1)}, bf16[8,16,1024]{2,1,0:T(8,128)(2,1)})) %all-reduce.15.cloned.1.call-update) | async-done | bytes 524304 | tf_op jit(solution)/shard_map/psum | solution.py:125
  514.4 7.2 copy.102
  539.2 8.3 pad_maximum_fusion
  552.9 8.3 pad_maximum_fusion.1
  569.6 56.4 %reduce-scatter.22.cloned.1.call-done = f32[64,2]{1,0:T(8,128)} async-done(((f32[1024,2]{1,0:T(8,128)}), f32[64,2]{1,0:T(8,128)}) %reduce-scatter.22.cloned.1.call-update) | async-done | bytes 528
  627.3 283.8 %all-reduce.13.cloned.1.call-done = (f32[2,512,1024]{1,0,2:T(2,128)}, f32[2,1408,1024]{1,0,2:T(2,128)}) async-done(((f32[2,512,1024]{1,0,2:T(2,128)}, f32[2,1408,1024]{1,0,2:T(2,128)}), (f32[2,512,1024]{1,0,2:T(2,128)}, f32[2,1408,1024]{1,0,2:T(2,128)})) %all-reduce.13.cloned.1.call-update) | async-done | bytes 15728656
  914.9 72.9 %reduce-scatter.12.cloned.1.call-done = f32[2,64,512]{2,1,0:T(8,128)} async-done(((f32[2,1024,512]{2,1,0:T(8,128)}), f32[2,64,512]{2,1,0:T(8,128)}) %reduce-scatter.12.cloned.1.call-update) | async-done | bytes 262160 | tf_op jit(solution)/shard_map/reduce_scatter | solution.py:283
  987.8 76.6 %reduce-scatter.14.cloned.1.call-done = f32[2,64,512]{2,1,0:T(8,128)} async-done(((f32[2,1024,512]{2,1,0:T(8,128)}), f32[2,64,512]{2,1,0:T(8,128)}) %reduce-scatter.14.cloned.1.call-update) | async-done | bytes 262160 | tf_op jit(solution)/shard_map/reduce_scatter | solution.py:284
  1064.5 76.0 %reduce-scatter.16.cloned.1.call-done = f32[2,64,512]{2,1,0:T(8,128)} async-done(((f32[2,1024,512]{2,1,0:T(8,128)}), f32[2,64,512]{2,1,0:T(8,128)}) %reduce-scatter.16.cloned.1.call-update) | async-done | bytes 262160 | tf_op jit(solution)/shard_map/reduce_scatter | solution.py:285
  1140.4 130.5 %reduce-scatter.18.cloned.1.call-done = f32[2,64,1408]{2,1,0:T(8,128)} async-done(((f32[2,1024,1408]{2,1,0:T(8,128)}), f32[2,64,1408]{2,1,0:T(8,128)}) %reduce-scatter.18.cloned.1.call-update) | async-done | bytes 720912 | tf_op jit(solution)/shard_map/reduce_scatter | solution.py:287
  1270.9 130.6 %reduce-scatter.20.cloned.1.call-done = f32[2,64,1408]{2,1,0:T(8,128)} async-done(((f32[2,1024,1408]{2,1,0:T(8,128)}), f32[2,64,1408]{2,1,0:T(8,128)}) %reduce-scatter.20.cloned.1.call-update) | async-done | bytes 720912 | tf_op jit(solution)/shard_map/reduce_scatter | solution.py:288
  (262 shorter events, 136.9 us)
Async XLA Ops:
  7.2 47.1 %all-gather.8.cloned.1.call-start = ((), (), s32[]{:S(2)}) async-start(), calls=%async_computation.7 | async-start | bytes 2228224 | tf_op jit(solution)/shard_map/all_gather | solution.py:170
  7.9 88.7 %all-gather.12.cloned.1.call-start = ((), (), s32[]{:S(2)}) async-start(), calls=%async_computation.9 | async-start | bytes 2228224 | tf_op jit(solution)/shard_map/all_gather | solution.py:169
  8.7 130.4 %all-gather.10.cloned.1.call-start = ((), (), s32[]{:S(2)}) async-start(), calls=%async_computation.8 | async-start | bytes 2228224 | tf_op jit(solution)/shard_map/all_gather | solution.py:168
  9.4 172.4 %all-gather.14.cloned.1.call-start = ((), (), s32[]{:S(2)}) async-start(), calls=%async_computation.10 | async-start | bytes 2228224 | tf_op jit(solution)/shard_map/all_gather | solution.py:171
  11.2 221.4 %all-reduce.9.cloned.1.call-start = ((), (), s32[]{:S(2)}) async-start(), calls=%async_computation.11 | async-start | bytes 1048576 | tf_op jit(solution)/shard_map/psum | solution.py:118
  13.0 446.8 %copy-start.39 = (pred[16]{0:T(512)(128)(4,1)}, pred[16]{0:T(512)(128)(4,1)S(1)}, u32[]{:S(2)}) copy-start(pred[16]{0:T(512)(128)(4,1)S(1)} %get-tuple-element.83) | copy-start | bytes 52
  15.7 124.8 %copy-start.31 = (bf16[8,16,1024]{2,1,0:T(8,128)(2,1)}, bf16[8,16,1024]{2,1,0:T(8,128)(2,1)S(1)}, u32[]{:S(2)}) copy-start(bf16[8,16,1024]{2,1,0:T(8,128)(2,1)S(1)} %fusion.87) | copy-start | bytes 786436
  57.6 86.0 %copy-start.33 = (bf16[8,16,8,64]{3,2,1,0:T(8,128)(2,1)}, bf16[8,16,8,64]{3,2,1,0:T(8,128)(2,1)S(1)}, u32[]{:S(2)}) copy-start(bf16[8,16,8,64]{3,2,1,0:T(8,128)(2,1)S(1)} %reshape.213) | copy-start | bytes 393220
  99.9 43.6 %copy-start.18 = (bf16[8,16,8,64]{3,2,1,0:T(8,128)(2,1)}, bf16[8,16,8,64]{3,2,1,0:T(8,128)(2,1)S(1)}, u32[]{:S(2)}) copy-start(bf16[8,16,8,64]{3,2,1,0:T(8,128)(2,1)S(1)} %reshape.215) | copy-start | bytes 393220
  142.6 45.7 %copy-start.25 = (f32[8,8,16,16]{2,3,1,0:T(8,128)}, f32[8,8,16,16]{2,3,1,0:T(8,128)S(1)}, u32[]{:S(2)}) copy-start(f32[8,8,16,16]{2,3,1,0:T(8,128)S(1)} %fusion.56) | copy-start | bytes 196612
  144.2 52.0 %copy-start.15 = (bf16[8,16,512]{2,1,0:T(8,128)(2,1)}, bf16[8,16,512]{2,1,0:T(8,128)(2,1)S(1)}, u32[]{:S(2)}) copy-start(bf16[8,16,512]{2,1,0:T(8,128)(2,1)S(1)} %convert_element_type.113) | copy-start | bytes 393220
  197.4 89.6 %all-gather.20.cloned.1.call-start = ((), (), s32[]{:S(2)}) async-start(), calls=%async_computation.14 | async-start | bytes 6127616 | tf_op jit(solution)/shard_map/all_gather | solution.py:174
  198.6 148.4 %all-gather.16.cloned.1.call-start = ((), (), s32[]{:S(2)}) async-start(), calls=%async_computation.12 | async-start | bytes 6127616 | tf_op jit(solution)/shard_map/all_gather | solution.py:172
  199.3 207.9 %all-gather.18.cloned.1.call-start = ((), (), s32[]{:S(2)}) async-start(), calls=%async_computation.13 | async-start | bytes 6127616 | tf_op jit(solution)/shard_map/all_gather | solution.py:173
  200.1 259.7 %all-reduce.11.cloned.1.call-start = ((), (), s32[]{:S(2)}) async-start(), calls=%async_computation.15 | async-start | bytes 1048576 | tf_op jit(solution)/shard_map/psum | solution.py:240
  427.2 80.1 %all-reduce.15.cloned.1.call-start = ((), (), s32[]{:S(2)}) async-start(), calls=%async_computation.24 | async-start | bytes 1048576 | tf_op jit(solution)/shard_map/psum | solution.py:125
  479.9 87.2 %reduce-scatter.24.cloned.1.call-start = ((), (), s32[]{:S(2)}) async-start(), calls=%async_computation.22 | async-start | bytes 557056
  483.7 142.2 %reduce-scatter.22.cloned.1.call-start = ((), (), s32[]{:S(2)}) async-start(), calls=%async_computation.21 | async-start | bytes 557056
  509.6 401.5 %all-reduce.13.cloned.1.call-start = ((), (), s32[]{:S(2)}) async-start(), calls=%async_computation.23 | async-start | bytes 31457280
  521.7 466.1 %reduce-scatter.12.cloned.1.call-start = ((), (), s32[]{:S(2)}) async-start(), calls=%async_computation.16 | async-start | bytes 4456448 | tf_op jit(solution)/shard_map/reduce_scatter | solution.py:283
  526.3 538.2 %reduce-scatter.14.cloned.1.call-start = ((), (), s32[]{:S(2)}) async-start(), calls=%async_computation.17 | async-start | bytes 4456448 | tf_op jit(solution)/shard_map/reduce_scatter | solution.py:284
  529.8 610.6 %reduce-scatter.16.cloned.1.call-start = ((), (), s32[]{:S(2)}) async-start(), calls=%async_computation.18 | async-start | bytes 4456448 | tf_op jit(solution)/shard_map/reduce_scatter | solution.py:285
  533.7 737.1 %reduce-scatter.18.cloned.1.call-start = ((), (), s32[]{:S(2)}) async-start(), calls=%async_computation.19 | async-start | bytes 12255232 | tf_op jit(solution)/shard_map/reduce_scatter | solution.py:287
  547.6 853.9 %reduce-scatter.20.cloned.1.call-start = ((), (), s32[]{:S(2)}) async-start(), calls=%async_computation.20 | async-start | bytes 12255232 | tf_op jit(solution)/shard_map/reduce_scatter | solution.py:288
  (53 other events, 254.2 us)
Sparse Core Ops, SparseCore 0:
  10.2 44.0 all-gather.7
  56.5 40.1 all-gather.11
  98.8 40.1 all-gather.9
  141.6 40.1 all-gather.13
  197.5 27.3 all-reduce.8
  227.9 59.0 all-gather.19
  289.5 57.4 all-gather.15
  349.5 57.6 all-gather.17
  427.3 27.2 all-reduce.10
  480.0 27.2 all-reduce.14
  511.3 55.7 reduce-scatter.23
  571.0 54.8 reduce-scatter.21
  630.6 280.4 all-reduce.12
  915.4 72.3 reduce-scatter.11
  992.6 71.8 reduce-scatter.13
  1068.8 71.6 reduce-scatter.15
  1145.5 125.3 reduce-scatter.17
  1275.4 126.0 reduce-scatter.19
where the time goes:
time: 1410 us
  waiting for transfers between devices  1140 us (81%)
  local copies, waits for them, and re-layouts  98.7 us (7%)
  matrix products  67.8 us (5%)
  other arithmetic  53.3 us (4%)
  blocking collectives  31.6 us (2%)
  between operations  15.9 us (1%)
    unnamed x21, waiting for transfers between devices  348 us
    reduce_scatter x1, waiting for transfers between devices, per_device(): lax.psum_scatter(up_grad, 'dp', scatter_dimension=1, tiled=True)  131 us
    reduce_scatter x1, waiting for transfers between devices, per_device(): lax.psum_scatter(gate_grad, 'dp', scatter_dimension=1, tiled=True)  130 us
    reduce_scatter x1, waiting for transfers between devices, per_device(): lax.psum_scatter(key_grad, 'dp', scatter_dimension=1, tiled=True)  76.6 us
    reduce_scatter x1, waiting for transfers between devices, per_device(): lax.psum_scatter(value_grad, 'dp', scatter_dimension=1, tiled=True)  76 us
    reduce_scatter x1, waiting for transfers between devices, per_device(): lax.psum_scatter(query_grad, 'dp', scatter_dimension=1, tiled=True)  72.9 us
    all_gather x1, waiting for transfers between devices, per_device(): lax.all_gather(up_weight, 'dp', axis=1, tiled=True)  54.2 us
    all_gather x1, waiting for transfers between devices, per_device(): lax.all_gather(down_weight, 'dp', axis=2, tiled=True)  52.4 us
  transfers between devices with their start and end apart: 18, of which 16 were waited for; matrix products, arithmetic and copies ran while one was open for 11% of the time, Pallas kernels for 0%

commit v1 on v0

v1 whole, which is shorter than its diff:
```python
import jax
import jax.numpy as jnp
from jax import lax
from jax.experimental import pallas as pl
from jax.experimental.pallas import tpu as pltpu
from jax.sharding import PartitionSpec as P

HDIM = 64
EPSILON = 1e-05
INNER = 16
ZN = 4
LANES = 128
MESH = pl.DeviceIdType.MESH
BF = jnp.bfloat16
F32 = jnp.float32
NN = (((1,), (0,)), ((), ()))
NT = (((1,), (1,)), ((), ()))
TN = (((0,), (0,)), ((), ()))


def dot(a, b, dims=NN):
    return lax.dot_general(a, b, dims, preferred_element_type=F32)


def layer_kernel(
    frames, cot, dialogue, padding, table, set_mask, gain_one, gain_two,
    wq, wk, wv, wo, wg, wu, wd,
    mixed, frames_grad, dq, dk, dv, do, dg, du, dd, gains_grad,
    st1, st2, ga1, ga2, w1, w2,
    n1, sd, n2, hl, pf,
    sb, sr, so, ru, rd,
    qs, ks, vs, att, probs, act, gg, ug, gt, up,
    dw1, dw2, re1, re2, fi1, fi2,
    cnt, gain_col, gain_face, halves,
    u_one, u_two, hid, hgrad, small,
    z1_s, z1_r, z2_s, z2_r, m1_s, m1_r, m2_s, m2_r,
    ag_s, ag_r, rs_sib_s, rs_sib_r, rs_s, rs_ru, rs_rd,
    gr_s, gr_r, gf_s, gf_r, c_s, c_r, y_s, y_r, gcs, gcr, gfs, gfr,
):
    idx = lax.axis_index("dp")
    y = lax.axis_index("tensor")
    inner = lax.rem(idx, INNER)
    base = idx - inner
    z = lax.div(inner, 4)
    x = lax.rem(lax.div(inner, 2), 2)
    c = lax.rem(inner, 2)

    def dev(zz, xx, cc, yy):
        return (base + zz * 4 + xx * 2 + cc, yy)

    def flip(v, bit):
        return 1 - v if bit else v

    def remote(src, dst, ssem, rsem, device):
        return pltpu.make_async_remote_copy(
            src_ref=src, dst_ref=dst, send_sem=ssem, recv_sem=rsem,
            device_id=device, device_id_type=MESH,
        )

    me = dev(z, x, c, y)
    sibling = dev(z, x, 1 - c, y)
    above = dev(lax.rem(z + 1, ZN), x, c, y)
    below = dev(lax.rem(z + ZN - 1, ZN), x, c, y)
    column = [dev(lax.rem(z + k, ZN), x, c, y) for k in (1, 2, 3)]
    face = [
        (flip(x, a), flip(c, b), flip(y, d))
        for a in (0, 1) for b in (0, 1) for d in (0, 1) if a or b or d
    ]
    rows = n1.shape[1]
    group = 8 * rows
    width = n1.shape[2]
    half = rows // 16
    qb = w1.shape[2] // 4
    fb = w2.shape[2] // 3
    hidden_units = wg.shape[2]
    d_rows = wq.shape[1]
    own_slot = 2 * z + c
    mine = pl.ds(half * y, half)
    slice_mine = 2 * x + c
    pending = []

    def send(cond, src, dst, ssem, rsem, device):
        def go():
            remote(src, dst, ssem, rsem, device).start()

        def done():
            remote(src, dst, ssem, rsem, device).wait_send()

        if cond is None:
            go()
        else:
            pl.when(cond)(go)
        pending.append((cond, done))

    def arrived(dst, rsem):
        remote(dst, dst, rsem, rsem, sibling).wait_recv()

    barrier = pltpu.get_barrier_semaphore()
    for d in column:
        pl.semaphore_signal(barrier, inc=1, device_id=d, device_id_type=MESH)
    for xx, cc, yy in face:
        pl.semaphore_signal(barrier, inc=1, device_id=dev(z, xx, cc, yy), device_id_type=MESH)

    eye = (
        lax.broadcasted_iota(jnp.int32, (d_rows, d_rows), 0)
        == lax.broadcasted_iota(jnp.int32, (d_rows, d_rows), 1)
    ).astype(BF)
    for s in range(2):
        wot = dot(eye, wo[s], NT).astype(BF)
        for b in range(ZN):
            part = slice(b * qb, (b + 1) * qb)
            st1[b, s, :, 0:qb] = wq[s, :, part]
            st1[b, s, :, qb:2 * qb] = wk[s, :, part]
            st1[b, s, :, 2 * qb:3 * qb] = wv[s, :, part]
            st1[b, s, :, 3 * qb:4 * qb] = wot[:, part]

    def zero(ref):
        ref[...] = jnp.zeros_like(ref)

    pl.when(z == 0)(lambda: zero(ru))
    pl.when(z == ZN - 1)(lambda: zero(rd))

    pl.semaphore_wait(barrier, len(column) + len(face))

    def spread(st, ga, ssem, rsem):
        for k in (1, 2, 3):
            zz = lax.rem(z + k, ZN)
            send(None, st.at[zz], ga.at[z], ssem.at[k], rsem.at[z], dev(zz, x, c, y))

    def multicast(src, zz, w, ssem, rsem):
        piece = zz * 4 + slice_mine
        dst = w.at[:, pl.ds(pl.multiple_of(piece * d_rows, d_rows), d_rows), :]
        for a in (0, 1):
            for b in (0, 1):
                target = dev(z, flip(x, a), y, flip(y, b))
                sem = ssem.at[zz, 2 * a + b]
                if a or b:
                    send(None, src, dst, sem, rsem.at[piece], target)
                else:
                    send(c != y, src, dst, sem, rsem.at[piece], sibling)
                    local = pltpu.make_async_copy(src, dst, rsem.at[piece])
                    pl.when(c == y)(local.start)

    def weights_here(w, rsem):
        for piece in range(INNER):
            arrived(w.at[:, pl.ds(piece * d_rows, d_rows), :], rsem.at[piece])

    spread(st1, ga1, z1_s, z1_r)
    multicast(st1.at[z], z, w1, m1_s, m1_r)

    def gain_full(gain):
        m1 = set_mask[1].astype(F32)[:, 0:1]
        g0 = gain[0:1, :]
        g1 = gain[1:2, :]
        return jnp.where(m1 > 0.5, g1, g0)

    def tile_rows(v):
        return jnp.broadcast_to(v[None], (half, 16, v.shape[1])).reshape(rows, v.shape[1])

    def normalize(values, gain):
        inverse = lax.rsqrt(jnp.sum(values * values, axis=-1, keepdims=True) / width + EPSILON)
        unit = values * inverse
        return unit, inverse, (unit * tile_rows(gain_full(gain))).astype(BF)

    block = frames[mine].reshape(rows, width).astype(F32)
    unit, inverse, normed = normalize(block, gain_one)
    u_one[...] = unit
    small[0] = jnp.broadcast_to(inverse, (rows, LANES))
    n1[own_slot] = normed

    def gather_start(which, buf):
        s, r = ag_s.at[which], ag_r.at[which]
        src = buf.at[own_slot]
        send(z < ZN - 1, src, src, s.at[own_slot, 1], r.at[own_slot], above)
        send(z > 0, src, src, s.at[own_slot, 2], r.at[own_slot], below)
        send(None, src, src, s.at[own_slot, 0], r.at[own_slot], sibling)

    def gather_step(which, buf, k):
        s, r = ag_s.at[which], ag_r.at[which]

        def from_below():
            slot = 2 * (z - k) + c
            arrived(buf.at[slot], r.at[slot])

        def from_above():
            slot = 2 * (z + k) + c
            arrived(buf.at[slot], r.at[slot])

        pl.when(z >= k)(from_below)
        lo = 2 * jnp.maximum(z - k, 0) + c
        send((z >= k) & (z < ZN - 1), buf.at[lo], buf.at[lo], s.at[lo, 1], r.at[lo], above)
        send(z >= k, buf.at[lo], buf.at[lo], s.at[lo, 0], r.at[lo], sibling)
        pl.when(z + k <= ZN - 1)(from_above)
        hi = 2 * jnp.minimum(z + k, ZN - 1) + c
        send((z + k <= ZN - 1) & (z > 0), buf.at[hi], buf.at[hi], s.at[hi, 2], r.at[hi], below)
        send(z + k <= ZN - 1, buf.at[hi], buf.at[hi], s.at[hi, 0], r.at[hi], sibling)

    def gather_end(which, buf):
        for zz in range(ZN):
            slot = 2 * zz + (1 - c)
            arrived(buf.at[slot], ag_r.at[which, slot])

    gather_start(0, n1)

    cnt[0, z] = table[...]
    for k in (1, 2, 3):
        send(None, table, cnt.at[0, z], c_s.at[0, k], c_r.at[0, z], dev(lax.rem(z + k, ZN), x, c, y))

    for k in (1, 2, 3):
        zz = lax.rem(z + k, ZN)
        arrived(ga1.at[zz], z1_r.at[zz])
        multicast(ga1.at[zz], zz, w1, m1_s, m1_r)
        gather_step(0, n1, k)

    for k in (1, 2, 3):
        zz = lax.rem(z + k, ZN)
        arrived(cnt.at[0, zz], c_r.at[0, zz])
    cnt[1, slice_mine] = cnt[0, 0] + cnt[0, 1] + cnt[0, 2] + cnt[0, 3]
    for a, b in ((0, 1), (1, 0), (1, 1)):
        send(None, cnt.at[1, slice_mine], cnt.at[1, slice_mine], c_s.at[1, 2 * a + b], c_r.at[1, slice_mine],
             dev(z, flip(x, a), flip(c, b), y))

    for s in range(2):
        wdt = dot(eye, wd[s], NT).astype(BF)
        for b in range(ZN):
            n = min(fb, hidden_units - b * fb)
            part = slice(b * fb, b * fb + n)
            for j, v in enumerate((wg[s, :, part], wu[s, :, part], wdt[:, part])):
                st2[b, s, :, j * fb:j * fb + n] = v
                if n < fb:
                    st2[b, s, :, j * fb + n:(j + 1) * fb] = jnp.zeros((d_rows, fb - n), BF)
    spread(st2, ga2, z2_s, z2_r)
    multicast(st2.at[z], z, w2, m2_s, m2_r)

    for a, b in ((0, 1), (1, 0), (1, 1)):
        j = 2 * flip(x, a) + flip(c, b)
        arrived(cnt.at[1, j], c_r.at[1, j])
    counts = cnt[1, 0] + cnt[1, 1] + cnt[1, 2] + cnt[1, 3]
    lane = lax.broadcasted_iota(jnp.int32, (8, LANES), 1)
    unpadded = padding[...].astype(F32)
    per_frame = jnp.sum(jnp.where(dialogue[...] == lane, counts, 0.0), axis=1, keepdims=True)
    loss = unpadded * (frames.shape[0] * 1.0) / (per_frame + 1.0)
    small[1, 0:8, :] = loss
    loss_mine = small[1, mine, :]
    weight_rows = jnp.broadcast_to(loss_mine[:, None, 0:1], (half, 16, width)).reshape(rows, width)
    seed = cot[mine].reshape(rows, width).astype(F32) * weight_rows
    sd[own_slot] = seed.astype(BF)
    gather_start(1, sd)
    gather_end(0, n1)

    def masked(v, s):
        n = v.shape[1]
        m = set_mask[s]
        m = m if n == width else m[:, 0:n]
        return (v.reshape(group // 16, 16, n) * m[None]).reshape(group, n)

    def flat(buf):
        return buf[...].reshape(group, width)

    weights_here(w1, m1_r)
    qkv = dot(masked(flat(n1), 0), w1[0, :, 0:3 * qb]) + dot(masked(flat(n1), 1), w1[1, :, 0:3 * qb])
    qkv = qkv.astype(BF)
    qs[...] = qkv[:, 0:qb]
    ks[...] = qkv[:, qb:2 * qb]
    vs[...] = qkv[:, 2 * qb:3 * qb]

    bl = LANES
    r_at = lax.broadcasted_iota(jnp.int32, (bl, bl), 0)
    c_at = lax.broadcasted_iota(jnp.int32, (bl, bl), 1)
    seen = (c_at <= r_at) & (lax.div(r_at, 16) == lax.div(c_at, 16))
    heads = qb // HDIM
    head_of = lax.div(lax.broadcasted_iota(jnp.int32, (bl, qb), 1), HDIM)
    scale = HDIM ** (-0.5)

    def only(v, h):
        return jnp.where(head_of == h, v, jnp.zeros_like(v))

    for t in range(group // bl):
        rs_ = pl.ds(t * bl, bl)
        q, kk, v = qs[rs_, :], ks[rs_, :], vs[rs_, :]
        out = jnp.zeros((bl, qb), F32)
        for h in range(heads):
            scores = dot(only(q, h), kk, NT) * scale
            scores = jnp.where(seen, scores, -1e30)
            e = jnp.exp(scores - jnp.max(scores, axis=-1, keepdims=True))
            e = jnp.where(seen, e, 0.0)
            p = e / jnp.sum(e, axis=-1, keepdims=True)
            probs[t, h] = p
            out = jnp.where(head_of == h, dot(p.astype(BF), v), out)
        att[rs_, :] = out.astype(BF)

    def scatter_start(n):
        for b in (3, 0, 2, 1):
            sb[n, b] = pf[2 * b + 1 - c].astype(BF)
            send(None, sb.at[n, b], sr.at[n, b], rs_sib_s.at[n, b], rs_sib_r.at[n, b], sibling)

    def chip_sum(n, b):
        arrived(sr.at[n, b], rs_sib_r.at[n, b])
        return pf[2 * b + c] + sr[n, b].astype(F32)

    def scatter_chain(n):
        for rising, b in ((True, 3), (False, 0), (True, 2), (False, 1), (True, 1), (False, 2)):
            if rising:
                cond, inflow, buf, r, target = b > z, z > 0, ru, rs_ru, above
            else:
                cond, inflow, buf, r, target = b < z, z < ZN - 1, rd, rs_rd, below

            def step(b=b, inflow=inflow, buf=buf, r=r):
                total = chip_sum(n, b)
                pl.when(inflow)(lambda: arrived(buf.at[n, b], r.at[n, b]))
                so[n, b] = (total + buf[n, b].astype(F32)).astype(BF)

            pl.when(cond)(step)
            send(cond, so.at[n, b], buf.at[n, b], rs_s.at[n, b], r.at[n, b], target)

    def scatter_end(n):
        total = chip_sum(n, z)
        pl.when(z > 0)(lambda: arrived(ru.at[n, z], rs_ru.at[n, z]))
        pl.when(z < ZN - 1)(lambda: arrived(rd.at[n, z], rs_rd.at[n, z]))
        return total + ru[n, z].astype(F32) + rd[n, z].astype(F32)

    def put_partial(v):
        pf[...] = v.reshape(8, rows, width)

    put_partial(
        dot(masked(att[...], 0), w1[0, :, 3 * qb:4 * qb], NT)
        + dot(masked(att[...], 1), w1[1, :, 3 * qb:4 * qb], NT)
    )
    scatter_start(0)
    gather_step(1, sd, 1)
    scatter_chain(0)
    attention = scatter_end(0)

    hidden = block + attention
    hid[...] = hidden
    unit, inverse, normed = normalize(hidden, gain_two)
    u_two[...] = unit
    small[2] = jnp.broadcast_to(inverse, (rows, LANES))
    n2[own_slot] = normed
    gather_start(2, n2)
    for k in (1, 2, 3):
        gather_step(2, n2, k)

    for k in (2, 3):
        gather_step(1, sd, k)
    for k in (1, 2, 3):
        zz = lax.rem(z + k, ZN)
        arrived(ga2.at[zz], z2_r.at[zz])
        multicast(ga2.at[zz], zz, w2, m2_s, m2_r)
    gather_end(1, sd)
    weights_here(w2, m2_r)
    gather_end(2, n2)

    g0, u0, d0 = slice(0, fb), slice(fb, 2 * fb), slice(2 * fb, 3 * fb)
    gu = dot(masked(flat(n2), 0), w2[0, :, 0:2 * fb]) + dot(masked(flat(n2), 1), w2[1, :, 0:2 * fb])
    gt[...] = gu[:, 0:fb]
    up[...] = gu[:, fb:2 * fb]
    active_grad = dot(masked(flat(sd), 0), w2[0, :, d0]) + dot(masked(flat(sd), 1), w2[1, :, d0])
    gate = gt[...]
    sig = jax.nn.sigmoid(gate)
    silu = gate * sig
    act[...] = (silu * up[...]).astype(BF)
    gg[...] = (active_grad * up[...] * sig * (1.0 + gate * (1.0 - sig))).astype(BF)
    ug[...] = (active_grad * silu).astype(BF)

    put_partial(
        dot(masked(gg[...], 0), w2[0, :, g0], NT)
        + dot(masked(gg[...], 1), w2[1, :, g0], NT)
        + dot(masked(ug[...], 0), w2[0, :, u0], NT)
        + dot(masked(ug[...], 1), w2[1, :, u0], NT)
    )
    scatter_start(1)

    def reduce_send(n, dw, re, lo, cols):
        for a in (0, 1):
            for b in (0, 1):
                xx, cc = flip(x, a), flip(c, b)
                src = dw.at[:, :, 2 * xx + cc, :, pl.ds(lo, cols)]
                dst = re.at[2 * x + y, :, :, :, pl.ds(lo, cols)]
                rsem = gr_r.at[n, 2 * x + y]
                if a or b:
                    send(None, src, dst, gr_s.at[n, 2 * a + b], rsem, dev(z, xx, cc, c))
                else:
                    send(c != y, src, dst, gr_s.at[n, 0], rsem, dev(z, x, c, c))
                    local = pltpu.make_async_copy(src, dst, rsem)
                    pl.when(c == y)(local.start)

    def reduce_sum(n, re, fi, lo, cols):
        cs = pl.ds(lo, cols)
        for j in range(4):
            arrived(re.at[j, :, :, :, cs], gr_r.at[n, j])
        for k in (1, 2, 3, 0):
            zz = lax.rem(z + k, ZN)
            for s in range(2):
                total = re[0, s, zz, :, cs].astype(F32)
                for j in (1, 2, 3):
                    total = total + re[j, s, zz, :, cs].astype(F32)
                if k:
                    re[0, s, zz, :, cs] = total.astype(BF)
                else:
                    fi[z, s, :, cs] = total.astype(BF)
            if k:
                send(None, re.at[0, :, zz, :, cs], fi.at[z, :, :, cs], gf_s.at[n, k], gf_r.at[n, z],
                     dev(zz, x, c, y))

    def reduce_end(n, fi, lo, cols):
        for k in (1, 2, 3):
            zz = lax.rem(z + k, ZN)
            arrived(fi.at[zz, :, :, pl.ds(lo, cols)], gf_r.at[n, zz])

    def weight_grad(dw, lo, cols, values, grads):
        for s in range(2):
            product = dot(masked(values, s), grads, TN).astype(BF)
            dw[s, :, :, :, pl.ds(lo, cols)] = product.reshape(ZN, 4, d_rows, cols)

    scatter_chain(1)
    normed_two_grad = scatter_end(1)

    def set_sums(v, at):
        three = v.reshape(half, 16, width)
        for s in range(2):
            m = set_mask[s].astype(F32)
            gain_col[z, at + s:at + s + 1, :] = jnp.sum(
                (three * m[None]).reshape(rows, width), axis=0, keepdims=True
            )

    def norm_back(gradient, gain, unit, inverse):
        scaled = gradient * tile_rows(gain_full(gain))
        return inverse * (scaled - unit * (jnp.sum(scaled * unit, axis=-1, keepdims=True) / width))

    gain_col[z] = jnp.zeros((8, width), F32)
    unit = u_two[...]
    set_sums(normed_two_grad * unit, 2)
    seed = cot[mine].reshape(rows, width).astype(F32) * weight_rows
    hidden_grad = seed + norm_back(normed_two_grad, gain_two, unit, small[2][:, 0:1])
    hgrad[...] = hidden_grad
    hl[own_slot] = hidden_grad.astype(BF)
    gather_start(3, hl)

    put_partial(
        dot(masked(act[...], 0), w2[0, :, d0], NT)
        + dot(masked(act[...], 1), w2[1, :, d0], NT)
    )
    scatter_start(2)
    gather_step(3, hl, 1)
    weight_grad(dw2, 2 * fb, fb, flat(sd), act[...])
    reduce_send(0, dw2, re2, 2 * fb, fb)
    gather_step(3, hl, 2)
    weight_grad(dw2, 0, fb, flat(n2), gg[...])
    gather_step(3, hl, 3)
    weight_grad(dw2, fb, fb, flat(n2), ug[...])
    reduce_send(1, dw2, re2, 0, 2 * fb)
    gather_end(3, hl)

    attended_grad = dot(masked(flat(hl), 0), w1[0, :, 3 * qb:4 * qb]) + dot(
        masked(flat(hl), 1), w1[1, :, 3 * qb:4 * qb]
    )
    datt = attended_grad.astype(BF)
    gq, gk, gv = [], [], []
    for t in range(group // bl):
        rs_ = pl.ds(t * bl, bl)
        q, kk, v = qs[rs_, :], ks[rs_, :], vs[rs_, :]
        da = datt[t * bl:(t + 1) * bl, :]
        tq = jnp.zeros((bl, qb), F32)
        tk, tv = tq, tq
        for h in range(heads):
            p = probs[t, h]
            dp_ = dot(only(da, h), v, NT)
            tv = jnp.where(head_of == h, dot(p.astype(BF), da, TN), tv)
            ds_ = (p * (dp_ - jnp.sum(dp_ * p, axis=-1, keepdims=True))).astype(BF)
            tq = jnp.where(head_of == h, dot(ds_, kk) * scale, tq)
            tk = jnp.where(head_of == h, dot(ds_, q, TN) * scale, tk)
        gq.append(tq.astype(BF))
        gk.append(tk.astype(BF))
        gv.append(tv.astype(BF))
    for t in range(group // bl):
        rs_ = pl.ds(t * bl, bl)
        qs[rs_, :] = gq[t]
        ks[rs_, :] = gk[t]
        vs[rs_, :] = gv[t]
    total = None
    for s in range(2):
        for j, ref in enumerate((qs, ks, vs)):
            term = dot(masked(ref[...], s), w1[s, :, j * qb:(j + 1) * qb], NT)
            total = term if total is None else total + term
    scatter_chain(2)
    branch = scatter_end(2)
    put_partial(total)
    scatter_start(3)
    weight_grad(dw1, 3 * qb, qb, flat(hl), att[...])
    for j, ref in enumerate((qs, ks, vs)):
        weight_grad(dw1, j * qb, qb, flat(n1), ref[...])
    reduce_send(2, dw1, re1, 0, 4 * qb)

    halves[0, mine] = (hid[...] + branch).astype(BF).reshape(half, 16, width)
    other = dev(z, x, c, 1 - y)
    send(None, halves.at[0, mine], halves.at[0, mine], y_s.at[0], y_r.at[0], other)

    scatter_chain(3)
    normed_one_grad = scatter_end(3)
    unit = u_one[...]
    set_sums(normed_one_grad * unit, 0)
    for k in (1, 2, 3):
        send(None, gain_col.at[z], gain_col.at[z], gcs.at[k], gcr.at[z], dev(lax.rem(z + k, ZN), x, c, y))
    result = hgrad[...] + norm_back(normed_one_grad, gain_one, unit, small[0][:, 0:1])
    halves[1, mine] = result.astype(BF).reshape(half, 16, width)
    send(None, halves.at[1, mine], halves.at[1, mine], y_s.at[1], y_r.at[1], other)

    reduce_sum(0, re2, fi2, 2 * fb, fb)
    reduce_sum(1, re2, fi2, 0, 2 * fb)
    reduce_sum(2, re1, fi1, 0, 4 * qb)

    for k in (1, 2, 3):
        zz = lax.rem(z + k, ZN)
        arrived(gain_col.at[zz], gcr.at[zz])
    place = 4 * x + 2 * c + y
    gain_face[place] = gain_col[0] + gain_col[1] + gain_col[2] + gain_col[3]
    for k, (xx, cc, yy) in enumerate(face):
        send(None, gain_face.at[place], gain_face.at[place], gfs.at[k], gfr.at[place], dev(z, xx, cc, yy))

    reduce_end(0, fi2, 2 * fb, fb)
    for b in range(ZN):
        n = min(fb, hidden_units - b * fb)
        both = fi2[b, :, :, d0].reshape(2 * d_rows, fb).astype(F32).T
        for s in range(2):
            dd[s, b * fb:b * fb + n, :] = both[0:n, s * d_rows:(s + 1) * d_rows]
    reduce_end(1, fi2, 0, 2 * fb)
    for b in range(ZN):
        n = min(fb, hidden_units - b * fb)
        dg[:, :, b * fb:b * fb + n] = fi2[b, :, :, 0:n].astype(F32)
        du[:, :, b * fb:b * fb + n] = fi2[b, :, :, fb:fb + n].astype(F32)
    reduce_end(2, fi1, 0, 4 * qb)
    for b in range(ZN):
        part = slice(b * qb, (b + 1) * qb)
        dq[:, :, part] = fi1[b, :, :, 0:qb].astype(F32)
        dk[:, :, part] = fi1[b, :, :, qb:2 * qb].astype(F32)
        dv[:, :, part] = fi1[b, :, :, 2 * qb:3 * qb].astype(F32)
        both = fi1[b, :, :, 3 * qb:4 * qb].reshape(2 * d_rows, qb).astype(F32).T
        for s in range(2):
            do[s, part, :] = both[:, s * d_rows:(s + 1) * d_rows]

    for j, out in ((0, mixed), (1, frames_grad)):
        theirs = pl.ds(half * (1 - y), half)
        arrived(halves.at[j, theirs], y_r.at[j])
        out[...] = halves[j]
    for xx, cc, yy in face:
        j = 4 * xx + 2 * cc + yy
        arrived(gain_face.at[j], gfr.at[j])
    total = gain_face[0]
    for j in range(1, 8):
        total = total + gain_face[j]
    gains_grad[...] = total

    for cond, done in pending:
        if cond is None:
            done()
        else:
            pl.when(cond)(done)


def run_layer(frames, cot, dialogue, padding, table, set_mask, gain_one, gain_two, weights):
    wq, wk, wv, wo, wg, wu, wd = weights
    width = frames.shape[2]
    rows = frames.shape[0] * frames.shape[1] // 2
    d_rows = wq.shape[1]
    qb = wq.shape[2] // ZN
    units = wg.shape[2]
    fb = -(-units // (ZN * LANES)) * LANES
    group = 8 * rows
    dma = pltpu.SemaphoreType.DMA
    vm = pltpu.VMEM
    out_shape = [
        jax.ShapeDtypeStruct(frames.shape, BF),
        jax.ShapeDtypeStruct(frames.shape, BF),
        jax.ShapeDtypeStruct(wq.shape, F32),
        jax.ShapeDtypeStruct(wk.shape, F32),
        jax.ShapeDtypeStruct(wv.shape, F32),
        jax.ShapeDtypeStruct(wo.shape, F32),
        jax.ShapeDtypeStruct(wg.shape, F32),
        jax.ShapeDtypeStruct(wu.shape, F32),
        jax.ShapeDtypeStruct(wd.shape, F32),
        jax.ShapeDtypeStruct((8, width), F32),
    ]
    scratch = [
        vm((ZN, 2, d_rows, 4 * qb), BF), vm((ZN, 2, d_rows, 3 * fb), BF),
        vm((ZN, 2, d_rows, 4 * qb), BF), vm((ZN, 2, d_rows, 3 * fb), BF),
        vm((2, width, 4 * qb), BF), vm((2, width, 3 * fb), BF),
        vm((8, rows, width), BF), vm((8, rows, width), BF), vm((8, rows, width), BF), vm((8, rows, width), BF),
        vm((8, rows, width), F32),
        vm((4, 4, rows, width), BF), vm((4, 4, rows, width), BF), vm((4, 4, rows, width), BF),
        vm((4, 4, rows, width), BF), vm((4, 4, rows, width), BF),
        vm((group, qb), BF), vm((group, qb), BF), vm((group, qb), BF), vm((group, qb), BF),
        vm((group // LANES, qb // HDIM, LANES, LANES), F32),
        vm((group, fb), BF), vm((group, fb), BF), vm((group, fb), BF), vm((group, fb), F32), vm((group, fb), F32),
        vm((2, ZN, 4, d_rows, 4 * qb), BF), vm((2, ZN, 4, d_rows, 3 * fb), BF),
        vm((4, 2, ZN, d_rows, 4 * qb), BF), vm((4, 2, ZN, d_rows, 3 * fb), BF),
        vm((ZN, 2, d_rows, 4 * qb), BF), vm((ZN, 2, d_rows, 3 * fb), BF),
        vm((2, 4, 8, LANES), F32), vm((ZN, 8, width), F32), vm((8, 8, width), F32),
        vm((2,) + frames.shape, BF),
        vm((rows, width), F32), vm((rows, width), F32), vm((rows, width), F32), vm((rows, width), F32),
        vm((3, rows, LANES), F32),
        dma((4,)), dma((4,)), dma((4,)), dma((4,)),
        dma((4, 4)), dma((INNER,)), dma((4, 4)), dma((INNER,)),
        dma((4, 8, 3)), dma((4, 8)),
        dma((4, 4)), dma((4, 4)), dma((4, 4)), dma((4, 4)), dma((4, 4)),
        dma((3, 4)), dma((3, 4)), dma((3, 4)), dma((3, 4)),
        dma((2, 4)), dma((2, 4)), dma((2,)), dma((2,)),
        dma((4,)), dma((4,)), dma((8,)), dma((8,)),
    ]
    spec = pl.BlockSpec(memory_space=pltpu.VMEM)
    return pl.pallas_call(
        layer_kernel,
        out_shape=out_shape,
        in_specs=[spec] * 15,
        out_specs=[spec] * 10,
        scratch_shapes=scratch,
        compiler_params=pltpu.CompilerParams(
            collective_id=0, has_side_effects=True, vmem_limit_bytes=63 * 2**20
        ),
        cost_estimate=pl.CostEstimate(flops=10**10, bytes_accessed=10**7, transcendentals=0),
        name="layer",
    )(frames, cot, dialogue, padding, table, set_mask, gain_one, gain_two, wq, wk, wv, wo, wg, wu, wd)


def per_device(
    frames, cotangent, dialogue, padding, position_set,
    query_weight, key_weight, value_weight, output_weight, gate_weight, up_weight, down_weight,
    attention_gain, feedforward_gain,
):
    dp = lax.axis_size("dp")
    outer = dp // INNER
    groups = [[o * INNER + i for o in range(outer)] for i in range(INNER)]
    weights = [query_weight, key_weight, value_weight, output_weight, gate_weight, up_weight, down_weight]
    axes = [1, 1, 1, 2, 1, 1, 2]
    width = frames.shape[-1]

    def to_kernel(v):
        if outer == 1:
            return v
        cut = v.reshape(v.shape[:-1] + (outer, INNER, width // dp))
        return jnp.swapaxes(cut, -3, -2).reshape(v.shape)

    def from_kernel(v):
        if outer == 1:
            return v
        cut = v.reshape(v.shape[:-1] + (INNER, outer, width // dp))
        return jnp.swapaxes(cut, -3, -2).reshape(v.shape)

    if outer > 1:
        weights = [
            lax.all_gather(w, "dp", axis=a, tiled=True, axis_index_groups=groups) for w, a in zip(weights, axes)
        ]
    unpadded = padding.astype(F32)
    hit = dialogue[:, None] == jnp.arange(LANES, dtype=jnp.int32)[None, :]
    table = jnp.sum(jnp.where(hit, unpadded[:, None], 0.0), axis=0, keepdims=True)
    if outer > 1:
        table = lax.psum(table, "dp", axis_index_groups=groups)
    table = jnp.broadcast_to(table, (8, LANES))
    set_mask = jnp.stack([position_set == s for s in range(2)]).astype(BF)
    set_mask = jnp.broadcast_to(set_mask[:, :, None], set_mask.shape + (width,))
    (mixed, frames_grad, *grads, gains) = run_layer(
        to_kernel(frames), to_kernel(cotangent),
        jnp.broadcast_to(dialogue[:, None], (dialogue.shape[0], LANES)),
        jnp.broadcast_to(padding[:, None], (padding.shape[0], LANES)),
        table, set_mask, to_kernel(attention_gain), to_kernel(feedforward_gain), weights,
    )
    index = lax.axis_index("dp")
    gains = gains[0:4]
    if outer > 1:
        grads = [
            lax.psum_scatter(g, "dp", scatter_dimension=a, tiled=True, axis_index_groups=groups)
            for g, a in zip(grads, axes)
        ]
        gains = from_kernel(lax.psum(gains, "dp", axis_index_groups=groups))
    gains = lax.dynamic_slice_in_dim(gains, index * (width // dp), width // dp, axis=1)
    return (from_kernel(mixed), from_kernel(frames_grad), *grads, gains[0:2], gains[2:4])


def solution(mesh):
    column = P(None, "dp", "tensor")
    row = P(None, "tensor", "dp")
    rows = P("dp", None, None)
    in_specs = (
        rows, rows, P("dp"), P("dp"), P(),
        column, column, column, row, column, column, row, P(), P(),
    )
    out_specs = (
        rows, rows, column, column, column, row, column, column, row, P(None, "dp"), P(None, "dp"),
    )
    return jax.shard_map(per_device, mesh=mesh, in_specs=in_specs, out_specs=out_specs, check_vma=False)
```

time: 1410 us -> 273 us (0.19)
  waiting for transfers between devices: 1140 us -> 0 us
  Pallas kernels: 0 us -> 249 us
  local copies, waits for them, and re-layouts: 98.7 us -> 16.8 us
  matrix products: 67.8 us -> 0 us
  other arithmetic: 53.3 us -> 0.77 us
  blocking collectives: 31.6 us -> 0 us
  between operations: 15.9 us -> 0.7 us
    reduce_scatter x5 -> x0, waiting for transfers between devices: 487 us -> none  [the longest x1 131 us: per_device(): lax.psum_scatter(up_grad, 'dp', scatter_dimension=1, tiled=True)]
    unnamed x21 -> x0, waiting for transfers between devices: 348 us -> none
    all_gather x7 -> x0, waiting for transfers between devices: 282 us -> none  [the longest x1 54.2 us: per_device(): lax.all_gather(up_weight, 'dp', axis=1, tiled=True)]
    pallas_call x0 -> x1, Pallas kernels: none -> 249 us  [run_layer(): pl.pallas_call(layer_kernel, out_shape=out_shape, in_specs=[spec] * 15, o...]
    dot_general x48 -> x0, matrix products: 67.8 us -> none  [the longest x14 23.6 us: weight_gradient(): jnp.einsum('fpk,fpe->ke', jnp.where(set_mask, values, zero_low), gradient...]
    another operation x9 -> x1, other arithmetic: 40.1 us -> 0.67 us  [per_device(): set_mask = jnp.stack([position_set == s for s in range(2)]).astype(BF)]
    unnamed x133 -> x31, local copies, waits for them, and re-layouts: 50.4 us -> 12.7 us
    psum x1 -> x0, blocking collectives: 31.6 us -> none  [per_device(): counts = lax.psum(jnp.sum(dialogue_table * unpadded[:, None], axis=0), 'dp')]
  transfers between devices with their start and end apart: 18 -> 0, of which waited for: 16 -> 0; matrix products, arithmetic and copies ran while one was open for 11% -> 0% of each run, Pallas kernels for 0% -> 0%
where the time goes in v1:
time: 273 us; the launch traced here: 268 us
  Pallas kernels  249 us (91%)
  local copies, waits for them, and re-layouts  16.8 us (6%)
    pallas_call x1, Pallas kernels, run_layer(): pl.pallas_call(layer_kernel, out_shape=out_shape, in_specs=[spec] * 15, o...  249 us
    unnamed x31, local copies, waits for them, and re-layouts  12.7 us

profile of v1, /device:TPU:0, one launch (start us, length us, event | category | flops | bytes accessed | tf_op | source)
XLA Modules:
  0.0 267.7 jit_solution(2624993658640608966)
XLA Ops:
  0.7 0.7 compare_bitcast_fusion.1
  1.3 0.7 broadcast_in_dim.25.set_mask
  2.1 2.1 copy.26.wd
  4.2 1.7 copy.25.wo
  5.9 0.1 select_reduce_fusion
  6.0 0.6 broadcast_in_dim.24.table
  6.6 0.7 broadcast_in_dim.20.dialogue
  7.3 0.7 broadcast_in_dim.21.padding
  7.9 249.4 %layer.1 = (bf16[8,16,1024]{2,1,0:T(8,128)(2,1)}, bf16[8,16,1024]{2,1,0:T(8,128)(2,1)}, f32[2,64,512]{2,1,0:T(8,128)}, f32[2,64,512]{2,1,0:T(8,128)}, f32[2,64,5...) custom-call(bf16[8,16,1024]{2,1,0:T(8,128)(2,1)} %frames.1, ...), custom_call_target="tpu_custom_call" | custom-call | flops 10000000000 | bytes 10000000 | tf_op jit(solution)/shard_map/layer/pallas_call | solution.py:611
  257.4 0.0 copy-start.2
  257.4 0.8 slice.9
  258.2 0.1 constant_dynamic-slice_fusion
  258.3 0.6 fusion
  258.8 2.7 %copy.28 = f32[2,1408,64]{1,2,0:T(8,128)} copy(f32[2,1408,64]{2,1,0:T(8,128)} %get-tuple-element.39) | data formatting | bytes 1441792
  261.5 0.9 copy.27
  262.4 0.7 copy.36
  263.1 0.7 copy.37
  263.9 0.7 copy.38
  264.6 0.0 copy-done.4
  264.6 0.7 copy.39
  265.3 0.7 copy.40
  266.0 0.0 copy-done.1
  266.0 0.9 copy.41
  266.8 0.9 copy.42
  (19 shorter events, 0.0 us)
Async XLA Ops:
  0.6 5.3 %copy-start.9 = (s32[8]{0:T(128)S(1)}, s32[8]{0:T(128)}, u32[]{:S(2)}) copy-start(s32[8]{0:T(128)} %param.17) | copy-start | bytes 100
  0.7 5.3 %copy-start.8 = (s32[8]{0:T(128)S(1)}, s32[8]{0:T(128)}, u32[]{:S(2)}) copy-start(s32[8]{0:T(128)} %param.16) | copy-start | bytes 100
  257.4 4.2 %copy-start.2 = (f32[2,512,64]{2,1,0:T(8,128)S(1)}, f32[2,512,64]{2,1,0:T(8,128)}, u32[]{:S(2)}) copy-start(f32[2,512,64]{2,1,0:T(8,128)} %get-tuple-element.36) | copy-start | bytes 786436
  258.8 3.6 %copy-start.7 = (bf16[8,16,1024]{2,1,0:T(8,128)(2,1)S(1)}, bf16[8,16,1024]{2,1,0:T(8,128)(2,1)}, u32[]{:S(2)}) copy-start(bf16[8,16,1024]{2,1,0:T(8,128)(2,1)} %get-tuple-element.57) | copy-start | bytes 786436
  258.8 4.3 %copy-start.6 = (bf16[8,16,1024]{2,1,0:T(8,128)(2,1)S(1)}, bf16[8,16,1024]{2,1,0:T(8,128)(2,1)}, u32[]{:S(2)}) copy-start(bf16[8,16,1024]{2,1,0:T(8,128)(2,1)} %get-tuple-element.58) | copy-start | bytes 786436
  261.5 2.3 copy-start.5
  261.5 3.0 %copy-start.4 = (f32[2,64,512]{2,1,0:T(8,128)S(1)}, f32[2,64,512]{2,1,0:T(8,128)}, u32[]{:S(2)}) copy-start(f32[2,64,512]{2,1,0:T(8,128)} %get-tuple-element.60) | copy-start | bytes 786436
  261.5 3.7 %copy-start.3 = (f32[2,64,512]{2,1,0:T(8,128)S(1)}, f32[2,64,512]{2,1,0:T(8,128)}, u32[]{:S(2)}) copy-start(f32[2,64,512]{2,1,0:T(8,128)} %get-tuple-element.61) | copy-start | bytes 786436
  262.4 3.5 %copy-start.1 = (f32[2,64,1408]{2,1,0:T(8,128)S(1)}, f32[2,64,1408]{2,1,0:T(8,128)}, u32[]{:S(2)}) copy-start(f32[2,64,1408]{2,1,0:T(8,128)} %get-tuple-element.63) | copy-start | bytes 2162692
  263.9 3.0 %copy-start = (f32[2,64,1408]{2,1,0:T(8,128)S(1)}, f32[2,64,1408]{2,1,0:T(8,128)}, u32[]{:S(2)}) copy-start(f32[2,64,1408]{2,1,0:T(8,128)} %get-tuple-element.64) | copy-start | bytes 2162692

commit v2 on v1

v2 whole, which is shorter than its diff:
```python
import jax
import jax.numpy as jnp
from jax import lax
from jax.experimental import pallas as pl
from jax.experimental.pallas import tpu as pltpu
from jax.sharding import PartitionSpec as P

HDIM = 64
EPSILON = 1e-05
INNER = 16
ZN = 4
LANES = 128
CUTS = 2
MESH = pl.DeviceIdType.MESH
BF = jnp.bfloat16
F32 = jnp.float32
NN = (((1,), (0,)), ((), ()))
NT = (((1,), (1,)), ((), ()))
TN = (((0,), (0,)), ((), ()))
QKV, OUT, UPS, DOWN = range(4)


def dot(a, b, dims=NN):
    return lax.dot_general(a, b, dims, preferred_element_type=F32)


def layer_kernel(
    frames, cot, dialogue, padding, position_set, gain_one, gain_two,
    wq, wk, wv, wo, wg, wu, wd,
    fi0, fi1, fi2, fi3, halves, gains_out,
    st0, st1, st2, st3, ga0, ga1, ga2, ga3, w0, w1, w2, w3,
    dw0, dw1, dw2, dw3, rc0, rc1, rc2, rc3, sx0, sx1, sx2, sx3, rx0, rx1, rx2, rx3,
    set_mask, n1, sd, n2, hl, pf,
    sb, sr, so, ru, rd,
    qs, ks, vs, att2, probs, act2, gu2, gt, up,
    cnt, gain_col, gain_face,
    u_one, u_two, hid, hgrad, small,
    sp_s, sp_r, mc_s, mc_r, fw_s, ag_s, ag_r, rs_sib_s, rs_sib_r, rs_s, rs_ru, rs_rd,
    gc_s, gc_r, gx_s, gx_r, gf_s, gf_r, c_s, c_r, y_s, y_r, gcs, gcr, gfs, gfr,
):
    st, ga, w = (st0, st1, st2, st3), (ga0, ga1, ga2, ga3), (w0, w1, w2, w3)
    dw, fi = (dw0, dw1, dw2, dw3), (fi0, fi1, fi2, fi3)
    rc, sx, rx = (rc0, rc1, rc2, rc3), (sx0, sx1, sx2, sx3), (rx0, rx1, rx2, rx3)
    idx = lax.axis_index("dp")
    y = lax.axis_index("tensor")
    inner = lax.rem(idx, INNER)
    base = idx - inner
    z = lax.div(inner, 4)
    x = lax.rem(lax.div(inner, 2), 2)
    c = lax.rem(inner, 2)

    def dev(zz, xx, cc, yy):
        return (base + zz * 4 + xx * 2 + cc, yy)

    def flip(v, bit):
        return 1 - v if bit else v

    def hop(k):
        return lax.rem(z + k, ZN)

    def remote(src, dst, ssem, rsem, device):
        return pltpu.make_async_remote_copy(
            src_ref=src, dst_ref=dst, send_sem=ssem, recv_sem=rsem,
            device_id=device, device_id_type=MESH,
        )

    partner = dev(z, x, c, 1 - y)
    sibling = dev(z, x, 1 - c, y)
    across = dev(z, 1 - x, c, y)
    above = dev(hop(1), x, c, y)
    below = dev(hop(ZN - 1), x, c, y)
    column = [dev(hop(k), x, c, y) for k in (1, 2, 3)]
    face = [
        (flip(x, a), flip(c, b), flip(y, d))
        for a in (0, 1) for b in (0, 1) for d in (0, 1) if a or b or d
    ]
    rows, width = n1.shape[1:]
    group = 8 * rows
    half = rows // 16
    qb = w0.shape[1] // 6
    fb = w3.shape[1] // 2
    units = wg.shape[2]
    d_rows = wq.shape[1]
    own_slot = 2 * z + y
    mine = pl.ds(half * y, half)
    slice_mine = 2 * x + c
    pending = []

    def send(cond, src, dst, ssem, rsem, device):
        def go():
            remote(src, dst, ssem, rsem, device).start()

        def done():
            remote(src, dst, ssem, rsem, device).wait_send()

        if cond is None:
            go()
        else:
            pl.when(cond)(go)
        pending.append((cond, done))

    def keep(src, dst, rsem):
        pltpu.make_async_copy(src, dst, rsem).start()

    def arrived(dst, rsem, cond=None):
        def wait():
            remote(dst, dst, rsem, rsem, sibling).wait_recv()

        if cond is None:
            wait()
        else:
            pl.when(cond)(wait)

    barrier = pltpu.get_barrier_semaphore()
    for d in column:
        pl.semaphore_signal(barrier, inc=1, device_id=d, device_id_type=MESH)
    for xx, cc, yy in face:
        pl.semaphore_signal(barrier, inc=1, device_id=dev(z, xx, cc, yy), device_id_type=MESH)

    def stage(g, parts, cols, total):
        for b in range(ZN):
            n = min(cols, total - b * cols)
            for s in range(2):
                for j, ref in enumerate(parts):
                    at = (s * len(parts) + j) * cols
                    st[g][b, :, at:at + n] = ref[s, :, b * cols:b * cols + n]
                    if n < cols:
                        st[g][b, :, at + n:at + cols] = jnp.zeros((d_rows, cols - n), BF)

    stage(QKV, (wq, wk, wv), qb, wq.shape[2])

    row_at = lax.broadcasted_iota(jnp.int32, (16, width), 0)
    row_set = jnp.zeros((16, width), jnp.int32)
    for p in range(16):
        row_set = jnp.where(row_at == p, position_set[p], row_set)
    for s in range(2):
        set_mask[s] = jnp.where(row_set == s, 1.0, 0.0).astype(BF)

    def gain_full(gain):
        m1 = set_mask[1].astype(F32)
        return jnp.where(m1 > 0.5, gain[1:2, :], gain[0:1, :])

    def tile_rows(v):
        return jnp.broadcast_to(v[None], (half, 16, v.shape[1])).reshape(rows, v.shape[1])

    def normalize(values, gain):
        inverse = lax.rsqrt(jnp.sum(values * values, axis=-1, keepdims=True) / width + EPSILON)
        unit = values * inverse
        return unit, inverse, (unit * tile_rows(gain_full(gain))).astype(BF)

    def own_rows(ref):
        return ref[mine].reshape(rows, width).astype(F32)

    def zero(ref):
        ref[...] = jnp.zeros_like(ref)

    unit, inverse, normed = normalize(own_rows(frames), gain_one)
    u_one[...] = unit
    small[0] = jnp.broadcast_to(inverse, (rows, LANES))
    n1[own_slot] = normed
    pl.when(z == 0)(lambda: zero(ru))
    pl.when(z == ZN - 1)(lambda: zero(rd))

    lane = lax.broadcasted_iota(jnp.int32, (8, LANES), 1)
    table = jnp.zeros((8, LANES), F32)
    for f in range(frames.shape[0]):
        table = table + jnp.where(lane == dialogue[f], padding[f].astype(F32), 0.0)
    cnt[0, z] = table
    pl.semaphore_wait(barrier, len(column) + len(face))

    def spread(g, k):
        send(None, st[g].at[hop(k)], ga[g].at[z], sp_s.at[g, k], sp_r.at[g, z], dev(hop(k), x, c, y))

    def piece_of(g, k, xx, cc):
        piece = hop(k) * 4 + 2 * xx + cc
        return w[g].at[pl.ds(pl.multiple_of(piece * d_rows, d_rows), d_rows), :], mc_r.at[g, piece]

    def multicast(g, k):
        if k:
            arrived(ga[g].at[hop(k)], sp_r.at[g, hop(k)])
        src = ga[g].at[hop(k)] if k else st[g].at[z]
        dst, rsem = piece_of(g, k, x, c)
        send(None, src, dst, mc_s.at[g, k, 0], rsem, across)
        send(None, src, dst, mc_s.at[g, k, 1], rsem, sibling)
        keep(src, dst, rsem)

    def forward(g, k):
        dst, rsem = piece_of(g, k, 1 - x, c)
        arrived(dst, rsem)
        send(None, dst, dst, fw_s.at[g, k], rsem, sibling)

    def weights_here(g):
        for k in range(ZN):
            for cc in (c, 1 - c):
                dst, rsem = piece_of(g, k, x, cc)
                arrived(dst, rsem)
            dst, rsem = piece_of(g, k, 1 - x, 1 - c)
            arrived(dst, rsem)

    cut_rows = rows // CUTS

    def cut(q):
        return pl.ds(q * cut_rows, cut_rows)

    def gather_send(which, buf, slot, q, cond, way, device):
        src = buf.at[slot, cut(q)]
        send(cond, src, src, ag_s.at[which, 3 * slot + way, q], ag_r.at[which, slot, q], device)

    def gather_start(which, buf):
        for q in range(CUTS):
            gather_send(which, buf, own_slot, q, z < ZN - 1, 1, above)
            gather_send(which, buf, own_slot, q, z > 0, 2, below)
            gather_send(which, buf, own_slot, q, None, 0, partner)

    def gather_step(which, buf, k):
        lo = 2 * jnp.maximum(z - k, 0) + y
        hi = 2 * jnp.minimum(z + k, ZN - 1) + y
        up, down = z >= k, z + k <= ZN - 1
        for q in range(CUTS):
            arrived(buf.at[lo, cut(q)], ag_r.at[which, lo, q], cond=up)
            gather_send(which, buf, lo, q, up & (z < ZN - 1), 1, above)
            gather_send(which, buf, lo, q, up, 0, partner)
            arrived(buf.at[hi, cut(q)], ag_r.at[which, hi, q], cond=down)
            gather_send(which, buf, hi, q, down & (z > 0), 2, below)
            gather_send(which, buf, hi, q, down, 0, partner)

    def gather_end(which, buf):
        slot = 2 * z + 1 - y
        for q in range(CUTS):
            arrived(buf.at[slot, cut(q)], ag_r.at[which, slot, q])
        for k in (1, 2, 3):
            lo = 2 * jnp.maximum(z - k, 0) + 1 - y
            hi = 2 * jnp.minimum(z + k, ZN - 1) + 1 - y
            for q in range(CUTS):
                arrived(buf.at[lo, cut(q)], ag_r.at[which, lo, q], cond=z >= k)
                arrived(buf.at[hi, cut(q)], ag_r.at[which, hi, q], cond=z + k <= ZN - 1)

    def far_first(i):
        orders = ((3, 2, 1, 0), (3, 0, 2, 1), (0, 3, 1, 2), (0, 1, 2, 3))
        b = jnp.int32(0)
        for zz, order in enumerate(orders):
            b = b + jnp.where(z == zz, order[i], 0)
        return b

    def scatter_put(n, partial):
        pf[n % 2] = partial.reshape(8, rows, width)

    def scatter_send(n, i):
        b = far_first(i)
        for q in range(CUTS):
            sb[n, b, cut(q), :] = pf[n % 2, 2 * b + 1 - y, cut(q), :].astype(BF)
            send(None, sb.at[n, b, cut(q)], sr.at[n, b, cut(q)], rs_sib_s.at[n, b, q], rs_sib_r.at[n, b, q], partner)

    def scatter_start(n, partial):
        scatter_put(n, partial)
        for i in range(4):
            scatter_send(n, i)

    def chip_sum(n, b, q):
        arrived(sr.at[n, b, cut(q)], rs_sib_r.at[n, b, q])
        return pf[n % 2, 2 * b + y, cut(q), :] + sr[n, b, cut(q), :].astype(F32)

    def scatter_chain(n, between=None):
        plan = (
            (True, 3, z <= 1), (False, 0, z >= 2), (True, 3, z == 2), (False, 0, z == 1),
            (True, 2, z <= 1), (False, 1, z >= 2), (True, 1, z == 0), (False, 2, z == 3),
        )
        for at, (rising, b, cond) in enumerate(plan):
            if rising:
                inflow, buf, r, target = z > 0, ru, rs_ru, above
            else:
                inflow, buf, r, target = z < ZN - 1, rd, rs_rd, below
            for q in range(CUTS):

                def step(b=b, q=q, inflow=inflow, buf=buf, r=r):
                    total = chip_sum(n, b, q)
                    arrived(buf.at[n, b, cut(q)], r.at[n, b, q], cond=inflow)
                    so[n, b, cut(q), :] = (total + buf[n, b, cut(q), :].astype(F32)).astype(BF)

                pl.when(cond)(step)
                send(cond, so.at[n, b, cut(q)], buf.at[n, b, cut(q)], rs_s.at[n, b, q], r.at[n, b, q], target)
            for action in (between or {}).get(at, ()):
                action()

    def scatter_end(n):
        totals = []
        for q in range(CUTS):
            total = chip_sum(n, z, q)
            arrived(ru.at[n, z, cut(q)], rs_ru.at[n, z, q], cond=z > 0)
            arrived(rd.at[n, z, cut(q)], rs_rd.at[n, z, q], cond=z < ZN - 1)
            totals.append(total + ru[n, z, cut(q), :].astype(F32) + rd[n, z, cut(q), :].astype(F32))
        return jnp.concatenate(totals, axis=0)

    def both_sets(v):
        n = v.shape[1]
        three = v.reshape(group // 16, 16, n)
        return jnp.concatenate([(three * set_mask[s, :, 0:n][None]).reshape(group, n) for s in range(2)], axis=1)

    def choose(v):
        n = v.shape[1] // 2
        m = jnp.broadcast_to(set_mask[1, :, 0:n].astype(F32)[None], (group // 16, 16, n)).reshape(group, n)
        return jnp.where(m > 0.5, v[:, n:], v[:, 0:n])

    def flat(buf):
        return buf[...].reshape(group, width)

    for k in (1, 2, 3):
        send(None, cnt.at[0, z], cnt.at[0, z], c_s.at[0, k], c_r.at[0, z], dev(hop(k), x, c, y))
    gather_start(0, n1)
    spread(QKV, 1)
    multicast(QKV, 0)
    stage(OUT, (wo,), qb, wo.shape[2])
    stage(UPS, (wg, wu), fb, units)
    stage(DOWN, (wd,), fb, units)
    for k in (1, 2, 3):
        arrived(cnt.at[0, hop(k)], c_r.at[0, hop(k)])
    cnt[1, slice_mine] = cnt[0, 0] + cnt[0, 1] + cnt[0, 2] + cnt[0, 3]
    for a, b in ((0, 1), (1, 0), (1, 1)):
        send(None, cnt.at[1, slice_mine], cnt.at[1, slice_mine], c_s.at[1, 2 * a + b], c_r.at[1, slice_mine],
             dev(z, flip(x, a), flip(c, b), y))
    gather_step(0, n1, 1)
    spread(QKV, 2)
    forward(QKV, 0)
    gather_step(0, n1, 2)
    spread(QKV, 3)
    for k in (2, 1, 3):
        spread(OUT, k)
    multicast(QKV, 3)
    gather_step(0, n1, 3)
    spread(UPS, 2)
    spread(UPS, 1)
    multicast(QKV, 2)
    forward(QKV, 3)
    multicast(QKV, 1)
    forward(QKV, 2)
    for a, b in ((0, 1), (1, 0), (1, 1)):
        j = 2 * flip(x, a) + flip(c, b)
        arrived(cnt.at[1, j], c_r.at[1, j])
    counts = cnt[1, 0] + cnt[1, 1] + cnt[1, 2] + cnt[1, 3]
    for f in range(frames.shape[0]):
        found = jnp.sum(jnp.where(lane == dialogue[f], counts, 0.0), axis=1, keepdims=True)
        loss = padding[f].astype(F32) * (frames.shape[0] * 1.0) / (found + 1.0)
        small[1, f:f + 1, :] = jnp.broadcast_to(loss[0:1, :], (1, LANES))
    frame_weight = small[1, mine, :]
    weight_rows = jnp.broadcast_to(frame_weight[:, None, 0:1], (half, 16, width)).reshape(rows, width)
    sd[own_slot] = (own_rows(cot) * weight_rows).astype(BF)
    forward(QKV, 1)
    multicast(OUT, 0)
    multicast(UPS, 0)
    gather_end(0, n1)
    weights_here(QKV)
    qkv = choose(dot(flat(n1), w[QKV][...])).astype(BF)
    qs[...] = qkv[:, 0:qb]
    ks[...] = qkv[:, qb:2 * qb]
    vs[...] = qkv[:, 2 * qb:3 * qb]
    for k in (2, 1, 3):
        multicast(OUT, k)
    forward(OUT, 0)

    bl = LANES
    r_at = lax.broadcasted_iota(jnp.int32, (bl, bl), 0)
    c_at = lax.broadcasted_iota(jnp.int32, (bl, bl), 1)
    seen = (c_at <= r_at) & (lax.div(r_at, 16) == lax.div(c_at, 16))
    heads = qb // HDIM
    head_of = lax.div(lax.broadcasted_iota(jnp.int32, (bl, qb), 1), HDIM)
    scale = HDIM ** (-0.5)

    def only(v, h):
        return jnp.where(head_of == h, v, jnp.zeros_like(v))

    attended = []
    for t in range(group // bl):
        at = pl.ds(t * bl, bl)
        q, kk, v = qs[at, :], ks[at, :], vs[at, :]
        out = jnp.zeros((bl, qb), F32)
        for h in range(heads):
            scores = dot(only(q, h), kk, NT) * scale
            scores = jnp.where(seen, scores, -1e30)
            e = jnp.exp(scores - jnp.max(scores, axis=-1, keepdims=True))
            e = jnp.where(seen, e, 0.0)
            p = e / jnp.sum(e, axis=-1, keepdims=True)
            probs[t, h] = p
            out = jnp.where(head_of == h, dot(p.astype(BF), v), out)
        attended.append(out.astype(BF))
    att2[...] = both_sets(jnp.concatenate(attended, axis=0))
    for k in (2, 1, 3):
        forward(OUT, k)
    weights_here(OUT)
    scatter_start(0, dot(att2[...], w[OUT][...], NT))
    multicast(UPS, 2)
    forward(UPS, 0)
    scatter_chain(0, {
        1: (lambda: gather_start(1, sd),),
        5: (lambda: multicast(UPS, 3), lambda: forward(UPS, 2)),
    })
    spread(UPS, 3)
    gather_step(1, sd, 1)
    attention = scatter_end(0)

    hidden = own_rows(frames) + attention
    hid[...] = hidden
    unit, inverse, normed = normalize(hidden, gain_two)
    u_two[...] = unit
    small[2] = jnp.broadcast_to(inverse, (rows, LANES))
    n2[own_slot] = normed
    gather_start(2, n2)
    spread(DOWN, 2)
    multicast(DOWN, 0)
    forward(UPS, 3)
    gather_step(2, n2, 1)
    gather_step(1, sd, 2)
    spread(DOWN, 1)
    multicast(UPS, 1)
    forward(DOWN, 0)
    gather_step(2, n2, 2)
    spread(DOWN, 3)
    forward(UPS, 1)
    gather_step(2, n2, 3)
    gather_step(1, sd, 3)
    for k in (2, 3, 1):
        multicast(DOWN, k)
    gather_end(1, sd)
    gather_end(2, n2)
    weights_here(UPS)

    gu = choose(dot(flat(n2), w[UPS][...]))
    gt[...] = gu[:, 0:fb]
    up[...] = gu[:, fb:2 * fb]
    for k in (2, 3, 1):
        forward(DOWN, k)
    weights_here(DOWN)
    active_grad = choose(dot(flat(sd), w[DOWN][...]))
    gate = gt[...]
    sig = jax.nn.sigmoid(gate)
    silu = gate * sig
    act2[...] = both_sets((silu * up[...]).astype(BF))
    gate_grad = (active_grad * up[...] * sig * (1.0 + gate * (1.0 - sig))).astype(BF)
    up_grad = (active_grad * silu).astype(BF)
    gu2[...] = both_sets(jnp.concatenate([gate_grad, up_grad], axis=1))
    scatter_start(1, dot(gu2[...], w[UPS][...], NT))

    def weight_grad(g, values, grads):
        dw[g][...] = dot(values, grads, TN).astype(BF).reshape(dw[g].shape)
        for xx in (1 - x, x):
            send(None, dw[g].at[:, 2 * xx + 1 - c], rc[g].at[xx], gc_s.at[g, xx], gc_r.at[g, xx], sibling)

    def reduce_across(g):
        arrived(rc[g].at[1 - x], gc_r.at[g, 1 - x])
        for k in (2, 1, 3, 0):
            zz = hop(k)
            sx[g][zz] = (dw[g][zz, 2 * (1 - x) + c].astype(F32) + rc[g][1 - x, zz].astype(F32)).astype(BF)
            send(None, sx[g].at[zz], rx[g].at[zz], gx_s.at[g, zz], gx_r.at[g, zz], across)

    def reduce_column(g, ks):
        for k in ks:
            zz = hop(k)
            if k == 2:
                arrived(rc[g].at[x], gc_r.at[g, x])
            arrived(rx[g].at[zz], gx_r.at[g, zz])
            total = dw[g][zz, 2 * x + c].astype(F32) + rc[g][x, zz].astype(F32) + rx[g][zz].astype(F32)
            if k:
                rx[g][zz] = total.astype(BF)
                send(None, rx[g].at[zz], fi[g].at[z], gf_s.at[g, k], gf_r.at[g, z], dev(zz, x, c, y))
            else:
                fi[g][z] = total.astype(BF)

    def reduce_end(g):
        for k in (1, 2, 3):
            arrived(fi[g].at[hop(k)], gf_r.at[g, hop(k)])

    weight_grad(DOWN, flat(sd), act2[...])
    weight_grad(UPS, flat(n2), gu2[...])
    scatter_chain(1, {1: (lambda: reduce_across(DOWN),), 3: (lambda: reduce_across(UPS),)})
    scatter_put(2, dot(act2[...], w[DOWN][...], NT))
    scatter_send(2, 0)
    scatter_send(2, 1)
    normed_two_grad = scatter_end(1)

    def set_sums(v, at):
        three = v.reshape(half, 16, width)
        for s in range(2):
            part = (three * set_mask[s].astype(F32)[None]).reshape(rows, width)
            gain_col[z, at + s:at + s + 1, :] = jnp.sum(part, axis=0, keepdims=True)

    def norm_back(gradient, gain, unit, inverse):
        scaled = gradient * tile_rows(gain_full(gain))
        return inverse * (scaled - unit * (jnp.sum(scaled * unit, axis=-1, keepdims=True) / width))

    unit = u_two[...]
    seed = own_rows(cot) * weight_rows
    hidden_grad = seed + norm_back(normed_two_grad, gain_two, unit, small[2][:, 0:1])
    hgrad[...] = hidden_grad
    hl[own_slot] = hidden_grad.astype(BF)
    gather_start(3, hl)
    gain_col[z] = jnp.zeros((8, width), F32)
    set_sums(normed_two_grad * unit, 2)
    gather_step(3, hl, 1)
    reduce_column(DOWN, (2,))
    gather_step(3, hl, 2)
    reduce_column(DOWN, (1,))
    gather_step(3, hl, 3)
    reduce_column(DOWN, (3, 0))
    reduce_column(UPS, (2,))
    scatter_send(2, 2)
    scatter_send(2, 3)
    gather_end(3, hl)

    datt = choose(dot(flat(hl), w[OUT][...])).astype(BF)
    gq, gk, gv = [], [], []
    for t in range(group // bl):
        at = pl.ds(t * bl, bl)
        q, kk, v = qs[at, :], ks[at, :], vs[at, :]
        da = datt[t * bl:(t + 1) * bl, :]
        tq = jnp.zeros((bl, qb), F32)
        tk, tv = tq, tq
        for h in range(heads):
            p = probs[t, h]
            dp = dot(only(da, h), v, NT)
            tv = jnp.where(head_of == h, dot(p.astype(BF), da, TN), tv)
            ds = (p * (dp - jnp.sum(dp * p, axis=-1, keepdims=True))).astype(BF)
            tq = jnp.where(head_of == h, dot(ds, kk) * scale, tq)
            tk = jnp.where(head_of == h, dot(ds, q, TN) * scale, tk)
        gq.append(tq.astype(BF))
        gk.append(tk.astype(BF))
        gv.append(tv.astype(BF))
    low_grads = jnp.concatenate([jnp.concatenate(v, axis=0) for v in (gq, gk, gv)], axis=1)
    gqkv2 = both_sets(low_grads)
    scatter_start(3, dot(gqkv2, w[QKV][...], NT))
    weight_grad(QKV, flat(n1), gqkv2)
    weight_grad(OUT, flat(hl), att2[...])
    scatter_chain(3, {1: (lambda: reduce_across(QKV), lambda: reduce_across(OUT))})
    reduce_column(UPS, (1, 3, 0))
    scatter_chain(2)
    normed_one_grad = scatter_end(3)
    unit = u_one[...]
    set_sums(normed_one_grad * unit, 0)
    for k in (1, 2, 3):
        send(None, gain_col.at[z], gain_col.at[z], gcs.at[k], gcr.at[z], dev(hop(k), x, c, y))
    result = hgrad[...] + norm_back(normed_one_grad, gain_one, unit, small[0][:, 0:1])
    halves[1, mine] = result.astype(BF).reshape(half, 16, width)
    send(None, halves.at[1, mine], halves.at[1, mine], y_s.at[1], y_r.at[1], partner)
    reduce_column(QKV, (2, 1, 3, 0))
    reduce_column(OUT, (2, 1, 3, 0))
    branch = scatter_end(2)
    halves[0, mine] = (hid[...] + branch).astype(BF).reshape(half, 16, width)
    send(None, halves.at[0, mine], halves.at[0, mine], y_s.at[0], y_r.at[0], partner)

    for k in (1, 2, 3):
        arrived(gain_col.at[hop(k)], gcr.at[hop(k)])
    place = 4 * x + 2 * c + y
    gain_face[place] = gain_col[0] + gain_col[1] + gain_col[2] + gain_col[3]
    for k, (xx, cc, yy) in enumerate(face):
        send(None, gain_face.at[place], gain_face.at[place], gfs.at[k], gfr.at[place], dev(z, xx, cc, yy))
    for g in (DOWN, UPS, QKV, OUT):
        reduce_end(g)
    for j in (0, 1):
        theirs = pl.ds(half * (1 - y), half)
        arrived(halves.at[j, theirs], y_r.at[j])
    total = gain_face[place]
    for xx, cc, yy in face:
        j = 4 * xx + 2 * cc + yy
        arrived(gain_face.at[j], gfr.at[j])
    total = gain_face[0]
    for j in range(1, 8):
        total = total + gain_face[j]
    gains_out[...] = total

    for cond, done in pending:
        if cond is None:
            done()
        else:
            pl.when(cond)(done)


def output_kernel(
    fi0, fi1, fi2, fi3, halves, gains,
    mixed, frames_grad, dq, dk, dv, do, dg, du, dd, first_gain, second_gain,
):
    inner = lax.rem(lax.axis_index("dp"), INNER)
    mixed[...] = halves[0]
    frames_grad[...] = halves[1]
    for fi, outs in ((fi0, (dq, dk, dv)), (fi1, (do,)), (fi2, (dg, du)), (fi3, (dd,))):
        cols = fi.shape[2] // (2 * len(outs))
        for b in range(ZN):
            n = min(cols, outs[0].shape[2] - b * cols)
            for s in range(2):
                for j, out in enumerate(outs):
                    at = (s * len(outs) + j) * cols
                    out[s, :, b * cols:b * cols + n] = fi[b, :, at:at + n].astype(F32)
    width = gains.shape[1]
    share = first_gain.shape[1]
    turned = pltpu.roll(gains[...], lax.rem(width - inner * share, width), 1)
    first_gain[...] = turned[0:2, 0:share]
    second_gain[...] = turned[2:4, 0:share]


def run_layer(frames, cot, dialogue, padding, position_set, gain_one, gain_two, weights):
    wq, wk, wv, wo, wg, wu, wd = weights
    width = frames.shape[2]
    rows = frames.shape[0] * frames.shape[1] // 2
    d_rows = wq.shape[1]
    qb = wq.shape[2] // ZN
    units = wg.shape[2]
    fb = -(-units // (ZN * LANES)) * LANES
    group = 8 * rows
    dma = pltpu.SemaphoreType.DMA
    vm = pltpu.VMEM
    shape = jax.ShapeDtypeStruct
    cols = (6 * qb, 2 * qb, 4 * fb, 2 * fb)
    blocks = [(ZN, d_rows, n) for n in cols]
    block_rows = (8, rows, width)
    four = (4, 4, rows, width)
    scratch = (
        [vm(b, BF) for b in blocks] * 2
        + [vm((width, n), BF) for n in cols]
        + [vm((ZN, 4, d_rows, n), BF) for n in cols]
        + [vm((2, ZN, d_rows, n), BF) for n in cols]
        + [vm((ZN, d_rows, n), BF) for n in cols] * 2
        + [vm((2, 16, width), BF)]
        + [vm(block_rows, BF)] * 4 + [vm((2,) + block_rows, F32)]
        + [vm(four, BF)] * 5
        + [vm((group, qb), BF)] * 3
        + [vm((group, 2 * qb), BF), vm((group // LANES, qb // HDIM, LANES, LANES), F32)]
        + [vm((group, 2 * fb), BF), vm((group, 4 * fb), BF), vm((group, fb), F32), vm((group, fb), F32)]
        + [vm((2, 4, 8, LANES), F32), vm((ZN, 8, width), F32), vm((8, 8, width), F32)]
        + [vm((rows, width), F32)] * 4 + [vm((3, rows, LANES), F32)]
        + [dma((4, 4)), dma((4, 4)), dma((4, 4, 2)), dma((4, INNER)), dma((4, 4)), dma((4, 24, CUTS)), dma((4, 8, CUTS))]
        + [dma((4, 4, CUTS))] * 5
        + [dma((4, 2)), dma((4, 2)), dma((4, 4)), dma((4, 4)), dma((4, 4)), dma((4, 4))]
        + [dma((2, 4)), dma((2, 4)), dma((2,)), dma((2,)), dma((4,)), dma((4,)), dma((8,)), dma((8,))]
    )
    spec = pl.BlockSpec(memory_space=pltpu.VMEM)
    scalars = pl.BlockSpec(memory_space=pltpu.SMEM)
    packed = pl.pallas_call(
        layer_kernel,
        out_shape=[shape(b, BF) for b in blocks] + [shape((2,) + frames.shape, BF), shape((8, width), F32)],
        in_specs=[spec] * 2 + [scalars] * 3 + [spec] * 9,
        out_specs=[spec] * 6,
        scratch_shapes=scratch,
        compiler_params=pltpu.CompilerParams(
            collective_id=0, has_side_effects=True, vmem_limit_bytes=63 * 2**20
        ),
        cost_estimate=pl.CostEstimate(flops=10**10, bytes_accessed=10**7, transcendentals=0),
        name="layer",
    )(frames, cot, dialogue, padding, position_set, gain_one, gain_two, *weights)
    grads = [shape(v.shape, F32) for v in weights]
    return pl.pallas_call(
        output_kernel,
        out_shape=[shape(frames.shape, BF)] * 2 + grads + [shape((2, d_rows), F32)] * 2,
        in_specs=[spec] * 6,
        out_specs=[spec] * 11,
        compiler_params=pltpu.CompilerParams(vmem_limit_bytes=63 * 2**20),
        cost_estimate=pl.CostEstimate(flops=10**6, bytes_accessed=10**7, transcendentals=0),
        name="outputs",
    )(*packed)


def per_device(
    frames, cotangent, dialogue, padding, position_set,
    query_weight, key_weight, value_weight, output_weight, gate_weight, up_weight, down_weight,
    attention_gain, feedforward_gain,
):
    dp = lax.axis_size("dp")
    outer = dp // INNER
    groups = [[o * INNER + i for o in range(outer)] for i in range(INNER)]
    width = frames.shape[-1]
    turn = (False, False, False, True, False, False, True)
    weights = [query_weight, key_weight, value_weight, output_weight, gate_weight, up_weight, down_weight]
    weights = [jnp.swapaxes(v, 1, 2) if t else v for v, t in zip(weights, turn)]

    def to_kernel(v):
        if outer == 1:
            return v
        cut = v.reshape(v.shape[:-1] + (outer, INNER, width // dp))
        return jnp.swapaxes(cut, -3, -2).reshape(v.shape)

    def from_kernel(v):
        if outer == 1:
            return v
        cut = v.reshape(v.shape[:-1] + (INNER, outer, width // dp))
        return jnp.swapaxes(cut, -3, -2).reshape(v.shape)

    if outer > 1:
        weights = [lax.all_gather(v, "dp", axis=1, tiled=True, axis_index_groups=groups) for v in weights]
    mixed, frames_grad, *rest = run_layer(
        to_kernel(frames), to_kernel(cotangent), dialogue, padding, position_set,
        to_kernel(attention_gain), to_kernel(feedforward_gain), weights,
    )
    grads, gains = rest[:7], rest[7:]
    if outer > 1:
        grads = [
            lax.psum_scatter(v, "dp", scatter_dimension=1, tiled=True, axis_index_groups=groups) for v in grads
        ]
        gains = [
            lax.psum_scatter(v, "dp", scatter_dimension=1, tiled=True, axis_index_groups=groups) for v in gains
        ]
    grads = [jnp.swapaxes(v, 1, 2) if t else v for v, t in zip(grads, turn)]
    return (from_kernel(mixed), from_kernel(frames_grad), *grads, *gains)


def solution(mesh):
    column = P(None, "dp", "tensor")
    row = P(None, "tensor", "dp")
    rows = P("dp", None, None)
    in_specs = (
        rows, rows, P("dp"), P("dp"), P(),
        column, column, column, row, column, column, row, P(), P(),
    )
    out_specs = (
        rows, rows, column, column, column, row, column, column, row, P(None, "dp"), P(None, "dp"),
    )
    return jax.shard_map(per_device, mesh=mesh, in_specs=in_specs, out_specs=out_specs, check_vma=False)
```

time: 273 us -> 199 us (0.73); the launches traced: 268 us -> 199 us
  Pallas kernels: 249 us -> 198 us
  local copies, waits for them, and re-layouts: 16.8 us -> 0 us
    pallas_call x1 -> x2, Pallas kernels: 249 us -> 198 us  [the longest x1 195 us: run_layer(): pl.pallas_call(layer_kernel, out_shape=[shape(b, BF) for b in blocks] + [...]
    unnamed x31 -> x0, local copies, waits for them, and re-layouts: 12.7 us -> none
where the time goes in v2:
time: 199 us
  Pallas kernels  198 us (99%)
    pallas_call x1, Pallas kernels, run_layer(): pl.pallas_call(layer_kernel, out_shape=[shape(b, BF) for b in blocks] + [...  195 us

profile of v2, /device:TPU:0, one launch (start us, length us, event | category | flops | bytes accessed | tf_op | source)
XLA Modules:
  0.0 199.0 jit_solution(15020305034666129838)
XLA Ops:
  0.6 194.9 %layer.1 = (bf16[4,64,768]{2,1,0:T(8,128)(2,1)}, bf16[4,64,256]{2,1,0:T(8,128)(2,1)}, bf16[4,64,1536]{2,1,0:T(8,128)(2,1)}, bf16[4,64,768]{2,1,0:T(8,128)(2,1)},...) custom-call(bf16[8,16,1024]{2,1,0:T(8,128)(2,1)} %frames.1, bf16[8,16,1024]{2,1,0:T(8,128)(2,1)} %cot.1, s32[8]{0:T(128)} %dialogue.1, ...), custom_call_target="tpu_custom_call" | custom-call | flops 10000000000 | bytes 10000000 | tf_op jit(solution)/shard_map/layer/pallas_call | solution.py:634
  195.5 3.5 %outputs.1 = (bf16[8,16,1024]{2,1,0:T(8,128)(2,1)}, bf16[8,16,1024]{2,1,0:T(8,128)(2,1)}, f32[2,64,512]{2,1,0:T(8,128)}, f32[2,64,512]{2,1,0:T(8,128)}, f32[2,64...) custom-call(bf16[4,64,768]{2,1,0:T(8,128)(2,1)} %get-tuple-element.2, ...), custom_call_target="tpu_custom_call" | custom-call | flops 1000000 | bytes 10000000 | tf_op jit(solution)/shard_map/outputs/pallas_call | solution.py:647

commit v3 on v2

v3 whole, which is shorter than its diff:
```python
import jax
import jax.numpy as jnp
from jax import lax
from jax.experimental import pallas as pl
from jax.experimental.pallas import tpu as pltpu
from jax.sharding import PartitionSpec as P

HDIM = 64
EPSILON = 1e-05
INNER = 16
ZN = 4
LANES = 128
CUTS = 2
MESH = pl.DeviceIdType.MESH
BF = jnp.bfloat16
F32 = jnp.float32
NN = (((1,), (0,)), ((), ()))
NT = (((1,), (1,)), ((), ()))
TN = (((0,), (0,)), ((), ()))
QKV, OUT, UPS, DOWN = range(4)
BLOCKS = (2, 2, 4, 4)


def dot(a, b, dims=NN):
    return lax.dot_general(a, b, dims, preferred_element_type=F32)


def layer_kernel(
    frames, cot, dialogue, padding, position_set, gain_one, gain_two,
    wq, wk, wv, wo, wg, wu, wd,
    fi0, fi1, fi2, fi3, halves, gains_out,
    st0, st1, st2, st3, ga0, ga1, ga2, ga3, w0, w1, w2, w3,
    dw0, dw1, dw2, dw3, rc0, rc1, rc2, rc3, sx0, sx1, sx2, sx3, rx0, rx1, rx2, rx3,
    set_mask, n1, sd, n2, hl, pf,
    sb, sr, so, ru, rd,
    qs, ks, vs, att2, probs, gqkv2, act2, gu2, gt, up,
    cnt, gain_col, gain_face,
    u_one, u_two, hid, hgrad, small,
    sp_s, sp_r, mc_s, mc_r, fw_s, ag_s, ag_r, rs_sib_s, rs_sib_r, rs_s, rs_ru, rs_rd,
    gc_s, gc_r, gx_s, gx_r, gf_s, gf_r, c_s, c_r, y_s, y_r, gcs, gcr, gfs, gfr,
):
    st, ga, w = (st0, st1, st2, st3), (ga0, ga1, ga2, ga3), (w0, w1, w2, w3)
    dw, fi = (dw0, dw1, dw2, dw3), (fi0, fi1, fi2, fi3)
    rc, sx, rx = (rc0, rc1, rc2, rc3), (sx0, sx1, sx2, sx3), (rx0, rx1, rx2, rx3)
    idx = lax.axis_index("dp")
    y = lax.axis_index("tensor")
    inner = lax.rem(idx, INNER)
    base = idx - inner
    z = lax.div(inner, 4)
    x = lax.rem(lax.div(inner, 2), 2)
    c = lax.rem(inner, 2)

    def dev(zz, xx, cc, yy):
        return (base + zz * 4 + xx * 2 + cc, yy)

    def flip(v, bit):
        return 1 - v if bit else v

    def hop(k):
        return lax.rem(z + k, ZN)

    def remote(src, dst, ssem, rsem, device):
        return pltpu.make_async_remote_copy(
            src_ref=src, dst_ref=dst, send_sem=ssem, recv_sem=rsem,
            device_id=device, device_id_type=MESH,
        )

    low = lax.rem(z, 2)
    partner = dev(z, x, c, 1 - y)
    beside = dev(z + 1 - 2 * low, x, c, y)
    sibling = dev(z, x, 1 - c, y)
    across = dev(z, 1 - x, c, y)
    above = dev(hop(1), x, c, y)
    below = dev(hop(ZN - 1), x, c, y)
    column = [dev(hop(k), x, c, y) for k in (1, 2, 3)]
    face = [
        (flip(x, a), flip(c, b), flip(y, d))
        for a in (0, 1) for b in (0, 1) for d in (0, 1) if a or b or d
    ]
    rows, width = n1.shape[1:]
    half = rows // 16
    qb = w0.shape[1] // 6
    fb = w3.shape[1] // 2
    units = wg.shape[2]
    d_rows = wq.shape[1]
    own_slot = 2 * z + y
    pair_slot = 2 * low + y
    mine = pl.ds(half * y, half)
    slice_mine = 2 * x + c
    pending = []

    def send(cond, src, dst, ssem, rsem, device):
        def go():
            remote(src, dst, ssem, rsem, device).start()

        def done():
            remote(src, dst, ssem, rsem, device).wait_send()

        if cond is None:
            go()
        else:
            pl.when(cond)(go)
        pending.append((cond, done))

    def arrived(dst, rsem, cond=None):
        def wait():
            remote(dst, dst, rsem, rsem, sibling).wait_recv()

        if cond is None:
            wait()
        else:
            pl.when(cond)(wait)

    barrier = pltpu.get_barrier_semaphore()
    for d in column:
        pl.semaphore_signal(barrier, inc=1, device_id=d, device_id_type=MESH)
    for xx, cc, yy in face:
        pl.semaphore_signal(barrier, inc=1, device_id=dev(z, xx, cc, yy), device_id_type=MESH)

    def stage(g, parts, cols, total):
        for b in range(BLOCKS[g]):
            n = min(cols, total - b * cols)
            for s in range(2):
                for j, ref in enumerate(parts):
                    at = (s * len(parts) + j) * cols
                    st[g][b, :, at:at + n] = ref[s, :, b * cols:b * cols + n]
                    if n < cols:
                        st[g][b, :, at + n:at + cols] = jnp.zeros((d_rows, cols - n), BF)

    stage(QKV, (wq, wk, wv), qb, wq.shape[2])

    row_at = lax.broadcasted_iota(jnp.int32, (16, width), 0)
    row_set = jnp.zeros((16, width), jnp.int32)
    for p in range(16):
        row_set = jnp.where(row_at == p, position_set[p], row_set)
    for s in range(2):
        set_mask[s] = jnp.where(row_set == s, 1.0, 0.0).astype(BF)

    def gain_full(gain):
        m1 = set_mask[1].astype(F32)
        return jnp.where(m1 > 0.5, gain[1:2, :], gain[0:1, :])

    def tile_rows(v):
        return jnp.broadcast_to(v[None], (half, 16, v.shape[1])).reshape(rows, v.shape[1])

    def normalize(values, gain):
        inverse = lax.rsqrt(jnp.sum(values * values, axis=-1, keepdims=True) / width + EPSILON)
        unit = values * inverse
        return unit, inverse, (unit * tile_rows(gain_full(gain))).astype(BF)

    def own_rows(ref):
        return ref[mine].reshape(rows, width).astype(F32)

    def zero(ref):
        for n in (1, 2):
            ref[n] = jnp.zeros(ref.shape[1:], ref.dtype)

    unit, inverse, normed = normalize(own_rows(frames), gain_one)
    u_one[...] = unit
    small[0] = jnp.broadcast_to(inverse, (rows, LANES))
    n1[pair_slot] = normed
    pl.when(z == 0)(lambda: zero(ru))
    pl.when(z == ZN - 1)(lambda: zero(rd))

    lane = lax.broadcasted_iota(jnp.int32, (8, LANES), 1)
    table = jnp.zeros((8, LANES), F32)
    for f in range(frames.shape[0]):
        table = table + jnp.where(lane == dialogue[f], padding[f].astype(F32), 0.0)
    cnt[0, z] = table
    pl.semaphore_wait(barrier, len(column) + len(face))

    def spread(g, k):
        send(None, st[g].at[lax.rem(hop(k), BLOCKS[g])], ga[g].at[z], sp_s.at[g, k], sp_r.at[g, z], dev(hop(k), x, c, y))

    def piece_of(g, k, xx, cc):
        piece = hop(k) * 4 + 2 * xx + cc
        return w[g].at[pl.ds(pl.multiple_of(piece * d_rows, d_rows), d_rows), :], mc_r.at[g, piece]

    def multicast(g, k):
        if k:
            arrived(ga[g].at[hop(k)], sp_r.at[g, hop(k)])
        src = ga[g].at[hop(k)] if k else st[g].at[lax.rem(z, BLOCKS[g])]
        dst, rsem = piece_of(g, k, x, c)
        send(None, src, dst, mc_s.at[g, k, 0], rsem, across)
        send(None, src, dst, mc_s.at[g, k, 1], rsem, sibling)
        dst[...] = src[...]

    def forward(g, k):
        dst, rsem = piece_of(g, k, 1 - x, c)
        arrived(dst, rsem)
        send(None, dst, dst, fw_s.at[g, k], rsem, sibling)

    def weights_here(g):
        for k in range(ZN):
            dst, rsem = piece_of(g, k, x, 1 - c)
            arrived(dst, rsem)
            dst, rsem = piece_of(g, k, 1 - x, 1 - c)
            arrived(dst, rsem)

    cut_rows = rows // CUTS

    def cut(q):
        return pl.ds(q * cut_rows, cut_rows)

    def gather_send(which, buf, slot, q, cond, way, device):
        src = buf.at[slot, cut(q)]
        send(cond, src, src, ag_s.at[which, 3 * slot + way, q], ag_r.at[which, slot, q], device)

    def gather_start(which, buf):
        for q in range(CUTS):
            gather_send(which, buf, own_slot, q, z < ZN - 1, 1, above)
            gather_send(which, buf, own_slot, q, z > 0, 2, below)
            gather_send(which, buf, own_slot, q, None, 0, partner)

    def gather_step(which, buf, k):
        lo = 2 * jnp.maximum(z - k, 0) + y
        hi = 2 * jnp.minimum(z + k, ZN - 1) + y
        up, down = z >= k, z + k <= ZN - 1
        for q in range(CUTS):
            arrived(buf.at[lo, cut(q)], ag_r.at[which, lo, q], cond=up)
            gather_send(which, buf, lo, q, up & (z < ZN - 1), 1, above)
            gather_send(which, buf, lo, q, up, 0, partner)
            arrived(buf.at[hi, cut(q)], ag_r.at[which, hi, q], cond=down)
            gather_send(which, buf, hi, q, down & (z > 0), 2, below)
            gather_send(which, buf, hi, q, down, 0, partner)

    def gather_end(which, buf):
        slot = 2 * z + 1 - y
        for q in range(CUTS):
            arrived(buf.at[slot, cut(q)], ag_r.at[which, slot, q])
        for k in (1, 2, 3):
            lo = 2 * jnp.maximum(z - k, 0) + 1 - y
            hi = 2 * jnp.minimum(z + k, ZN - 1) + 1 - y
            for q in range(CUTS):
                arrived(buf.at[lo, cut(q)], ag_r.at[which, lo, q], cond=z >= k)
                arrived(buf.at[hi, cut(q)], ag_r.at[which, hi, q], cond=z + k <= ZN - 1)

    def pair_start(which, buf):
        for q in range(CUTS):
            gather_send(which, buf, pair_slot, q, None, 1, beside)
            gather_send(which, buf, pair_slot, q, None, 0, partner)

    def pair_step(which, buf):
        slot = 2 * (1 - low) + y
        for q in range(CUTS):
            arrived(buf.at[slot, cut(q)], ag_r.at[which, slot, q])
            gather_send(which, buf, slot, q, None, 0, partner)

    def pair_end(which, buf):
        slot, far = 2 * low + 1 - y, 2 * (1 - low) + 1 - y
        for q in range(CUTS):
            arrived(buf.at[slot, cut(q)], ag_r.at[which, slot, q])
            arrived(buf.at[far, cut(q)], ag_r.at[which, far, q])

    def far_first(i):
        orders = ((3, 2, 1, 0), (3, 0, 2, 1), (0, 3, 1, 2), (0, 1, 2, 3))
        b = jnp.int32(0)
        for zz, order in enumerate(orders):
            b = b + jnp.where(z == zz, order[i], 0)
        return b

    def scatter_put(n, partial):
        blocks = partial.shape[0] // rows
        pf[n % 2, 0:blocks] = partial.reshape(blocks, rows, width)

    def scatter_send(n, i, b=None):
        b = far_first(i) if b is None else b
        for q in range(CUTS):
            sb[n, b, cut(q), :] = pf[n % 2, 2 * b + 1 - y, cut(q), :].astype(BF)
            send(None, sb.at[n, b, cut(q)], sr.at[n, b, cut(q)], rs_sib_s.at[n, b, q], rs_sib_r.at[n, b, q], partner)

    def chip_sum(n, b, q):
        arrived(sr.at[n, b, cut(q)], rs_sib_r.at[n, b, q])
        return pf[n % 2, 2 * b + y, cut(q), :] + sr[n, b, cut(q), :].astype(F32)

    plan = (
        (True, 3, z <= 1), (False, 0, z >= 2), (True, 3, z == 2), (False, 0, z == 1),
        (True, 2, z <= 1), (False, 1, z >= 2), (True, 1, z == 0), (False, 2, z == 3),
    )

    def scatter_step(n, at):
        rising, b, cond = plan[at]
        if rising:
            inflow, buf, r, target = z > 0, ru, rs_ru, above
        else:
            inflow, buf, r, target = z < ZN - 1, rd, rs_rd, below
        for q in range(CUTS):

            def step(q=q):
                total = chip_sum(n, b, q)
                arrived(buf.at[n, b, cut(q)], r.at[n, b, q], cond=inflow)
                so[n, b, cut(q), :] = (total + buf[n, b, cut(q), :].astype(F32)).astype(BF)

            pl.when(cond)(step)
            send(cond, so.at[n, b, cut(q)], buf.at[n, b, cut(q)], rs_s.at[n, b, q], r.at[n, b, q], target)

    def scatter_end(n):
        totals = []
        for q in range(CUTS):
            total = chip_sum(n, z, q)
            arrived(ru.at[n, z, cut(q)], rs_ru.at[n, z, q], cond=z > 0)
            arrived(rd.at[n, z, cut(q)], rs_rd.at[n, z, q], cond=z < ZN - 1)
            totals.append(total + ru[n, z, cut(q), :].astype(F32) + rd[n, z, cut(q), :].astype(F32))
        return jnp.concatenate(totals, axis=0)

    def pair_scatter_send(n):
        scatter_send(n, 2, 1 - low)
        scatter_send(n, 3, low)

    def pair_scatter_step(n):
        b = 1 - low
        for q in range(CUTS):
            so[n, b, cut(q), :] = chip_sum(n, b, q).astype(BF)
            send(None, so.at[n, b, cut(q)], ru.at[n, b, cut(q)], rs_s.at[n, b, q], rs_ru.at[n, b, q], beside)

    def pair_scatter_end(n):
        totals = []
        for q in range(CUTS):
            total = chip_sum(n, low, q)
            arrived(ru.at[n, low, cut(q)], rs_ru.at[n, low, q])
            totals.append(total + ru[n, low, cut(q), :].astype(F32))
        return jnp.concatenate(totals, axis=0)

    def both_sets(v):
        count, n = v.shape
        three = v.reshape(count // 16, 16, n)
        return jnp.concatenate([(three * set_mask[s, :, 0:n][None]).reshape(count, n) for s in range(2)], axis=1)

    def choose(v):
        count, n = v.shape[0], v.shape[1] // 2
        m = jnp.broadcast_to(set_mask[1, :, 0:n].astype(F32)[None], (count // 16, 16, n)).reshape(count, n)
        return jnp.where(m > 0.5, v[:, n:], v[:, 0:n])

    def flat(buf):
        return buf[...].reshape(buf.shape[0] * rows, width)

    def weight_grad(g, values, grads):
        dw[g][...] = dot(values, grads, TN).astype(BF).reshape(dw[g].shape)
        for xx in (1 - x, x):
            send(None, dw[g].at[:, 2 * xx + 1 - c], rc[g].at[xx], gc_s.at[g, xx], gc_r.at[g, xx], sibling)

    def reduce_across(g):
        arrived(rc[g].at[1 - x], gc_r.at[g, 1 - x])
        for k in (2, 1, 3, 0):
            zz = hop(k)
            sx[g][zz] = (dw[g][zz, 2 * (1 - x) + c].astype(F32) + rc[g][1 - x, zz].astype(F32)).astype(BF)
            send(None, sx[g].at[zz], rx[g].at[zz], gx_s.at[g, zz], gx_r.at[g, zz], across)

    def reduce_column(g, k):
        zz = hop(k)
        if k == 2:
            arrived(rc[g].at[x], gc_r.at[g, x])
        arrived(rx[g].at[zz], gx_r.at[g, zz])
        total = dw[g][zz, 2 * x + c].astype(F32) + rc[g][x, zz].astype(F32) + rx[g][zz].astype(F32)
        if k:
            rx[g][zz] = total.astype(BF)
            send(None, rx[g].at[zz], fi[g].at[z], gf_s.at[g, k], gf_r.at[g, z], dev(zz, x, c, y))
        else:
            fi[g][z] = total.astype(BF)

    def reduce_end(g):
        for k in (1, 2, 3):
            arrived(fi[g].at[hop(k)], gf_r.at[g, hop(k)])

    def counts_start():
        for k in (1, 2, 3):
            send(None, cnt.at[0, z], cnt.at[0, z], c_s.at[0, k], c_r.at[0, z], dev(hop(k), x, c, y))

    def counts_step():
        for k in (1, 2, 3):
            arrived(cnt.at[0, hop(k)], c_r.at[0, hop(k)])
        cnt[1, slice_mine] = cnt[0, 0] + cnt[0, 1] + cnt[0, 2] + cnt[0, 3]
        for a, b in ((0, 1), (1, 0), (1, 1)):
            send(None, cnt.at[1, slice_mine], cnt.at[1, slice_mine], c_s.at[1, 2 * a + b], c_r.at[1, slice_mine],
                 dev(z, flip(x, a), flip(c, b), y))

    def seed_rows():
        frame_weight = small[1, mine, :]
        weight_rows = jnp.broadcast_to(frame_weight[:, None, 0:1], (half, 16, width)).reshape(rows, width)
        return own_rows(cot) * weight_rows

    def seed_here():
        for a, b in ((0, 1), (1, 0), (1, 1)):
            j = 2 * flip(x, a) + flip(c, b)
            arrived(cnt.at[1, j], c_r.at[1, j])
        counts = cnt[1, 0] + cnt[1, 1] + cnt[1, 2] + cnt[1, 3]
        for f in range(frames.shape[0]):
            found = jnp.sum(jnp.where(lane == dialogue[f], counts, 0.0), axis=1, keepdims=True)
            loss = padding[f].astype(F32) * (frames.shape[0] * 1.0) / (found + 1.0)
            small[1, f:f + 1, :] = jnp.broadcast_to(loss[0:1, :], (1, LANES))
        sd[own_slot] = seed_rows().astype(BF)

    def stage_rest():
        stage(OUT, (wo,), qb, wo.shape[2])
        stage(UPS, (wg, wu), fb, units)
        stage(DOWN, (wd,), fb, units)

    bl = LANES
    r_at = lax.broadcasted_iota(jnp.int32, (bl, bl), 0)
    c_at = lax.broadcasted_iota(jnp.int32, (bl, bl), 1)
    seen = (c_at <= r_at) & (lax.div(r_at, 16) == lax.div(c_at, 16))
    heads = qb // HDIM
    head_of = lax.div(lax.broadcasted_iota(jnp.int32, (bl, qb), 1), HDIM)
    scale = HDIM ** (-0.5)

    def only(v, h):
        return jnp.where(head_of == h, v, jnp.zeros_like(v))

    def project_heads():
        qkv = choose(dot(flat(n1), w[QKV][...])).astype(BF)
        qs[...] = qkv[:, 0:qb]
        ks[...] = qkv[:, qb:2 * qb]
        vs[...] = qkv[:, 2 * qb:3 * qb]

    def attend():
        attended = []
        for t in range(qs.shape[0] // bl):
            at = pl.ds(t * bl, bl)
            q, kk, v = qs[at, :], ks[at, :], vs[at, :]
            out = jnp.zeros((bl, qb), F32)
            for h in range(heads):
                scores = dot(only(q, h), kk, NT) * scale
                scores = jnp.where(seen, scores, -1e30)
                e = jnp.exp(scores - jnp.max(scores, axis=-1, keepdims=True))
                e = jnp.where(seen, e, 0.0)
                p = e / jnp.sum(e, axis=-1, keepdims=True)
                probs[t, h] = p
                out = jnp.where(head_of == h, dot(p.astype(BF), v), out)
            attended.append(out.astype(BF))
        att2[...] = both_sets(jnp.concatenate(attended, axis=0))

    def attend_back():
        datt = choose(dot(flat(hl), w[OUT][...])).astype(BF)
        gq, gk, gv = [], [], []
        for t in range(qs.shape[0] // bl):
            at = pl.ds(t * bl, bl)
            q, kk, v = qs[at, :], ks[at, :], vs[at, :]
            da = datt[t * bl:(t + 1) * bl, :]
            tq = jnp.zeros((bl, qb), F32)
            tk, tv = tq, tq
            for h in range(heads):
                p = probs[t, h]
                dp = dot(only(da, h), v, NT)
                tv = jnp.where(head_of == h, dot(p.astype(BF), da, TN), tv)
                ds = (p * (dp - jnp.sum(dp * p, axis=-1, keepdims=True))).astype(BF)
                tq = jnp.where(head_of == h, dot(ds, kk) * scale, tq)
                tk = jnp.where(head_of == h, dot(ds, q, TN) * scale, tk)
            gq.append(tq.astype(BF))
            gk.append(tk.astype(BF))
            gv.append(tv.astype(BF))
        low_grads = jnp.concatenate([jnp.concatenate(v, axis=0) for v in (gq, gk, gv)], axis=1)
        gqkv2[...] = both_sets(low_grads)

    def gate_up():
        gu = choose(dot(flat(n2), w[UPS][...]))
        gt[...] = gu[:, 0:fb]
        up[...] = gu[:, fb:2 * fb]

    def gate_up_back():
        active_grad = choose(dot(flat(sd), w[DOWN][...]))
        gate = gt[...]
        sig = jax.nn.sigmoid(gate)
        silu = gate * sig
        act2[...] = both_sets((silu * up[...]).astype(BF))
        gate_grad = (active_grad * up[...] * sig * (1.0 + gate * (1.0 - sig))).astype(BF)
        up_grad = (active_grad * silu).astype(BF)
        gu2[...] = both_sets(jnp.concatenate([gate_grad, up_grad], axis=1))

    def set_sums(v, at):
        three = v.reshape(half, 16, width)
        for s in range(2):
            part = (three * set_mask[s].astype(F32)[None]).reshape(rows, width)
            gain_col[z, at + s:at + s + 1, :] = jnp.sum(part, axis=0, keepdims=True)

    def norm_back(gradient, gain, unit, inverse):
        scaled = gradient * tile_rows(gain_full(gain))
        return inverse * (scaled - unit * (jnp.sum(scaled * unit, axis=-1, keepdims=True) / width))

    def second_norm(attention):
        hidden = own_rows(frames) + attention
        hid[...] = hidden
        unit, inverse, normed = normalize(hidden, gain_two)
        u_two[...] = unit
        small[2] = jnp.broadcast_to(inverse, (rows, LANES))
        n2[own_slot] = normed

    def second_norm_back(normed_two_grad):
        unit = u_two[...]
        hidden_grad = seed_rows() + norm_back(normed_two_grad, gain_two, unit, small[2][:, 0:1])
        hgrad[...] = hidden_grad
        hl[pair_slot] = hidden_grad.astype(BF)
        gain_col[z] = jnp.zeros((8, width), F32)
        set_sums(normed_two_grad * unit, 2)

    def first_norm_back(normed_one_grad):
        unit = u_one[...]
        set_sums(normed_one_grad * unit, 0)
        result = hgrad[...] + norm_back(normed_one_grad, gain_one, unit, small[0][:, 0:1])
        halves[1, mine] = result.astype(BF).reshape(half, 16, width)

    def output_rows(branch):
        halves[0, mine] = (hid[...] + branch).astype(BF).reshape(half, 16, width)

    def half_send(j):
        send(None, halves.at[j, mine], halves.at[j, mine], y_s.at[j], y_r.at[j], partner)

    def half_end(j):
        theirs = pl.ds(half * (1 - y), half)
        arrived(halves.at[j, theirs], y_r.at[j])

    place = 4 * x + 2 * c + y

    def gains_start():
        for k in (1, 2, 3):
            send(None, gain_col.at[z], gain_col.at[z], gcs.at[k], gcr.at[z], dev(hop(k), x, c, y))

    def gains_step():
        for k in (1, 2, 3):
            arrived(gain_col.at[hop(k)], gcr.at[hop(k)])
        gain_face[place] = gain_col[0] + gain_col[1] + gain_col[2] + gain_col[3]
        for k, (xx, cc, yy) in enumerate(face):
            send(None, gain_face.at[place], gain_face.at[place], gfs.at[k], gfr.at[place], dev(z, xx, cc, yy))

    def gains_end():
        for xx, cc, yy in face:
            j = 4 * xx + 2 * cc + yy
            arrived(gain_face.at[j], gfr.at[j])
        total = gain_face[0]
        for j in range(1, 8):
            total = total + gain_face[j]
        gains_out[...] = total

    counts_start()
    spread(QKV, 3)
    spread(QKV, 1)
    stage_rest()
    multicast(QKV, 0)
    multicast(QKV, 1)
    spread(QKV, 2)
    multicast(QKV, 3)
    spread(OUT, 2)
    multicast(DOWN, 0)
    pair_start(0, n1)
    spread(OUT, 1)
    spread(OUT, 3)
    spread(DOWN, 1)
    spread(DOWN, 3)
    counts_step()
    multicast(OUT, 0)
    multicast(OUT, 1)
    multicast(OUT, 2)
    spread(DOWN, 2)
    seed_here()
    gather_start(1, sd)
    forward(QKV, 0)
    multicast(QKV, 2)
    pair_step(0, n1)
    spread(UPS, 1)
    forward(QKV, 1)
    spread(UPS, 3)
    forward(OUT, 2)
    forward(OUT, 1)
    multicast(OUT, 3)
    forward(QKV, 2)
    forward(OUT, 0)
    forward(QKV, 3)
    multicast(UPS, 0)
    forward(OUT, 3)
    multicast(DOWN, 2)
    weights_here(QKV)
    pair_end(0, n1)
    spread(UPS, 2)
    multicast(DOWN, 3)
    multicast(DOWN, 1)
    project_heads()
    weights_here(OUT)
    attend()
    scatter_put(0, dot(att2[...], w[OUT][...], NT))
    pair_scatter_send(0)
    gather_step(1, sd, 1)
    pair_scatter_step(0)
    multicast(UPS, 1)
    forward(UPS, 0)
    attention = pair_scatter_end(0)
    forward(DOWN, 2)
    multicast(UPS, 3)
    second_norm(attention)
    gather_start(2, n2)
    gather_step(1, sd, 2)
    gather_step(2, n2, 1)
    forward(UPS, 1)
    multicast(UPS, 2)
    forward(DOWN, 1)
    forward(DOWN, 3)
    gather_step(1, sd, 3)
    gather_step(2, n2, 2)
    forward(DOWN, 0)
    forward(UPS, 3)
    gather_step(2, n2, 3)
    forward(UPS, 2)
    weights_here(UPS)
    weights_here(DOWN)
    gather_end(1, sd)
    gather_end(2, n2)
    gate_up()
    gate_up_back()
    scatter_put(1, dot(gu2[...], w[UPS][...], NT))
    scatter_send(1, 0)
    weight_grad(DOWN, flat(sd), act2[...])
    scatter_send(1, 2)
    scatter_send(1, 1)
    scatter_put(2, dot(act2[...], w[DOWN][...], NT))
    scatter_send(2, 0)
    reduce_across(DOWN)
    scatter_step(1, 0)
    scatter_step(1, 1)
    scatter_step(1, 6)
    scatter_send(1, 3)
    scatter_step(1, 3)
    scatter_step(1, 7)
    reduce_column(DOWN, 2)
    scatter_send(2, 1)
    scatter_step(1, 2)
    weight_grad(UPS, flat(n2), gu2[...])
    scatter_step(1, 5)
    scatter_step(1, 4)
    scatter_send(2, 2)
    reduce_across(UPS)
    scatter_step(2, 1)
    scatter_step(2, 0)
    reduce_column(DOWN, 3)
    normed_two_grad = scatter_end(1)
    second_norm_back(normed_two_grad)
    scatter_step(2, 4)
    scatter_step(2, 5)
    pair_start(3, hl)
    reduce_column(UPS, 2)
    scatter_step(2, 6)
    reduce_column(DOWN, 1)
    pair_step(3, hl)
    scatter_send(2, 3)
    scatter_step(2, 2)
    reduce_column(UPS, 3)
    pair_end(3, hl)
    attend_back()
    weight_grad(QKV, flat(n1), gqkv2[...])
    scatter_put(3, dot(gqkv2[...], w[QKV][...], NT))
    pair_scatter_send(3)
    reduce_across(QKV)
    reduce_column(UPS, 1)
    pair_scatter_step(3)
    weight_grad(OUT, flat(hl), att2[...])
    reduce_column(QKV, 2)
    reduce_across(OUT)
    normed_one_grad = pair_scatter_end(3)
    first_norm_back(normed_one_grad)
    gains_start()
    reduce_column(UPS, 0)
    reduce_column(QKV, 1)
    scatter_step(2, 7)
    scatter_step(2, 3)
    reduce_column(QKV, 3)
    reduce_column(OUT, 2)
    gains_step()
    output_rows(scatter_end(2))
    half_send(1)
    reduce_end(UPS)
    half_send(0)
    reduce_end(DOWN)
    reduce_column(OUT, 1)
    reduce_column(OUT, 3)
    reduce_column(QKV, 0)
    reduce_column(OUT, 0)
    reduce_end(QKV)
    gains_end()
    reduce_column(DOWN, 0)
    half_end(0)
    half_end(1)
    reduce_end(OUT)
    for cond, done in pending:
        if cond is None:
            done()
        else:
            pl.when(cond)(done)


def output_kernel(
    fi0, fi1, fi2, fi3, halves, gains,
    mixed, frames_grad, dq, dk, dv, do, dg, du, dd, first_gain, second_gain,
):
    inner = lax.rem(lax.axis_index("dp"), INNER)
    mixed[...] = halves[0]
    frames_grad[...] = halves[1]
    for fi, outs in ((fi0, (dq, dk, dv)), (fi1, (do,)), (fi2, (dg, du)), (fi3, (dd,))):
        cols = fi.shape[2] // (2 * len(outs))
        blocks = -(-outs[0].shape[2] // cols)
        for b in range(blocks):
            n = min(cols, outs[0].shape[2] - b * cols)
            for s in range(2):
                for j, out in enumerate(outs):
                    at = (s * len(outs) + j) * cols
                    total = fi[b, :, at:at + n].astype(F32)
                    for other in range(b + blocks, ZN, blocks):
                        total = total + fi[other, :, at:at + n].astype(F32)
                    out[s, :, b * cols:b * cols + n] = total
    width = gains.shape[1]
    share = first_gain.shape[1]
    turned = pltpu.roll(gains[...], lax.rem(width - inner * share, width), 1)
    first_gain[...] = turned[0:2, 0:share]
    second_gain[...] = turned[2:4, 0:share]


def run_layer(frames, cot, dialogue, padding, position_set, gain_one, gain_two, weights):
    wq, wk, wv, wo, wg, wu, wd = weights
    width = frames.shape[2]
    rows = frames.shape[0] * frames.shape[1] // 2
    d_rows = wq.shape[1]
    qb = wq.shape[2] // BLOCKS[QKV]
    units = wg.shape[2]
    fb = -(-units // (BLOCKS[UPS] * LANES)) * LANES
    group, pair_group = 8 * rows, 4 * rows
    dma = pltpu.SemaphoreType.DMA
    vm = pltpu.VMEM
    shape = jax.ShapeDtypeStruct
    cols = (6 * qb, 2 * qb, 4 * fb, 2 * fb)
    blocks = [(ZN, d_rows, n) for n in cols]
    block_rows = (8, rows, width)
    pair_rows = (4, rows, width)
    four = (4, 4, rows, width)
    scratch = (
        [vm((count, d_rows, n), BF) for count, n in zip(BLOCKS, cols)]
        + [vm(b, BF) for b in blocks]
        + [vm((width, n), BF) for n in cols]
        + [vm((ZN, 4, d_rows, n), BF) for n in cols]
        + [vm((2, ZN, d_rows, n), BF) for n in cols]
        + [vm((ZN, d_rows, n), BF) for n in cols] * 2
        + [vm((2, 16, width), BF)]
        + [vm(pair_rows, BF), vm(block_rows, BF), vm(block_rows, BF), vm(pair_rows, BF)] + [vm((2,) + block_rows, F32)]
        + [vm(four, BF)] * 5
        + [vm((pair_group, qb), BF)] * 3
        + [vm((pair_group, 2 * qb), BF), vm((pair_group // LANES, qb // HDIM, LANES, LANES), F32)]
        + [vm((pair_group, 6 * qb), BF)]
        + [vm((group, 2 * fb), BF), vm((group, 4 * fb), BF), vm((group, fb), F32), vm((group, fb), F32)]
        + [vm((2, 4, 8, LANES), F32), vm((ZN, 8, width), F32), vm((8, 8, width), F32)]
        + [vm((rows, width), F32)] * 4 + [vm((3, rows, LANES), F32)]
        + [dma((4, 4)), dma((4, 4)), dma((4, 4, 2)), dma((4, INNER)), dma((4, 4)), dma((4, 24, CUTS)), dma((4, 8, CUTS))]
        + [dma((4, 4, CUTS))] * 5
        + [dma((4, 2)), dma((4, 2)), dma((4, 4)), dma((4, 4)), dma((4, 4)), dma((4, 4))]
        + [dma((2, 4)), dma((2, 4)), dma((2,)), dma((2,)), dma((4,)), dma((4,)), dma((8,)), dma((8,))]
    )
    spec = pl.BlockSpec(memory_space=pltpu.VMEM)
    scalars = pl.BlockSpec(memory_space=pltpu.SMEM)
    packed = pl.pallas_call(
        layer_kernel,
        out_shape=[shape(b, BF) for b in blocks] + [shape((2,) + frames.shape, BF), shape((8, width), F32)],
        in_specs=[spec] * 2 + [scalars] * 3 + [spec] * 9,
        out_specs=[spec] * 6,
        scratch_shapes=scratch,
        compiler_params=pltpu.CompilerParams(
            collective_id=0, has_side_effects=True, vmem_limit_bytes=63 * 2**20
        ),
        cost_estimate=pl.CostEstimate(flops=10**10, bytes_accessed=10**7, transcendentals=0),
        name="layer",
    )(frames, cot, dialogue, padding, position_set, gain_one, gain_two, *weights)
    grads = [shape(v.shape, F32) for v in weights]
    return pl.pallas_call(
        output_kernel,
        out_shape=[shape(frames.shape, BF)] * 2 + grads + [shape((2, d_rows), F32)] * 2,
        in_specs=[spec] * 6,
        out_specs=[spec] * 11,
        compiler_params=pltpu.CompilerParams(vmem_limit_bytes=63 * 2**20),
        cost_estimate=pl.CostEstimate(flops=10**6, bytes_accessed=10**7, transcendentals=0),
        name="outputs",
    )(*packed)


def per_device(
    frames, cotangent, dialogue, padding, position_set,
    query_weight, key_weight, value_weight, output_weight, gate_weight, up_weight, down_weight,
    attention_gain, feedforward_gain,
):
    dp = lax.axis_size("dp")
    outer = dp // INNER
    groups = [[o * INNER + i for o in range(outer)] for i in range(INNER)]
    width = frames.shape[-1]
    turn = (False, False, False, True, False, False, True)
    weights = [query_weight, key_weight, value_weight, output_weight, gate_weight, up_weight, down_weight]
    weights = [jnp.swapaxes(v, 1, 2) if t else v for v, t in zip(weights, turn)]

    def to_kernel(v):
        if outer == 1:
            return v
        cut = v.reshape(v.shape[:-1] + (outer, INNER, width // dp))
        return jnp.swapaxes(cut, -3, -2).reshape(v.shape)

    def from_kernel(v):
        if outer == 1:
            return v
        cut = v.reshape(v.shape[:-1] + (INNER, outer, width // dp))
        return jnp.swapaxes(cut, -3, -2).reshape(v.shape)

    if outer > 1:
        weights = [lax.all_gather(v, "dp", axis=1, tiled=True, axis_index_groups=groups) for v in weights]
    mixed, frames_grad, *rest = run_layer(
        to_kernel(frames), to_kernel(cotangent), dialogue, padding, position_set,
        to_kernel(attention_gain), to_kernel(feedforward_gain), weights,
    )
    grads, gains = rest[:7], rest[7:]
    if outer > 1:
        grads = [
            lax.psum_scatter(v, "dp", scatter_dimension=1, tiled=True, axis_index_groups=groups) for v in grads
        ]
        gains = [
            lax.psum_scatter(v, "dp", scatter_dimension=1, tiled=True, axis_index_groups=groups) for v in gains
        ]
    grads = [jnp.swapaxes(v, 1, 2) if t else v for v, t in zip(grads, turn)]
    return (from_kernel(mixed), from_kernel(frames_grad), *grads, *gains)


def solution(mesh):
    column = P(None, "dp", "tensor")
    row = P(None, "tensor", "dp")
    rows = P("dp", None, None)
    in_specs = (
        rows, rows, P("dp"), P("dp"), P(),
        column, column, column, row, column, column, row, P(), P(),
    )
    out_specs = (
        rows, rows, column, column, column, row, column, column, row, P(None, "dp"), P(None, "dp"),
    )
    return jax.shard_map(per_device, mesh=mesh, in_specs=in_specs, out_specs=out_specs, check_vma=False)
```

time: 199 us -> 168 us (0.84)
  Pallas kernels: 198 us -> 168 us
    pallas_call x1, Pallas kernels: 195 us -> 164 us  [run_layer(): pl.pallas_call(layer_kernel, out_shape=[shape(b, BF) for b in blocks] + [...]
where the time goes in v3:
time: 168 us
  Pallas kernels  168 us (100%)
    pallas_call x1, Pallas kernels, run_layer(): pl.pallas_call(layer_kernel, out_shape=[shape(b, BF) for b in blocks] + [...  164 us
    pallas_call x1, Pallas kernels, run_layer(): pl.pallas_call(output_kernel, out_shape=[shape(frames.shape, BF)] * 2 + g...  3.63 us

profile of v3, /device:TPU:0, one launch (start us, length us, event | category | flops | bytes accessed | tf_op | source)
XLA Modules:
  0.0 168.2 jit_solution(16837055911614015266)
XLA Ops:
  0.6 163.9 %layer.1 = (bf16[4,64,1536]{2,1,0:T(8,128)(2,1)}, bf16[4,64,512]{2,1,0:T(8,128)(2,1)}, bf16[4,64,1536]{2,1,0:T(8,128)(2,1)}, bf16[4,64,768]{2,1,0:T(8,128)(2,1)}...) custom-call(bf16[8,16,1024]{2,1,0:T(8,128)(2,1)} %frames.1, bf16[8,16,1024]{2,1,0:T(8,128)(2,1)} %cot.1, s32[8]{0:T(128)} %dialogue.1, ...), custom_call_target="tpu_custom_call" | custom-call | flops 10000000000 | bytes 10000000 | tf_op jit(solution)/shard_map/layer/pallas_call | solution.py:753
  164.5 3.6 %outputs.1 = (bf16[8,16,1024]{2,1,0:T(8,128)(2,1)}, bf16[8,16,1024]{2,1,0:T(8,128)(2,1)}, f32[2,64,512]{2,1,0:T(8,128)}, f32[2,64,512]{2,1,0:T(8,128)}, f32[2,64...) custom-call(bf16[4,64,1536]{2,1,0:T(8,128)(2,1)} %get-tuple-element., ...), custom_call_target="tpu_custom_call" | custom-call | flops 1000000 | bytes 10000000 | tf_op jit(solution)/shard_map/outputs/pallas_call | solution.py:766

commit v4 on v3

v4 whole, which is shorter than its diff:
```python
import jax
import jax.numpy as jnp
from jax import lax
from jax.experimental import pallas as pl
from jax.experimental.pallas import tpu as pltpu
from jax.sharding import PartitionSpec as P

HDIM = 64
EPSILON = 1e-05
INNER = 16
ZN = 4
LANES = 128
CUTS = 2
MESH = pl.DeviceIdType.MESH
BF = jnp.bfloat16
F32 = jnp.float32
NN = (((1,), (0,)), ((), ()))
NT = (((1,), (1,)), ((), ()))
TN = (((0,), (0,)), ((), ()))
Q, K, V, O, GT, UP, DN = range(7)
BLOCKS = (2, 2, 2, 2, 4, 4, 4)


def chip_columns(weight_columns):
    return [-(-n // (blocks * LANES)) * LANES for n, blocks in zip(weight_columns, BLOCKS)]


def dot(a, b, dims=NN):
    return lax.dot_general(a, b, dims, preferred_element_type=F32)


def layer_kernel(
    frames_in, cot_in, dialogue_in, padding_in, position_in, gain_one_in, gain_two_in, weights_in,
    grads_out, halves_out, gains_out,
    frames, cot, dialogue, padding, position_set, gain_one, gain_two, weights,
    st, ga, w, dw, rc, sx, rx, fi,
    set_mask, n1, sd, n2, hl, pf,
    sb, sr, so, ru, rd,
    heads_in, heads_grad, att2, probs, gate, up, act2, gate_grad, up_grad,
    cnt, gain_col, gain_face, gain_sum, halves,
    u_one, u_two, hid, hgrad, small,
    in_s, out_s, wt_s, sp_r, ax_r, mc_r, ag_s, ag_r, pr_r, sy_s, sy_r, py_r, sz_s, su_r, sd_r, pu_r,
    gc_s, gc_r, gx_s, gx_r, gf_s, gf_r, c_s, c_r, y_s, y_r, g_s, g_r,
):
    idx = lax.axis_index("dp")
    y = lax.axis_index("tensor")
    inner = lax.rem(idx, INNER)
    base = idx - inner
    z = lax.div(inner, 4)
    x = lax.rem(lax.div(inner, 2), 2)
    c = lax.rem(inner, 2)

    def dev(zz, xx, cc, yy):
        return (base + zz * 4 + xx * 2 + cc, yy)

    def flip(v, bit):
        return 1 - v if bit else v

    def hop(k):
        return lax.rem(z + k, ZN)

    def remote(src, dst, ssem, rsem, device):
        return pltpu.make_async_remote_copy(
            src_ref=src, dst_ref=dst, send_sem=ssem, recv_sem=rsem,
            device_id=device, device_id_type=MESH,
        )

    low = lax.rem(z, 2)
    partner = dev(z, x, c, 1 - y)
    beside = dev(z + 1 - 2 * low, x, c, y)
    sibling = dev(z, x, 1 - c, y)
    across = dev(z, 1 - x, c, y)
    above = dev(hop(1), x, c, y)
    below = dev(hop(ZN - 1), x, c, y)
    column = [dev(hop(k), x, c, y) for k in (1, 2, 3)]
    face = [
        (flip(x, a), flip(c, b), flip(y, d))
        for a in (0, 1) for b in (0, 1) for d in (0, 1) if a or b or d
    ]
    rows, width = n1.shape[1:]
    half = rows // 16
    columns = chip_columns([ref.shape[2] for ref in weights])
    d_rows = weights[0].shape[1]
    own_slot = 2 * z + y
    pair_slot = 2 * low + y
    mine = pl.ds(half * y, half)
    slice_mine = 2 * x + c

    def send(cond, src, dst, ssem, rsem, device):
        copy = remote(src, dst, ssem, rsem, device)
        if cond is None:
            copy.start()
        else:
            pl.when(cond)(copy.start)

    def sent(ref, ssem, cond=None):
        if cond is None:
            remote(ref, ref, ssem, ssem, sibling).wait_send()
        else:
            pl.when(cond)(remote(ref, ref, ssem, ssem, sibling).wait_send)

    def arrived(dst, rsem, cond=None):
        def wait():
            remote(dst, dst, rsem, rsem, sibling).wait_recv()

        if cond is None:
            wait()
        else:
            pl.when(cond)(wait)

    sources = (frames_in.at[mine], cot_in.at[mine], dialogue_in, padding_in, position_in, gain_one_in, gain_two_in)
    targets = (frames, cot, dialogue, padding, position_set, gain_one, gain_two)
    inputs = [
        pltpu.make_async_copy(src, dst, in_s.at[n])
        for n, (src, dst) in enumerate(zip(sources + tuple(weights_in), targets + tuple(weights)))
    ]
    weight_inputs = inputs[len(targets):]
    for n in (0, 4, 5):
        inputs[n].start()
    for copy in weight_inputs[:3]:
        copy.start()

    barrier = pltpu.get_barrier_semaphore()
    for d in column:
        pl.semaphore_signal(barrier, inc=1, device_id=d, device_id_type=MESH)
    for xx, cc, yy in face:
        pl.semaphore_signal(barrier, inc=1, device_id=dev(z, xx, cc, yy), device_id_type=MESH)
    for n in (2, 3, 1, 6):
        inputs[n].start()
    for copy in weight_inputs[3:]:
        copy.start()

    def stage(g):
        n, ref = columns[g], weights[g]
        for b in range(BLOCKS[g]):
            here = min(n, ref.shape[2] - b * n)
            for s in range(2):
                st[g][b, :, s * n:s * n + here] = ref[s, :, b * n:b * n + here]
                if here < n:
                    st[g][b, :, s * n + here:(s + 1) * n] = jnp.zeros((d_rows, n - here), BF)

    for g in (Q, K, V):
        weight_inputs[g].wait()
        stage(g)

    inputs[4].wait()
    row_at = lax.broadcasted_iota(jnp.int32, (16, width), 0)
    row_set = jnp.zeros((16, width), jnp.int32)
    for p in range(16):
        row_set = jnp.where(row_at == p, position_set[p], row_set)
    for s in range(2):
        set_mask[s] = jnp.where(row_set == s, 1.0, 0.0).astype(BF)

    def gain_full(gain):
        m1 = set_mask[1].astype(F32)
        return jnp.where(m1 > 0.5, gain[1:2, :], gain[0:1, :])

    def tile_rows(v):
        return jnp.broadcast_to(v[None], (half, 16, v.shape[1])).reshape(rows, v.shape[1])

    def normalize(values, gain):
        inverse = lax.rsqrt(jnp.sum(values * values, axis=-1, keepdims=True) / width + EPSILON)
        unit = values * inverse
        return unit, inverse, (unit * tile_rows(gain_full(gain))).astype(BF)

    def own_rows(ref):
        return ref[...].reshape(rows, width).astype(F32)

    def zero(ref):
        for n in (1, 2):
            ref[n] = jnp.zeros(ref.shape[1:], ref.dtype)

    inputs[0].wait()
    inputs[5].wait()
    unit, inverse, normed = normalize(own_rows(frames), gain_one)
    u_one[...] = unit
    small[0] = jnp.broadcast_to(inverse, (rows, LANES))
    n1[pair_slot] = normed
    pl.when(z == 0)(lambda: zero(ru))
    pl.when(z == ZN - 1)(lambda: zero(rd))

    inputs[2].wait()
    inputs[3].wait()
    lane = lax.broadcasted_iota(jnp.int32, (8, LANES), 1)
    table = jnp.zeros((8, LANES), F32)
    for f in range(dialogue.shape[0]):
        table = table + jnp.where(lane == dialogue[f], padding[f].astype(F32), 0.0)
    cnt[0, z] = table
    pl.semaphore_wait(barrier, len(column) + len(face))

    def spread(g, k):
        send(None, st[g].at[lax.rem(hop(k), BLOCKS[g])], ga[g].at[z], wt_s.at[g], sp_r.at[g, k - 1],
             dev(hop(k), x, c, y))

    def piece_of(g, k, xx, cc):
        piece = hop(k) * 4 + 2 * xx + cc
        return w[g].at[pl.ds(pl.multiple_of(piece * d_rows, d_rows), d_rows), :]

    def multicast(g, k):
        if k:
            arrived(ga[g].at[hop(k)], sp_r.at[g, 3 - k])
        src = ga[g].at[hop(k)] if k else st[g].at[lax.rem(z, BLOCKS[g])]
        dst = piece_of(g, k, x, c)
        send(None, src, dst, wt_s.at[g], ax_r.at[g, k], across)
        send(None, src, dst, wt_s.at[g], mc_r.at[g], sibling)
        dst[...] = src[...]

    def forward(g, k):
        dst = piece_of(g, k, 1 - x, c)
        arrived(dst, ax_r.at[g, k])
        send(None, dst, dst, wt_s.at[g], mc_r.at[g], sibling)

    def weights_here(g):
        arrived(w[g].at[pl.ds(0, 8 * d_rows), :], mc_r.at[g])

    cut_rows = rows // CUTS

    def cut(q):
        return pl.ds(q * cut_rows, cut_rows)

    def gather_sem(which, slot, q):
        return (pr_r if which in (0, 3) else ag_r).at[which // 2, slot, q]

    def gather_send(which, buf, slot, q, cond, way, device):
        src = buf.at[slot, cut(q)]
        send(cond, src, src, ag_s.at[which, min(way, 1)], gather_sem(which, slot, q), device)

    def gather_start(which, buf):
        for q in range(CUTS):
            gather_send(which, buf, own_slot, q, z < ZN - 1, 1, above)
            gather_send(which, buf, own_slot, q, z > 0, 2, below)
            gather_send(which, buf, own_slot, q, None, 0, partner)

    def gather_step(which, buf, k):
        lo = 2 * jnp.maximum(z - k, 0) + y
        hi = 2 * jnp.minimum(z + k, ZN - 1) + y
        up, down = z >= k, z + k <= ZN - 1
        for q in range(CUTS):
            arrived(buf.at[lo, cut(q)], gather_sem(which, lo, q), cond=up)
            gather_send(which, buf, lo, q, up & (z < ZN - 1), 1, above)
            gather_send(which, buf, lo, q, up, 0, partner)
            arrived(buf.at[hi, cut(q)], gather_sem(which, hi, q), cond=down)
            gather_send(which, buf, hi, q, down & (z > 0), 2, below)
            gather_send(which, buf, hi, q, down, 0, partner)

    def gather_end(which, buf):
        slot = 2 * z + 1 - y
        for q in range(CUTS):
            arrived(buf.at[slot, cut(q)], gather_sem(which, slot, q))
        for k in (1, 2, 3):
            lo = 2 * jnp.maximum(z - k, 0) + 1 - y
            hi = 2 * jnp.minimum(z + k, ZN - 1) + 1 - y
            for q in range(CUTS):
                arrived(buf.at[lo, cut(q)], gather_sem(which, lo, q), cond=z >= k)
                arrived(buf.at[hi, cut(q)], gather_sem(which, hi, q), cond=z + k <= ZN - 1)

    def pair_start(which, buf):
        for q in range(CUTS):
            gather_send(which, buf, pair_slot, q, None, 1, beside)
            gather_send(which, buf, pair_slot, q, None, 0, partner)

    def pair_step(which, buf):
        slot = 2 * (1 - low) + y
        for q in range(CUTS):
            arrived(buf.at[slot, cut(q)], gather_sem(which, slot, q))
            gather_send(which, buf, slot, q, None, 0, partner)

    def pair_end(which, buf):
        slot, far = 2 * low + 1 - y, 2 * (1 - low) + 1 - y
        for q in range(CUTS):
            arrived(buf.at[slot, cut(q)], gather_sem(which, slot, q))
            arrived(buf.at[far, cut(q)], gather_sem(which, far, q))

    def far_first(i):
        orders = ((3, 2, 1, 0), (3, 0, 2, 1), (0, 3, 1, 2), (0, 1, 2, 3))
        b = jnp.int32(0)
        for zz, order in enumerate(orders):
            b = b + jnp.where(z == zz, order[i], 0)
        return b

    def row_sem(n, b, q):
        return (py_r if n in (0, 3) else sy_r).at[n // 2, b, q]

    def scatter_put(n, partial):
        blocks = partial.shape[0] // rows
        pf[n % 2, 0:blocks] = partial.reshape(blocks, rows, width)

    def scatter_send(n, i, b=None):
        b = far_first(i) if b is None else b
        for q in range(CUTS):
            sb[n, b, cut(q), :] = pf[n % 2, 2 * b + 1 - y, cut(q), :].astype(BF)
            send(None, sb.at[n, b, cut(q)], sr.at[n, b, cut(q)], sy_s.at[n], row_sem(n, b, q), partner)

    def chip_sum(n, b, q):
        arrived(sr.at[n, b, cut(q)], row_sem(n, b, q))
        return pf[n % 2, 2 * b + y, cut(q), :] + sr[n, b, cut(q), :].astype(F32)

    plan = (
        (True, 3, z <= 1), (False, 0, z >= 2), (True, 3, z == 2), (False, 0, z == 1),
        (True, 2, z <= 1), (False, 1, z >= 2), (True, 1, z == 0), (False, 2, z == 3),
    )

    def scatter_step(n, at):
        rising, b, cond = plan[at]
        if rising:
            inflow, buf, r, target = z > 0, ru, su_r, above
        else:
            inflow, buf, r, target = z < ZN - 1, rd, sd_r, below
        for q in range(CUTS):

            def step(q=q):
                total = chip_sum(n, b, q)
                arrived(buf.at[n, b, cut(q)], r.at[n - 1, b, q], cond=inflow)
                so[n, b, cut(q), :] = (total + buf[n, b, cut(q), :].astype(F32)).astype(BF)

            pl.when(cond)(step)
            send(cond, so.at[n, b, cut(q)], buf.at[n, b, cut(q)], sz_s.at[n], r.at[n - 1, b, q], target)

    def scatter_end(n):
        totals = []
        for q in range(CUTS):
            total = chip_sum(n, z, q)
            arrived(ru.at[n, z, cut(q)], su_r.at[n - 1, z, q], cond=z > 0)
            arrived(rd.at[n, z, cut(q)], sd_r.at[n - 1, z, q], cond=z < ZN - 1)
            totals.append(total + ru[n, z, cut(q), :].astype(F32) + rd[n, z, cut(q), :].astype(F32))
        return jnp.concatenate(totals, axis=0)

    def pair_scatter_send(n):
        scatter_send(n, 2, 1 - low)
        scatter_send(n, 3, low)

    def pair_scatter_step(n):
        b = 1 - low
        for q in range(CUTS):
            so[n, b, cut(q), :] = chip_sum(n, b, q).astype(BF)
            send(None, so.at[n, b, cut(q)], ru.at[n, b, cut(q)], sz_s.at[n], pu_r.at[n // 2, q], beside)

    def pair_scatter_end(n):
        totals = []
        for q in range(CUTS):
            total = chip_sum(n, low, q)
            arrived(ru.at[n, low, cut(q)], pu_r.at[n // 2, q])
            totals.append(total + ru[n, low, cut(q), :].astype(F32))
        return jnp.concatenate(totals, axis=0)

    def both_sets(v):
        count, n = v.shape
        three = v.reshape(count // 16, 16, n)
        return jnp.concatenate([(three * set_mask[s, :, 0:n][None]).reshape(count, n) for s in range(2)], axis=1)

    def choose(v):
        count, n = v.shape[0], v.shape[1] // 2
        m = jnp.broadcast_to(set_mask[1, :, 0:n].astype(F32)[None], (count // 16, 16, n)).reshape(count, n)
        return jnp.where(m > 0.5, v[:, n:], v[:, 0:n])

    def flat(buf):
        return buf[...].reshape(buf.shape[0] * rows, width)

    def weight_grad(g, values, grads):
        dw[g][...] = dot(values, grads, TN).astype(BF).reshape(dw[g].shape)
        for xx in (1 - x, x):
            send(None, dw[g].at[:, 2 * xx + 1 - c], rc[g].at[xx], gc_s.at[g], gc_r.at[g, xx], sibling)

    def reduce_across(g):
        arrived(rc[g].at[1 - x], gc_r.at[g, 1 - x])
        for k in (2, 1, 3, 0):
            zz = hop(k)
            sx[g][zz] = (dw[g][zz, 2 * (1 - x) + c].astype(F32) + rc[g][1 - x, zz].astype(F32)).astype(BF)
            send(None, sx[g].at[zz], rx[g].at[zz], gx_s.at[g], gx_r.at[g, zz], across)

    def reduce_column(g, k):
        zz = hop(k)
        if k == 2:
            arrived(rc[g].at[x], gc_r.at[g, x])
        arrived(rx[g].at[zz], gx_r.at[g, zz])
        total = dw[g][zz, 2 * x + c].astype(F32) + rc[g][x, zz].astype(F32) + rx[g][zz].astype(F32)
        if k:
            rx[g][zz] = total.astype(BF)
            send(None, rx[g].at[zz], fi[g].at[z], gf_s.at[g], gf_r.at[g], dev(zz, x, c, y))
        else:
            fi[g][z] = total.astype(BF)

    def reduce_end(g):
        arrived(fi[g].at[pl.ds(0, 3)], gf_r.at[g])
        outputs[g].start()

    outputs = [
        pltpu.make_async_copy(src, dst, out_s.at[n])
        for n, (src, dst) in enumerate(zip(tuple(fi) + (halves, gain_sum), tuple(grads_out) + (halves_out, gains_out)))
    ]

    def counts_start():
        for k in (1, 2, 3):
            send(None, cnt.at[0, z], cnt.at[0, z], c_s.at[0], c_r.at[0], dev(hop(k), x, c, y))

    def counts_step():
        arrived(cnt.at[0, pl.ds(0, 3)], c_r.at[0])
        cnt[1, slice_mine] = cnt[0, 0] + cnt[0, 1] + cnt[0, 2] + cnt[0, 3]
        for a, b in ((0, 1), (1, 0), (1, 1)):
            send(None, cnt.at[1, slice_mine], cnt.at[1, slice_mine], c_s.at[1], c_r.at[1],
                 dev(z, flip(x, a), flip(c, b), y))

    def seed_rows():
        frame_weight = small[1, mine, :]
        weight_rows = jnp.broadcast_to(frame_weight[:, None, 0:1], (half, 16, width)).reshape(rows, width)
        return own_rows(cot) * weight_rows

    def seed_here():
        arrived(cnt.at[1, pl.ds(0, 3)], c_r.at[1])
        inputs[1].wait()
        counts = cnt[1, 0] + cnt[1, 1] + cnt[1, 2] + cnt[1, 3]
        for f in range(dialogue.shape[0]):
            found = jnp.sum(jnp.where(lane == dialogue[f], counts, 0.0), axis=1, keepdims=True)
            loss = padding[f].astype(F32) * (dialogue.shape[0] * 1.0) / (found + 1.0)
            small[1, f:f + 1, :] = jnp.broadcast_to(loss[0:1, :], (1, LANES))
        sd[own_slot] = seed_rows().astype(BF)

    def stage_rest():
        for g in (O, GT, UP, DN):
            weight_inputs[g].wait()
            stage(g)

    bl = LANES
    r_at = lax.broadcasted_iota(jnp.int32, (bl, bl), 0)
    c_at = lax.broadcasted_iota(jnp.int32, (bl, bl), 1)
    seen = (c_at <= r_at) & (lax.div(r_at, 16) == lax.div(c_at, 16))
    qb = heads_in[0].shape[1]
    heads = qb // HDIM
    head_of = lax.div(lax.broadcasted_iota(jnp.int32, (bl, qb), 1), HDIM)
    scale = HDIM ** (-0.5)

    def only(v, h):
        return jnp.where(head_of == h, v, jnp.zeros_like(v))

    def project_heads(g):
        heads_in[g][...] = choose(dot(flat(n1), w[g][...])).astype(BF)

    def attend():
        attended = []
        for t in range(att2.shape[0] // bl):
            at = pl.ds(t * bl, bl)
            q, kk, v = heads_in[Q][at, :], heads_in[K][at, :], heads_in[V][at, :]
            out = jnp.zeros((bl, qb), F32)
            for h in range(heads):
                scores = dot(only(q, h), kk, NT) * scale
                scores = jnp.where(seen, scores, -1e30)
                e = jnp.exp(scores - jnp.max(scores, axis=-1, keepdims=True))
                e = jnp.where(seen, e, 0.0)
                p = e / jnp.sum(e, axis=-1, keepdims=True)
                probs[t, h] = p
                out = jnp.where(head_of == h, dot(p.astype(BF), v), out)
            attended.append(out.astype(BF))
        att2[...] = both_sets(jnp.concatenate(attended, axis=0))

    def attend_back():
        datt = choose(dot(flat(hl), w[O][...])).astype(BF)
        gq, gk, gv = [], [], []
        for t in range(att2.shape[0] // bl):
            at = pl.ds(t * bl, bl)
            q, kk, v = heads_in[Q][at, :], heads_in[K][at, :], heads_in[V][at, :]
            da = datt[t * bl:(t + 1) * bl, :]
            tq = jnp.zeros((bl, qb), F32)
            tk, tv = tq, tq
            for h in range(heads):
                p = probs[t, h]
                dp = dot(only(da, h), v, NT)
                tv = jnp.where(head_of == h, dot(p.astype(BF), da, TN), tv)
                ds = (p * (dp - jnp.sum(dp * p, axis=-1, keepdims=True))).astype(BF)
                tq = jnp.where(head_of == h, dot(ds, kk) * scale, tq)
                tk = jnp.where(head_of == h, dot(ds, q, TN) * scale, tk)
            gq.append(tq.astype(BF))
            gk.append(tk.astype(BF))
            gv.append(tv.astype(BF))
        for g, parts in ((Q, gq), (K, gk), (V, gv)):
            heads_grad[g][...] = both_sets(jnp.concatenate(parts, axis=0))

    def heads_back():
        return sum(dot(heads_grad[g][...], w[g][...], NT) for g in (Q, K, V))

    def gate_rows():
        gate[...] = choose(dot(flat(n2), w[GT][...]))

    def up_rows():
        up[...] = choose(dot(flat(n2), w[UP][...]))

    def active_rows():
        v = gate[...]
        act2[...] = both_sets((v * jax.nn.sigmoid(v) * up[...]).astype(BF))

    def active_back():
        active_grad = choose(dot(flat(sd), w[DN][...]))
        v = gate[...]
        sig = jax.nn.sigmoid(v)
        gate_grad[...] = both_sets((active_grad * up[...] * sig * (1.0 + v * (1.0 - sig))).astype(BF))
        up_grad[...] = both_sets((active_grad * (v * sig)).astype(BF))

    def feed_back():
        return dot(gate_grad[...], w[GT][...], NT) + dot(up_grad[...], w[UP][...], NT)

    def feed_out():
        return dot(act2[...], w[DN][...], NT)

    def set_sums(v, at):
        three = v.reshape(half, 16, width)
        for s in range(2):
            part = (three * set_mask[s].astype(F32)[None]).reshape(rows, width)
            gain_col[z, at + s:at + s + 1, :] = jnp.sum(part, axis=0, keepdims=True)

    def norm_back(gradient, gain, unit, inverse):
        scaled = gradient * tile_rows(gain_full(gain))
        return inverse * (scaled - unit * (jnp.sum(scaled * unit, axis=-1, keepdims=True) / width))

    def second_norm(attention):
        inputs[6].wait()
        hidden = own_rows(frames) + attention
        hid[...] = hidden
        unit, inverse, normed = normalize(hidden, gain_two)
        u_two[...] = unit
        small[2] = jnp.broadcast_to(inverse, (rows, LANES))
        n2[own_slot] = normed

    def second_norm_back(normed_two_grad):
        unit = u_two[...]
        hidden_grad = seed_rows() + norm_back(normed_two_grad, gain_two, unit, small[2][:, 0:1])
        hgrad[...] = hidden_grad
        hl[pair_slot] = hidden_grad.astype(BF)
        gain_col[z] = jnp.zeros((8, width), F32)
        set_sums(normed_two_grad * unit, 2)

    def first_norm_back(normed_one_grad):
        unit = u_one[...]
        set_sums(normed_one_grad * unit, 0)
        result = hgrad[...] + norm_back(normed_one_grad, gain_one, unit, small[0][:, 0:1])
        halves[1, mine] = result.astype(BF).reshape(half, 16, width)

    def output_rows(branch):
        halves[0, mine] = (hid[...] + branch).astype(BF).reshape(half, 16, width)

    def half_send(j):
        send(None, halves.at[j, mine], halves.at[j, mine], y_s.at[j], y_r.at[j], partner)

    def half_end(j):
        theirs = pl.ds(half * (1 - y), half)
        arrived(halves.at[j, theirs], y_r.at[j])

    place = 4 * x + 2 * c + y

    def gains_start():
        for k in (1, 2, 3):
            send(None, gain_col.at[z], gain_col.at[z], g_s.at[0], g_r.at[0], dev(hop(k), x, c, y))

    def gains_step():
        arrived(gain_col.at[pl.ds(0, 3)], g_r.at[0])
        gain_face[place] = gain_col[0] + gain_col[1] + gain_col[2] + gain_col[3]
        for xx, cc, yy in face:
            send(None, gain_face.at[place], gain_face.at[place], g_s.at[1], g_r.at[1], dev(z, xx, cc, yy))

    def gains_end():
        arrived(gain_face.at[pl.ds(0, 7)], g_r.at[1])
        total = gain_face[0]
        for j in range(1, 8):
            total = total + gain_face[j]
        gain_sum[...] = total
        outputs[8].start()

    counts_start()
    spread(K, 2)
    stage_rest()
    spread(V, 1)
    spread(V, 3)
    multicast(GT, 0)
    spread(O, 2)
    spread(O, 1)
    multicast(V, 0)
    multicast(O, 0)
    spread(Q, 3)
    spread(Q, 1)
    spread(K, 1)
    spread(K, 3)
    pair_start(0, n1)
    multicast(Q, 0)
    multicast(K, 2)
    counts_step()
    multicast(DN, 0)
    multicast(V, 1)
    spread(O, 3)
    spread(GT, 1)
    multicast(K, 0)
    multicast(K, 3)
    spread(V, 2)
    multicast(O, 3)
    multicast(K, 1)
    multicast(O, 1)
    spread(GT, 3)
    pair_step(0, n1)
    spread(Q, 2)
    spread(UP, 3)
    multicast(GT, 3)
    multicast(Q, 3)
    forward(O, 3)
    multicast(V, 3)
    spread(UP, 1)
    forward(GT, 0)
    multicast(O, 2)
    forward(K, 2)
    multicast(V, 2)
    forward(V, 0)
    forward(K, 0)
    seed_here()
    multicast(Q, 1)
    forward(O, 1)
    gather_start(1, sd)
    forward(O, 2)
    forward(K, 3)
    multicast(Q, 2)
    spread(UP, 2)
    forward(Q, 3)
    pair_end(0, n1)
    multicast(UP, 0)
    forward(V, 3)
    forward(K, 1)
    forward(O, 0)
    multicast(UP, 3)
    forward(DN, 0)
    forward(Q, 0)
    weights_here(K)
    forward(V, 2)
    forward(V, 1)
    spread(DN, 1)
    forward(Q, 1)
    forward(Q, 2)
    spread(DN, 3)
    multicast(GT, 1)
    project_heads(K)
    weights_here(O)
    weights_here(Q)
    forward(GT, 3)
    spread(DN, 2)
    weights_here(V)
    project_heads(V)
    project_heads(Q)
    attend()
    scatter_put(0, dot(att2[...], w[O][...], NT))
    pair_scatter_send(0)
    multicast(UP, 1)
    pair_scatter_step(0)
    gather_step(1, sd, 1)
    attention = pair_scatter_end(0)
    second_norm(attention)
    forward(UP, 0)
    multicast(DN, 1)
    forward(UP, 1)
    gather_start(2, n2)
    forward(UP, 3)
    multicast(UP, 2)
    gather_step(2, n2, 1)
    multicast(DN, 3)
    forward(DN, 1)
    spread(GT, 2)
    gather_step(2, n2, 2)
    multicast(DN, 2)
    gather_step(2, n2, 3)
    forward(DN, 3)
    gather_step(1, sd, 2)
    forward(UP, 2)
    forward(DN, 2)
    multicast(GT, 2)
    weights_here(UP)
    weights_here(DN)
    gather_end(2, n2)
    up_rows()
    forward(GT, 1)
    gather_step(1, sd, 3)
    forward(GT, 2)
    weights_here(GT)
    gate_rows()
    active_rows()
    scatter_put(2, feed_out())
    scatter_send(2, 0)
    gather_end(1, sd)
    active_back()
    scatter_put(1, feed_back())
    scatter_send(1, 0)
    scatter_send(1, 1)
    scatter_step(2, 0)
    weight_grad(GT, flat(n2), gate_grad[...])
    scatter_send(1, 2)
    scatter_step(1, 0)
    scatter_step(2, 1)
    reduce_across(GT)
    scatter_step(1, 1)
    scatter_send(2, 1)
    weight_grad(DN, flat(sd), act2[...])
    scatter_send(1, 3)
    scatter_step(1, 4)
    reduce_column(GT, 2)
    scatter_send(2, 2)
    scatter_step(1, 2)
    scatter_step(1, 5)
    scatter_send(2, 3)
    reduce_across(DN)
    weight_grad(UP, flat(n2), up_grad[...])
    scatter_step(1, 3)
    scatter_step(1, 7)
    scatter_step(1, 6)
    scatter_step(2, 4)
    reduce_column(DN, 2)
    normed_two_grad = scatter_end(1)
    scatter_step(2, 5)
    second_norm_back(normed_two_grad)
    pair_start(3, hl)
    reduce_column(GT, 1)
    reduce_across(UP)
    reduce_column(GT, 3)
    reduce_column(DN, 1)
    scatter_step(2, 6)
    pair_step(3, hl)
    reduce_column(UP, 2)
    pair_end(3, hl)
    scatter_step(2, 3)
    reduce_column(UP, 1)
    weight_grad(O, flat(hl), att2[...])
    attend_back()
    weight_grad(V, flat(n1), heads_grad[V][...])
    reduce_column(UP, 3)
    scatter_put(3, heads_back())
    reduce_across(V)
    scatter_step(2, 2)
    reduce_column(DN, 3)
    pair_scatter_send(3)
    weight_grad(Q, flat(n1), heads_grad[Q][...])
    weight_grad(K, flat(n1), heads_grad[K][...])
    reduce_column(V, 2)
    reduce_column(DN, 0)
    reduce_across(K)
    reduce_across(Q)
    pair_scatter_step(3)
    reduce_column(V, 1)
    reduce_column(K, 2)
    reduce_column(K, 1)
    scatter_step(2, 7)
    reduce_column(V, 3)
    reduce_column(Q, 2)
    reduce_column(GT, 0)
    reduce_across(O)
    normed_one_grad = pair_scatter_end(3)
    first_norm_back(normed_one_grad)
    gains_start()
    reduce_column(UP, 0)
    reduce_end(UP)
    reduce_column(K, 3)
    reduce_column(V, 0)
    reduce_end(V)
    reduce_column(O, 2)
    half_send(1)
    reduce_column(Q, 1)
    output_rows(scatter_end(2))
    reduce_column(Q, 3)
    reduce_column(K, 0)
    reduce_end(K)
    half_send(0)
    reduce_column(O, 1)
    gains_step()
    reduce_column(O, 3)
    reduce_end(GT)
    half_end(1)
    half_end(0)
    reduce_end(DN)
    reduce_column(Q, 0)
    reduce_end(Q)
    gains_end()
    reduce_column(O, 0)
    reduce_end(O)
    outputs[7].start()
    for g in range(len(weights)):
        sent(w[g].at[pl.ds(0, 15 * d_rows), :], wt_s.at[g])
        sent(dw[g].at[:, pl.ds(0, 2)], gc_s.at[g])
        sent(sx[g], gx_s.at[g])
        sent(rx[g].at[pl.ds(0, 3)], gf_s.at[g])
    for which, buf in ((1, sd), (2, n2)):
        sent(buf.at[pl.ds(0, 4)], ag_s.at[which, 0])
        sent(buf.at[pl.ds(0, 1)], ag_s.at[which, 1], cond=(z == 0) | (z == ZN - 1))
        sent(buf.at[pl.ds(0, 5)], ag_s.at[which, 1], cond=(z > 0) & (z < ZN - 1))
        sent(sb.at[which], sy_s.at[which])
        sent(so.at[which, pl.ds(0, 3)], sz_s.at[which])
    for which, buf in ((0, n1), (3, hl)):
        sent(buf.at[pl.ds(0, 2)], ag_s.at[which, 0])
        sent(buf.at[pl.ds(0, 1)], ag_s.at[which, 1])
        sent(sb.at[which, pl.ds(0, 2)], sy_s.at[which])
        sent(so.at[which, pl.ds(0, 1)], sz_s.at[which])
    for j in (0, 1):
        sent(cnt.at[j, pl.ds(0, 3)], c_s.at[j])
        sent(halves.at[j, mine], y_s.at[j])
    sent(gain_col.at[pl.ds(0, 3)], g_s.at[0])
    sent(gain_face.at[pl.ds(0, 7)], g_s.at[1])
    for copy in outputs:
        copy.wait()


def output_kernel(
    fi, halves, gains,
    mixed, frames_grad, dq, dk, dv, do, dg, du, dd, first_gain, second_gain,
):
    inner = lax.rem(lax.axis_index("dp"), INNER)
    mixed[...] = halves[0]
    frames_grad[...] = halves[1]
    outs = (dq, dk, dv, do, dg, du, dd)
    for g, n in enumerate(chip_columns([ref.shape[2] for ref in outs])):
        for b in range(BLOCKS[g]):
            here = min(n, outs[g].shape[2] - b * n)
            for s in range(2):
                lanes = slice(s * n, s * n + here)
                parts = [fi[g][other, :, lanes].astype(F32) for other in range(b, ZN, BLOCKS[g])]
                outs[g][s, :, b * n:b * n + here] = sum(parts)
    width = gains.shape[1]
    share = first_gain.shape[1]
    turned = pltpu.roll(gains[...], lax.rem(width - inner * share, width), 1)
    first_gain[...] = turned[0:2, 0:share]
    second_gain[...] = turned[2:4, 0:share]


def run_layer(frames, cot, dialogue, padding, position_set, gain_one, gain_two, weights):
    width = frames.shape[2]
    rows = frames.shape[0] * frames.shape[1] // 2
    d_rows = weights[0].shape[1]
    sizes = chip_columns([v.shape[2] for v in weights])
    count = len(sizes)
    group, pair_group = 8 * rows, 4 * rows
    dma = pltpu.SemaphoreType.DMA
    vm = pltpu.VMEM
    shape = jax.ShapeDtypeStruct
    block_rows, pair_rows = (8, rows, width), (4, rows, width)
    four = (4, 4, rows, width)
    own = [(ZN, d_rows, 2 * n) for n in sizes]
    qb, fb = sizes[Q], sizes[GT]
    own_frames = (frames.shape[0] // 2,) + frames.shape[1:]
    scratch = (
        [vm(own_frames, BF)] * 2
        + [pltpu.SMEM(v.shape, v.dtype) for v in (dialogue, padding, position_set)]
        + [vm(gain_one.shape, F32)] * 2
        + [[vm(v.shape, BF) for v in weights]]
        + [[vm((blocks, d_rows, 2 * n), BF) for blocks, n in zip(BLOCKS, sizes)]]
        + [[vm(v, BF) for v in own]]
        + [[vm((width, 2 * n), BF) for n in sizes]]
        + [[vm((ZN, 4, d_rows, 2 * n), BF) for n in sizes]]
        + [[vm((2, ZN, d_rows, 2 * n), BF) for n in sizes]]
        + [[vm(v, BF) for v in own]] * 3
        + [vm((2, 16, width), BF)]
        + [vm(pair_rows, BF), vm(block_rows, BF), vm(block_rows, BF), vm(pair_rows, BF)] + [vm((2,) + block_rows, F32)]
        + [vm(four, BF)] * 5
        + [[vm((pair_group, qb), BF)] * 3, [vm((pair_group, 2 * qb), BF)] * 3, vm((pair_group, 2 * qb), BF)]
        + [vm((pair_group // LANES, qb // HDIM, LANES, LANES), F32)]
        + [vm((group, fb), F32)] * 2
        + [vm((group, 2 * fb), BF)] * 3
        + [vm((2, 4, 8, LANES), F32), vm((ZN, 8, width), F32), vm((8, 8, width), F32), vm((8, width), F32)]
        + [vm((2,) + frames.shape, BF)]
        + [vm((rows, width), F32)] * 4 + [vm((3, rows, LANES), F32)]
        + [dma((7 + count,)), dma((2 + count,))]
        + [dma((count,)), dma((count, 3)), dma((count, 4)), dma((count,))]
        + [dma((4, 2)), dma((2, 8, CUTS)), dma((2, 4, CUTS))]
        + [dma((4,)), dma((2, 4, CUTS)), dma((2, 2, CUTS)), dma((4,)), dma((2, 4, CUTS)), dma((2, 4, CUTS)), dma((2, CUTS))]
        + [dma((count,)), dma((count, 2)), dma((count,)), dma((count, 4)), dma((count,)), dma((count,))]
        + [dma((2,))] * 6
    )
    any_place = pl.BlockSpec(memory_space=pl.ANY)
    spec = pl.BlockSpec(memory_space=pltpu.VMEM)
    packed = pl.pallas_call(
        layer_kernel,
        out_shape=[[shape(v, BF) for v in own], shape((2,) + frames.shape, BF), shape((8, width), F32)],
        in_specs=[any_place] * 7 + [[any_place] * count],
        out_specs=[[any_place] * count, any_place, any_place],
        scratch_shapes=scratch,
        compiler_params=pltpu.CompilerParams(
            collective_id=0, has_side_effects=True, vmem_limit_bytes=63 * 2**20
        ),
        cost_estimate=pl.CostEstimate(flops=10**10, bytes_accessed=10**7, transcendentals=0),
        name="layer",
    )(frames, cot, dialogue, padding, position_set, gain_one, gain_two, list(weights))
    grads = [shape(v.shape, F32) for v in weights]
    return pl.pallas_call(
        output_kernel,
        out_shape=[shape(frames.shape, BF)] * 2 + grads + [shape((2, d_rows), F32)] * 2,
        in_specs=[[spec] * count, spec, spec],
        out_specs=[spec] * 11,
        compiler_params=pltpu.CompilerParams(vmem_limit_bytes=63 * 2**20),
        cost_estimate=pl.CostEstimate(flops=10**6, bytes_accessed=10**7, transcendentals=0),
        name="outputs",
    )(*packed)


def per_device(
    frames, cotangent, dialogue, padding, position_set,
    query_weight, key_weight, value_weight, output_weight, gate_weight, up_weight, down_weight,
    attention_gain, feedforward_gain,
):
    dp = lax.axis_size("dp")
    outer = dp // INNER
    groups = [[o * INNER + i for o in range(outer)] for i in range(INNER)]
    width = frames.shape[-1]
    turn = (False, False, False, True, False, False, True)
    weights = [query_weight, key_weight, value_weight, output_weight, gate_weight, up_weight, down_weight]
    weights = [jnp.swapaxes(v, 1, 2) if t else v for v, t in zip(weights, turn)]

    def to_kernel(v):
        if outer == 1:
            return v
        cut = v.reshape(v.shape[:-1] + (outer, INNER, width // dp))
        return jnp.swapaxes(cut, -3, -2).reshape(v.shape)

    def from_kernel(v):
        if outer == 1:
            return v
        cut = v.reshape(v.shape[:-1] + (INNER, outer, width // dp))
        return jnp.swapaxes(cut, -3, -2).reshape(v.shape)

    if outer > 1:
        weights = [lax.all_gather(v, "dp", axis=1, tiled=True, axis_index_groups=groups) for v in weights]
    mixed, frames_grad, *rest = run_layer(
        to_kernel(frames), to_kernel(cotangent), dialogue, padding, position_set,
        to_kernel(attention_gain), to_kernel(feedforward_gain), weights,
    )
    grads, gains = rest[:7], rest[7:]
    if outer > 1:
        grads = [
            lax.psum_scatter(v, "dp", scatter_dimension=1, tiled=True, axis_index_groups=groups) for v in grads
        ]
        gains = [
            lax.psum_scatter(v, "dp", scatter_dimension=1, tiled=True, axis_index_groups=groups) for v in gains
        ]
    grads = [jnp.swapaxes(v, 1, 2) if t else v for v, t in zip(grads, turn)]
    return (from_kernel(mixed), from_kernel(frames_grad), *grads, *gains)


def solution(mesh):
    column = P(None, "dp", "tensor")
    row = P(None, "tensor", "dp")
    rows = P("dp", None, None)
    in_specs = (
        rows, rows, P("dp"), P("dp"), P(),
        column, column, column, row, column, column, row, P(), P(),
    )
    out_specs = (
        rows, rows, column, column, column, row, column, column, row, P(None, "dp"), P(None, "dp"),
    )
    return jax.shard_map(per_device, mesh=mesh, in_specs=in_specs, out_specs=out_specs, check_vma=False)
```

time: 168 us -> 161 us (0.958)
  Pallas kernels: 168 us -> 160 us
    pallas_call x1, Pallas kernels: 164 us -> 157 us  [run_layer(): pl.pallas_call(layer_kernel, out_shape=[[shape(v, BF) for v in own], shap...]
where the time goes in v4:
time: 161 us
  Pallas kernels  160 us (99%)
    pallas_call x1, Pallas kernels, run_layer(): pl.pallas_call(layer_kernel, out_shape=[[shape(v, BF) for v in own], shap...  157 us
    pallas_call x1, Pallas kernels, run_layer(): pl.pallas_call(output_kernel, out_shape=[shape(frames.shape, BF)] * 2 + g...  3.6 us

profile of v4, /device:TPU:0, one launch (start us, length us, event | category | flops | bytes accessed | tf_op | source)
XLA Modules:
  0.0 161.1 jit_solution(8870582190015342511)
XLA Ops:
  0.6 156.9 %layer.1 = (bf16[4,64,512]{2,1,0:T(8,128)(2,1)}, bf16[4,64,512]{2,1,0:T(8,128)(2,1)}, bf16[4,64,512]{2,1,0:T(8,128)(2,1)}, bf16[4,64,512]{2,1,0:T(8,128)(2,1)}, ...) custom-call(bf16[8,16,1024]{2,1,0:T(8,128)(2,1)} %frames_in.1, ...), custom_call_target="tpu_custom_call" | custom-call | flops 10000000000 | bytes 10000000 | tf_op jit(solution)/shard_map/layer/pallas_call | solution.py:867
  157.5 3.6 %outputs.1 = (bf16[8,16,1024]{2,1,0:T(8,128)(2,1)}, bf16[8,16,1024]{2,1,0:T(8,128)(2,1)}, f32[2,64,512]{2,1,0:T(8,128)}, f32[2,64,512]{2,1,0:T(8,128)}, f32[2,64...) custom-call(bf16[4,64,512]{2,1,0:T(8,128)(2,1)} %get-tuple-element.3, ...), custom_call_target="tpu_custom_call" | custom-call | flops 1000000 | bytes 10000000 | tf_op jit(solution)/shard_map/outputs/pallas_call | solution.py:880

commit v5 on v4

--- a/solution.py
+++ b/solution.py
@@ -17,12 +17,28 @@
 NN = (((1,), (0,)), ((), ()))
 NT = (((1,), (1,)), ((), ()))
 TN = (((0,), (0,)), ((), ()))
-Q, K, V, O, GT, UP, DN = range(7)
-BLOCKS = (2, 2, 2, 2, 4, 4, 4)
-
-
-def chip_columns(weight_columns):
-    return [-(-n // (blocks * LANES)) * LANES for n, blocks in zip(weight_columns, BLOCKS)]
+Q, K, V, O, GA, UA, DA, B1, B2 = range(9)
+FEED = (4, 5, 6)
+ATTENTION_BLOCKS, TAIL = 2, 64
+
+
+def feed_columns(units):
+    part = units // (ZN * LANES) * LANES
+    assert units == ZN * part + ZN * TAIL + ZN // 2 * TAIL
+    return part, ZN * part, ZN * (part + TAIL)
+
+
+def group_lanes(attention_columns, units):
+    chip = attention_columns // ATTENTION_BLOCKS
+    return [2 * chip] * 4 + [2 * feed_columns(units)[0]] * 3 + [2 * TAIL * len(FEED)] * 2
+
+
+def swap_halves(v):
+    return pltpu.roll(v.astype(F32), TAIL, 1).astype(v.dtype)
+
+
+def lower_lanes(v):
+    return lax.broadcasted_iota(jnp.int32, v.shape, 1) < TAIL
 
 
 def dot(a, b, dims=NN):
@@ -36,7 +52,7 @@
     st, ga, w, dw, rc, sx, rx, fi,
     set_mask, n1, sd, n2, hl, pf,
     sb, sr, so, ru, rd,
-    heads_in, heads_grad, att2, probs, gate, up, act2, gate_grad, up_grad,
+    heads_in, heads_grad, att2, probs, gate, up, active_grad, act2, gate_grad, up_grad, tail_gate_up, tail_act,
     cnt, gain_col, gain_face, gain_sum, halves,
     u_one, u_two, hid, hgrad, small,
     in_s, out_s, wt_s, sp_r, ax_r, mc_r, ag_s, ag_r, pr_r, sy_s, sy_r, py_r, sz_s, su_r, sd_r, pu_r,
@@ -79,7 +95,9 @@
     ]
     rows, width = n1.shape[1:]
     half = rows // 16
-    columns = chip_columns([ref.shape[2] for ref in weights])
+    units = weights[FEED[0]].shape[2]
+    part, first_b1, first_b2 = feed_columns(units)
+    even = low == 0
     d_rows = weights[0].shape[1]
     own_slot = 2 * z + y
     pair_slot = 2 * low + y
@@ -130,14 +148,25 @@
     for copy in weight_inputs[3:]:
         copy.start()
 
+    def blocks_of(g):
+        return ATTENTION_BLOCKS if g <= O else ZN
+
     def stage(g):
-        n, ref = columns[g], weights[g]
-        for b in range(BLOCKS[g]):
-            here = min(n, ref.shape[2] - b * n)
+        n = st[g].shape[2] // 2
+        for b in range(blocks_of(g)):
             for s in range(2):
-                st[g][b, :, s * n:s * n + here] = ref[s, :, b * n:b * n + here]
-                if here < n:
-                    st[g][b, :, s * n + here:(s + 1) * n] = jnp.zeros((d_rows, n - here), BF)
+                st[g][b, :, s * n:(s + 1) * n] = weights[g][s, :, b * n:(b + 1) * n]
+
+    def stage_tail(g, first, b):
+        at = first + (b // 2 if g == B2 else b) * TAIL
+        tile = at // LANES * LANES
+        for m, weight in enumerate(FEED):
+            both = [weights[weight][s, :, tile:tile + LANES] for s in range(2)]
+            if at == tile:
+                here = jnp.where(lower_lanes(both[0]), both[0], swap_halves(both[1]))
+            else:
+                here = jnp.where(lower_lanes(both[0]), swap_halves(both[0]), both[1])
+            st[g][b, :, m * LANES:(m + 1) * LANES] = here
 
     for g in (Q, K, V):
         weight_inputs[g].wait()
@@ -188,30 +217,47 @@
     cnt[0, z] = table
     pl.semaphore_wait(barrier, len(column) + len(face))
 
+    def used(g, k=0):
+        if g != B2:
+            return None
+        return even if k % 2 == 0 else jnp.logical_not(even)
+
     def spread(g, k):
-        send(None, st[g].at[lax.rem(hop(k), BLOCKS[g])], ga[g].at[z], wt_s.at[g], sp_r.at[g, k - 1],
+        send(used(g, k), st[g].at[lax.rem(hop(k), blocks_of(g))], ga[g].at[z], wt_s.at[g], sp_r.at[g, k - 1],
              dev(hop(k), x, c, y))
 
     def piece_of(g, k, xx, cc):
         piece = hop(k) * 4 + 2 * xx + cc
         return w[g].at[pl.ds(pl.multiple_of(piece * d_rows, d_rows), d_rows), :]
 
+    def where_used(g, action):
+        if used(g) is None:
+            action()
+        else:
+            pl.when(used(g))(action)
+
     def multicast(g, k):
-        if k:
-            arrived(ga[g].at[hop(k)], sp_r.at[g, 3 - k])
-        src = ga[g].at[hop(k)] if k else st[g].at[lax.rem(z, BLOCKS[g])]
-        dst = piece_of(g, k, x, c)
-        send(None, src, dst, wt_s.at[g], ax_r.at[g, k], across)
-        send(None, src, dst, wt_s.at[g], mc_r.at[g], sibling)
-        dst[...] = src[...]
+        def action():
+            if k:
+                arrived(ga[g].at[hop(k)], sp_r.at[g, 3 - k])
+            src = ga[g].at[hop(k)] if k else st[g].at[lax.rem(z, blocks_of(g))]
+            dst = piece_of(g, k, x, c)
+            send(None, src, dst, wt_s.at[g], ax_r.at[g, k], across)
+            send(None, src, dst, wt_s.at[g], mc_r.at[g], sibling)
+            dst[...] = src[...]
+
+        where_used(g, action)
 
     def forward(g, k):
-        dst = piece_of(g, k, 1 - x, c)
-        arrived(dst, ax_r.at[g, k])
-        send(None, dst, dst, wt_s.at[g], mc_r.at[g], sibling)
+        def action():
+            dst = piece_of(g, k, 1 - x, c)
+            arrived(dst, ax_r.at[g, k])
+            send(None, dst, dst, wt_s.at[g], mc_r.at[g], sibling)
+
+        where_used(g, action)
 
     def weights_here(g):
-        arrived(w[g].at[pl.ds(0, 8 * d_rows), :], mc_r.at[g])
+        arrived(w[g].at[pl.ds(0, 8 * d_rows), :], mc_r.at[g], cond=used(g))
 
     cut_rows = rows // CUTS
 
@@ -285,6 +331,10 @@
         blocks = partial.shape[0] // rows
         pf[n % 2, 0:blocks] = partial.reshape(blocks, rows, width)
 
+    def scatter_add(n, partial):
+        blocks = partial.shape[0] // rows
+        pf[n % 2, 0:blocks] += partial.reshape(blocks, rows, width)
+
     def scatter_send(n, i, b=None):
         b = far_first(i) if b is None else b
         for q in range(CUTS):
@@ -358,30 +408,50 @@
 
     def weight_grad(g, values, grads):
         dw[g][...] = dot(values, grads, TN).astype(BF).reshape(dw[g].shape)
+        weight_grad_send(g)
+
+    def tail_grad(h):
+        g = (B1, B2)[h]
+        n = 2 * LANES
+        dw[g][:, :, :, 0:n] = dot(flat(n2), tail_gate_up[h][...], TN).astype(BF).reshape(ZN, 4, d_rows, n)
+        dw[g][:, :, :, n:] = dot(flat(sd), tail_act[h][...], TN).astype(BF).reshape(ZN, 4, d_rows, LANES)
+        weight_grad_send(g)
+
+    def weight_grad_send(g):
         for xx in (1 - x, x):
-            send(None, dw[g].at[:, 2 * xx + 1 - c], rc[g].at[xx], gc_s.at[g], gc_r.at[g, xx], sibling)
+            send(used(g), dw[g].at[:, 2 * xx + 1 - c], rc[g].at[xx], gc_s.at[g], gc_r.at[g, xx], sibling)
 
     def reduce_across(g):
-        arrived(rc[g].at[1 - x], gc_r.at[g, 1 - x])
-        for k in (2, 1, 3, 0):
+        def action():
+            arrived(rc[g].at[1 - x], gc_r.at[g, 1 - x])
+            for k in (2, 1, 3, 0):
+                zz = hop(k)
+                sx[g][zz] = (dw[g][zz, 2 * (1 - x) + c].astype(F32) + rc[g][1 - x, zz].astype(F32)).astype(BF)
+                send(None, sx[g].at[zz], rx[g].at[zz], gx_s.at[g], gx_r.at[g, zz], across)
+
+        where_used(g, action)
+
+    def reduce_column(g, k):
+        def action():
             zz = hop(k)
-            sx[g][zz] = (dw[g][zz, 2 * (1 - x) + c].astype(F32) + rc[g][1 - x, zz].astype(F32)).astype(BF)
-            send(None, sx[g].at[zz], rx[g].at[zz], gx_s.at[g], gx_r.at[g, zz], across)
-
-    def reduce_column(g, k):
-        zz = hop(k)
-        if k == 2:
-            arrived(rc[g].at[x], gc_r.at[g, x])
-        arrived(rx[g].at[zz], gx_r.at[g, zz])
-        total = dw[g][zz, 2 * x + c].astype(F32) + rc[g][x, zz].astype(F32) + rx[g][zz].astype(F32)
-        if k:
-            rx[g][zz] = total.astype(BF)
-            send(None, rx[g].at[zz], fi[g].at[z], gf_s.at[g], gf_r.at[g], dev(zz, x, c, y))
+            if k == 2:
+                arrived(rc[g].at[x], gc_r.at[g, x])
+            arrived(rx[g].at[zz], gx_r.at[g, zz])
+            total = dw[g][zz, 2 * x + c].astype(F32) + rc[g][x, zz].astype(F32) + rx[g][zz].astype(F32)
+            if k:
+                rx[g][zz] = total.astype(BF)
+                send(None, rx[g].at[zz], fi[g].at[z], gf_s.at[g], gf_r.at[g], dev(zz, x, c, y))
+            else:
+                fi[g][z] = total.astype(BF)
+
+        where_used(g, action)
+
+    def reduce_end(g):
+        if g == B2:
+            arrived(fi[g].at[pl.ds(0, 1)], gf_r.at[g], cond=even)
+            arrived(fi[g].at[pl.ds(0, 2)], gf_r.at[g], cond=jnp.logical_not(even))
         else:
-            fi[g][z] = total.astype(BF)
-
-    def reduce_end(g):
-        arrived(fi[g].at[pl.ds(0, 3)], gf_r.at[g])
+            arrived(fi[g].at[pl.ds(0, 3)], gf_r.at[g])
         outputs[g].start()
 
     outputs = [
@@ -416,9 +486,23 @@
         sd[own_slot] = seed_rows().astype(BF)
 
     def stage_rest():
-        for g in (O, GT, UP, DN):
-            weight_inputs[g].wait()
+        for copy in weight_inputs[O:]:
+            copy.wait()
+        for g in (O, GA, UA, DA):
             stage(g)
+        for b in range(ZN):
+            stage_tail(B1, first_b1, b)
+        for b in (0, 2):
+            stage_tail(B2, first_b2, b)
+        zero_unused()
+
+    def zero_unused():
+        def zero_weights():
+            w[B2][...] = jnp.zeros_like(w[B2])
+
+        pl.when(jnp.logical_not(even))(zero_weights)
+        for b in (1, 3):
+            fi[B2][b] = jnp.zeros(fi[B2].shape[1:], BF)
 
     bl = LANES
     r_at = lax.broadcasted_iota(jnp.int32, (bl, bl), 0)
@@ -477,34 +561,83 @@
     def heads_back():
         return sum(dot(heads_grad[g][...], w[g][...], NT) for g in (Q, K, V))
 
-    def gate_rows():
-        gate[...] = choose(dot(flat(n2), w[GT][...]))
-
-    def up_rows():
-        up[...] = choose(dot(flat(n2), w[UP][...]))
+    def choose_tail(one, two):
+        count = one.shape[0]
+        m = jnp.broadcast_to(set_mask[1, :, 0:LANES].astype(F32)[None], (count // 16, 16, LANES)).reshape(count, LANES)
+        first = jnp.where(lower_lanes(one), one, swap_halves(two))
+        second = jnp.where(lower_lanes(one), swap_halves(one), two)
+        return jnp.where(m > 0.5, second, first)
+
+    def split_tail(v):
+        count = v.shape[0]
+        turned = swap_halves(v)
+        m0, m1 = [
+            jnp.broadcast_to(set_mask[s, :, 0:LANES].astype(F32)[None], (count // 16, 16, LANES)).reshape(count, LANES)
+            for s in range(2)
+        ]
+        one = jnp.where(lower_lanes(v), v * m0, turned * m1)
+        two = jnp.where(lower_lanes(v), turned * m0, v * m1)
+        return one.astype(BF), two.astype(BF)
+
+    def gate_up_rows():
+        gate[0][...] = choose(dot(flat(n2), w[GA][...]))
+        up[0][...] = choose(dot(flat(n2), w[UA][...]))
+
+    def gate_up_tail():
+        one = dot(flat(n2), w[B1][:, 0:2 * LANES])
+        two = dot(flat(n2), w[B2][:, 0:2 * LANES])
+        gate[1][...] = choose_tail(one[:, 0:LANES], two[:, 0:LANES])
+        up[1][...] = choose_tail(one[:, LANES:], two[:, LANES:])
 
     def active_rows():
-        v = gate[...]
-        act2[...] = both_sets((v * jax.nn.sigmoid(v) * up[...]).astype(BF))
+        v = gate[0][...]
+        act2[...] = both_sets((v * jax.nn.sigmoid(v) * up[0][...]).astype(BF))
+
+    def active_tail():
+        v = gate[1][...]
+        for h, tile in enumerate(split_tail(v * jax.nn.sigmoid(v) * up[1][...])):
+            tail_act[h][...] = tile
+
+    def active_dot():
+        active_grad[0][...] = choose(dot(flat(sd), w[DA][...]))
+
+    def active_dot_tail():
+        active_grad[1][...] = choose_tail(dot(flat(sd), w[B1][:, 2 * LANES:]), dot(flat(sd), w[B2][:, 2 * LANES:]))
+
+    def gate_up_grads(h):
+        v = gate[h][...]
+        sig = jax.nn.sigmoid(v)
+        g = active_grad[h][...]
+        return g * up[h][...] * sig * (1.0 + v * (1.0 - sig)), g * (v * sig)
 
     def active_back():
-        active_grad = choose(dot(flat(sd), w[DN][...]))
-        v = gate[...]
-        sig = jax.nn.sigmoid(v)
-        gate_grad[...] = both_sets((active_grad * up[...] * sig * (1.0 + v * (1.0 - sig))).astype(BF))
-        up_grad[...] = both_sets((active_grad * (v * sig)).astype(BF))
+        first, second = gate_up_grads(0)
+        gate_grad[...] = both_sets(first.astype(BF))
+        up_grad[...] = both_sets(second.astype(BF))
+
+    def active_back_tail():
+        first, second = gate_up_grads(1)
+        for h, (g_tile, u_tile) in enumerate(zip(split_tail(first), split_tail(second))):
+            tail_gate_up[h][:, 0:LANES] = g_tile
+            tail_gate_up[h][:, LANES:] = u_tile
 
     def feed_back():
-        return dot(gate_grad[...], w[GT][...], NT) + dot(up_grad[...], w[UP][...], NT)
+        return dot(gate_grad[...], w[GA][...], NT) + dot(up_grad[...], w[UA][...], NT)
+
+    def feed_back_tail():
+        return sum(dot(tail_gate_up[h][...], w[g][:, 0:2 * LANES], NT) for h, g in enumerate((B1, B2)))
 
     def feed_out():
-        return dot(act2[...], w[DN][...], NT)
+        tail = sum(dot(tail_act[h][...], w[g][:, 2 * LANES:], NT) for h, g in enumerate((B1, B2)))
+        return dot(act2[...], w[DA][...], NT) + tail
 
     def set_sums(v, at):
         three = v.reshape(half, 16, width)
         for s in range(2):
             part = (three * set_mask[s].astype(F32)[None]).reshape(rows, width)
-            gain_col[z, at + s:at + s + 1, :] = jnp.sum(part, axis=0, keepdims=True)
+            total = jnp.sum(part, axis=0, keepdims=True)
+            for side in range(2):
+                gain_col[z, 4 * side + at + s:4 * side + at + s + 1, :] = total[:, side * width // 2:(side + 1) * width // 2]
 
     def norm_back(gradient, gain, unit, inverse):
         scaled = gradient * tile_rows(gain_full(gain))
@@ -524,7 +657,6 @@
         hidden_grad = seed_rows() + norm_back(normed_two_grad, gain_two, unit, small[2][:, 0:1])
         hgrad[...] = hidden_grad
         hl[pair_slot] = hidden_grad.astype(BF)
-        gain_col[z] = jnp.zeros((8, width), F32)
         set_sums(normed_two_grad * unit, 2)
 
     def first_norm_back(normed_one_grad):
@@ -561,222 +693,269 @@
         for j in range(1, 8):
             total = total + gain_face[j]
         gain_sum[...] = total
-        outputs[8].start()
+        outputs[len(st) + 1].start()
 
     counts_start()
-    spread(K, 2)
+    spread(K, 1)
+    spread(Q, 3)
+    spread(Q, 2)
+    spread(K, 3)
+    spread(V, 2)
+    pair_start(0, n1)
     stage_rest()
-    spread(V, 1)
-    spread(V, 3)
-    multicast(GT, 0)
+    spread(Q, 1)
+    multicast(V, 0)
+    multicast(Q, 0)
+    spread(B2, 3)
     spread(O, 2)
     spread(O, 1)
-    multicast(V, 0)
+    spread(V, 1)
+    spread(B1, 1)
+    counts_step()
     multicast(O, 0)
-    spread(Q, 3)
-    spread(Q, 1)
-    spread(K, 1)
-    spread(K, 3)
-    pair_start(0, n1)
-    multicast(Q, 0)
+    multicast(Q, 1)
+    multicast(Q, 2)
+    multicast(V, 2)
+    spread(K, 2)
+    spread(DA, 1)
+    multicast(K, 0)
+    multicast(B2, 1)
+    forward(V, 2)
+    forward(K, 0)
+    multicast(Q, 3)
+    forward(Q, 0)
+    multicast(K, 1)
+    multicast(O, 3)
+    spread(V, 3)
+    multicast(B2, 0)
+    forward(Q, 3)
+    forward(Q, 2)
+    multicast(O, 2)
+    pair_step(0, n1)
+    multicast(V, 3)
+    forward(V, 0)
+    forward(Q, 1)
+    spread(O, 3)
+    spread(UA, 1)
+    seed_here()
+    multicast(DA, 3)
+    forward(K, 1)
     multicast(K, 2)
-    counts_step()
-    multicast(DN, 0)
+    spread(DA, 3)
     multicast(V, 1)
-    spread(O, 3)
-    spread(GT, 1)
-    multicast(K, 0)
+    forward(B2, 1)
+    gather_start(1, sd)
     multicast(K, 3)
-    spread(V, 2)
-    multicast(O, 3)
-    multicast(K, 1)
     multicast(O, 1)
-    spread(GT, 3)
-    pair_step(0, n1)
-    spread(Q, 2)
-    spread(UP, 3)
-    multicast(GT, 3)
-    multicast(Q, 3)
+    weights_here(Q)
+    forward(DA, 3)
+    spread(GA, 3)
+    forward(O, 0)
+    spread(UA, 2)
+    forward(V, 1)
+    spread(B2, 2)
+    multicast(B1, 3)
+    pair_end(0, n1)
+    spread(GA, 1)
+    multicast(UA, 0)
+    spread(B1, 3)
+    forward(V, 3)
+    multicast(B1, 0)
+    gather_step(1, sd, 1)
+    spread(UA, 3)
+    multicast(DA, 1)
+    spread(B2, 1)
+    multicast(DA, 0)
     forward(O, 3)
-    multicast(V, 3)
-    spread(UP, 1)
-    forward(GT, 0)
-    multicast(O, 2)
+    forward(O, 2)
+    weights_here(V)
+    forward(B2, 0)
+    multicast(GA, 0)
+    forward(K, 3)
     forward(K, 2)
-    multicast(V, 2)
-    forward(V, 0)
-    forward(K, 0)
-    seed_here()
-    multicast(Q, 1)
+    project_heads(Q)
+    weights_here(K)
     forward(O, 1)
-    gather_start(1, sd)
-    forward(O, 2)
-    forward(K, 3)
-    multicast(Q, 2)
-    spread(UP, 2)
-    forward(Q, 3)
-    pair_end(0, n1)
-    multicast(UP, 0)
-    forward(V, 3)
-    forward(K, 1)
-    forward(O, 0)
-    multicast(UP, 3)
-    forward(DN, 0)
-    forward(Q, 0)
-    weights_here(K)
-    forward(V, 2)
-    forward(V, 1)
-    spread(DN, 1)
-    forward(Q, 1)
-    forward(Q, 2)
-    spread(DN, 3)
-    multicast(GT, 1)
     project_heads(K)
     weights_here(O)
-    weights_here(Q)
-    forward(GT, 3)
-    spread(DN, 2)
-    weights_here(V)
     project_heads(V)
-    project_heads(Q)
     attend()
     scatter_put(0, dot(att2[...], w[O][...], NT))
     pair_scatter_send(0)
-    multicast(UP, 1)
+    multicast(B2, 2)
+    multicast(GA, 3)
+    spread(GA, 2)
     pair_scatter_step(0)
-    gather_step(1, sd, 1)
+    multicast(GA, 1)
+    multicast(UA, 3)
+    multicast(B1, 1)
+    forward(B1, 0)
+    spread(DA, 2)
+    gather_step(1, sd, 2)
     attention = pair_scatter_end(0)
+    forward(DA, 0)
     second_norm(attention)
-    forward(UP, 0)
-    multicast(DN, 1)
-    forward(UP, 1)
     gather_start(2, n2)
-    forward(UP, 3)
-    multicast(UP, 2)
+    multicast(GA, 2)
+    gather_step(1, sd, 3)
+    multicast(B2, 3)
+    multicast(UA, 1)
+    spread(B1, 2)
+    forward(GA, 1)
+    multicast(UA, 2)
+    forward(UA, 0)
+    forward(B1, 1)
+    forward(B2, 2)
+    forward(B2, 3)
     gather_step(2, n2, 1)
-    multicast(DN, 3)
-    forward(DN, 1)
-    spread(GT, 2)
+    forward(UA, 3)
+    forward(GA, 3)
+    multicast(DA, 2)
+    forward(DA, 1)
+    weights_here(B2)
+    forward(UA, 1)
+    forward(GA, 2)
+    multicast(B1, 2)
+    forward(UA, 2)
+    forward(B1, 3)
     gather_step(2, n2, 2)
-    multicast(DN, 2)
+    forward(DA, 2)
+    forward(GA, 0)
+    gather_end(1, sd)
+    forward(B1, 2)
     gather_step(2, n2, 3)
-    forward(DN, 3)
-    gather_step(1, sd, 2)
-    forward(UP, 2)
-    forward(DN, 2)
-    multicast(GT, 2)
-    weights_here(UP)
-    weights_here(DN)
+    weights_here(B1)
+    weights_here(GA)
+    active_dot_tail()
+    weights_here(DA)
+    weights_here(UA)
+    active_dot()
     gather_end(2, n2)
-    up_rows()
-    forward(GT, 1)
-    gather_step(1, sd, 3)
-    forward(GT, 2)
-    weights_here(GT)
-    gate_rows()
+    gate_up_tail()
+    gate_up_rows()
     active_rows()
-    scatter_put(2, feed_out())
-    scatter_send(2, 0)
-    gather_end(1, sd)
+    active_tail()
     active_back()
+    active_back_tail()
     scatter_put(1, feed_back())
+    scatter_add(1, feed_back_tail())
     scatter_send(1, 0)
     scatter_send(1, 1)
-    scatter_step(2, 0)
-    weight_grad(GT, flat(n2), gate_grad[...])
+    weight_grad(GA, flat(n2), gate_grad[...])
+    scatter_put(2, feed_out())
+    reduce_across(GA)
     scatter_send(1, 2)
     scatter_step(1, 0)
-    scatter_step(2, 1)
-    reduce_across(GT)
+    scatter_send(1, 3)
     scatter_step(1, 1)
-    scatter_send(2, 1)
-    weight_grad(DN, flat(sd), act2[...])
-    scatter_send(1, 3)
-    scatter_step(1, 4)
-    reduce_column(GT, 2)
-    scatter_send(2, 2)
-    scatter_step(1, 2)
+    scatter_send(2, 0)
+    weight_grad(UA, flat(n2), up_grad[...])
     scatter_step(1, 5)
     scatter_send(2, 3)
-    reduce_across(DN)
-    weight_grad(UP, flat(n2), up_grad[...])
+    scatter_step(1, 4)
     scatter_step(1, 3)
+    scatter_step(1, 2)
+    reduce_column(GA, 2)
+    reduce_across(UA)
+    scatter_step(1, 6)
     scatter_step(1, 7)
-    scatter_step(1, 6)
-    scatter_step(2, 4)
-    reduce_column(DN, 2)
+    tail_grad(1)
+    weight_grad(DA, flat(sd), act2[...])
+    reduce_column(UA, 2)
+    scatter_send(2, 1)
+    reduce_across(DA)
+    scatter_step(2, 1)
+    scatter_step(2, 0)
     normed_two_grad = scatter_end(1)
-    scatter_step(2, 5)
     second_norm_back(normed_two_grad)
     pair_start(3, hl)
-    reduce_column(GT, 1)
-    reduce_across(UP)
-    reduce_column(GT, 3)
-    reduce_column(DN, 1)
-    scatter_step(2, 6)
+    reduce_column(GA, 1)
+    reduce_column(GA, 3)
+    reduce_column(DA, 2)
+    scatter_send(2, 2)
+    tail_grad(0)
+    reduce_across(B1)
+    reduce_column(UA, 1)
+    reduce_across(B2)
     pair_step(3, hl)
-    reduce_column(UP, 2)
+    reduce_column(B1, 2)
+    scatter_step(2, 3)
+    scatter_step(2, 5)
+    scatter_step(2, 4)
+    reduce_column(B1, 3)
+    scatter_step(2, 7)
+    reduce_column(B1, 0)
+    reduce_column(UA, 3)
     pair_end(3, hl)
-    scatter_step(2, 3)
-    reduce_column(UP, 1)
+    reduce_column(B2, 2)
+    reduce_column(DA, 3)
+    scatter_step(2, 2)
     weight_grad(O, flat(hl), att2[...])
+    reduce_column(B2, 3)
+    reduce_column(B1, 1)
+    reduce_across(O)
     attend_back()
     weight_grad(V, flat(n1), heads_grad[V][...])
-    reduce_column(UP, 3)
+    weight_grad(K, flat(n1), heads_grad[K][...])
+    scatter_step(2, 6)
+    reduce_column(O, 2)
     scatter_put(3, heads_back())
     reduce_across(V)
-    scatter_step(2, 2)
-    reduce_column(DN, 3)
+    reduce_column(O, 3)
+    reduce_column(O, 1)
     pair_scatter_send(3)
+    output_rows(scatter_end(2))
+    reduce_column(V, 2)
     weight_grad(Q, flat(n1), heads_grad[Q][...])
-    weight_grad(K, flat(n1), heads_grad[K][...])
-    reduce_column(V, 2)
-    reduce_column(DN, 0)
     reduce_across(K)
-    reduce_across(Q)
     pair_scatter_step(3)
+    half_send(0)
+    reduce_column(DA, 1)
+    reduce_column(B2, 1)
+    reduce_column(DA, 0)
     reduce_column(V, 1)
-    reduce_column(K, 2)
-    reduce_column(K, 1)
-    scatter_step(2, 7)
-    reduce_column(V, 3)
-    reduce_column(Q, 2)
-    reduce_column(GT, 0)
-    reduce_across(O)
+    reduce_column(GA, 0)
     normed_one_grad = pair_scatter_end(3)
     first_norm_back(normed_one_grad)
+    reduce_column(K, 2)
+    reduce_column(V, 3)
+    reduce_column(B2, 0)
+    reduce_column(K, 3)
+    reduce_across(Q)
+    reduce_column(UA, 0)
     gains_start()
-    reduce_column(UP, 0)
-    reduce_end(UP)
-    reduce_column(K, 3)
+    reduce_end(UA)
+    reduce_end(DA)
+    half_end(0)
+    reduce_end(GA)
     reduce_column(V, 0)
+    reduce_end(B1)
+    reduce_column(K, 1)
+    half_send(1)
+    reduce_column(O, 0)
+    reduce_column(Q, 2)
+    reduce_column(Q, 3)
     reduce_end(V)
-    reduce_column(O, 2)
-    half_send(1)
     reduce_column(Q, 1)
-    output_rows(scatter_end(2))
-    reduce_column(Q, 3)
+    reduce_column(Q, 0)
     reduce_column(K, 0)
+    half_end(1)
+    reduce_end(B2)
+    reduce_end(O)
+    gains_step()
+    gains_end()
     reduce_end(K)
-    half_send(0)
-    reduce_column(O, 1)
-    gains_step()
-    reduce_column(O, 3)
-    reduce_end(GT)
-    half_end(1)
-    half_end(0)
-    reduce_end(DN)
-    reduce_column(Q, 0)
     reduce_end(Q)
-    gains_end()
-    reduce_column(O, 0)
-    reduce_end(O)
-    outputs[7].start()
-    for g in range(len(weights)):
-        sent(w[g].at[pl.ds(0, 15 * d_rows), :], wt_s.at[g])
-        sent(dw[g].at[:, pl.ds(0, 2)], gc_s.at[g])
-        sent(sx[g], gx_s.at[g])
-        sent(rx[g].at[pl.ds(0, 3)], gf_s.at[g])
+    outputs[len(st)].start()
+    for g in range(len(st)):
+        if g == B2:
+            sent(w[g].at[pl.ds(0, 13 * d_rows), :], wt_s.at[g], cond=even)
+            sent(w[g].at[pl.ds(0, 2 * d_rows), :], wt_s.at[g], cond=jnp.logical_not(even))
+        else:
+            sent(w[g].at[pl.ds(0, 15 * d_rows), :], wt_s.at[g])
+        sent(dw[g].at[:, pl.ds(0, 2)], gc_s.at[g], cond=used(g))
+        sent(sx[g], gx_s.at[g], cond=used(g))
+        sent(rx[g].at[pl.ds(0, 3)], gf_s.at[g], cond=used(g))
     for which, buf in ((1, sd), (2, n2)):
         sent(buf.at[pl.ds(0, 4)], ag_s.at[which, 0])
         sent(buf.at[pl.ds(0, 1)], ag_s.at[which, 1], cond=(z == 0) | (z == ZN - 1))
@@ -798,64 +977,99 @@
 
 
 def output_kernel(
-    fi, halves, gains,
-    mixed, frames_grad, dq, dk, dv, do, dg, du, dd, first_gain, second_gain,
+    fi_in, halves_in, gains_in,
+    mixed_out, frames_grad_out, grads_out, first_out, second_out,
+    fi, halves, gains, grads, first_gain, second_gain, in_s, out_s,
 ):
     inner = lax.rem(lax.axis_index("dp"), INNER)
-    mixed[...] = halves[0]
-    frames_grad[...] = halves[1]
-    outs = (dq, dk, dv, do, dg, du, dd)
-    for g, n in enumerate(chip_columns([ref.shape[2] for ref in outs])):
-        for b in range(BLOCKS[g]):
-            here = min(n, outs[g].shape[2] - b * n)
+    order = (B1, B2, GA, UA, DA, Q, K, V, O)
+    copies = {
+        g: pltpu.make_async_copy(src, dst, in_s.at[g])
+        for g, (src, dst) in enumerate(zip(tuple(fi_in) + (halves_in, gains_in), tuple(fi) + (halves, gains)))
+    }
+    for g in order + (len(order), len(order) + 1):
+        copies[g].start()
+    leaving = []
+
+    def leave(src, dst):
+        leaving.append(pltpu.make_async_copy(src, dst, out_s.at[len(leaving)]))
+        leaving[-1].start()
+
+    units = grads[FEED[0]].shape[2]
+    _, first_b1, first_b2 = feed_columns(units)
+    copies[B1].wait()
+    copies[B2].wait()
+    for g, weight in ((GA, 4), (UA, 5), (DA, 6), (Q, 0), (K, 1), (V, 2), (O, 3)):
+        copies[g].wait()
+        out = grads[weight]
+        blocks = ATTENTION_BLOCKS if g <= O else ZN
+        n = fi[g].shape[2] // 2
+        for b in range(blocks):
             for s in range(2):
-                lanes = slice(s * n, s * n + here)
-                parts = [fi[g][other, :, lanes].astype(F32) for other in range(b, ZN, BLOCKS[g])]
-                outs[g][s, :, b * n:b * n + here] = sum(parts)
-    width = gains.shape[1]
+                parts = [fi[g][other, :, s * n:(s + 1) * n].astype(F32) for other in range(b, ZN, blocks)]
+                out[s, :, b * n:(b + 1) * n] = sum(parts)
+        if weight in FEED:
+            m = FEED.index(weight)
+            lanes = slice(m * LANES, (m + 1) * LANES)
+            for tail, first, pair in ((B1, first_b1, (0, 1)), (B1, first_b1 + LANES, (2, 3)), (B2, first_b2, (0, 2))):
+                one, two = [fi[tail][b, :, lanes].astype(F32) for b in pair]
+                out[0, :, first:first + LANES] = jnp.where(lower_lanes(one), one, swap_halves(two))
+                out[1, :, first:first + LANES] = jnp.where(lower_lanes(one), swap_halves(one), two)
+        leave(out, grads_out[weight])
+    copies[len(order)].wait()
+    leave(halves.at[0], mixed_out)
+    leave(halves.at[1], frames_grad_out)
+    copies[len(order) + 1].wait()
+    width = 2 * gains.shape[1]
     share = first_gain.shape[1]
-    turned = pltpu.roll(gains[...], lax.rem(width - inner * share, width), 1)
+    whole = jnp.concatenate([gains[0:4, :], gains[4:8, :]], axis=1)
+    turned = pltpu.roll(whole, lax.rem(width - inner * share, width), 1)
     first_gain[...] = turned[0:2, 0:share]
     second_gain[...] = turned[2:4, 0:share]
+    leave(first_gain, first_out)
+    leave(second_gain, second_out)
+    for copy in leaving:
+        copy.wait()
 
 
 def run_layer(frames, cot, dialogue, padding, position_set, gain_one, gain_two, weights):
     width = frames.shape[2]
     rows = frames.shape[0] * frames.shape[1] // 2
     d_rows = weights[0].shape[1]
-    sizes = chip_columns([v.shape[2] for v in weights])
-    count = len(sizes)
+    lanes = group_lanes(weights[0].shape[2], weights[FEED[0]].shape[2])
+    count = len(lanes)
     group, pair_group = 8 * rows, 4 * rows
     dma = pltpu.SemaphoreType.DMA
     vm = pltpu.VMEM
     shape = jax.ShapeDtypeStruct
     block_rows, pair_rows = (8, rows, width), (4, rows, width)
     four = (4, 4, rows, width)
-    own = [(ZN, d_rows, 2 * n) for n in sizes]
-    qb, fb = sizes[Q], sizes[GT]
+    own = [(ZN, d_rows, n) for n in lanes]
+    qb, part = lanes[Q] // 2, lanes[GA] // 2
     own_frames = (frames.shape[0] // 2,) + frames.shape[1:]
     scratch = (
         [vm(own_frames, BF)] * 2
         + [pltpu.SMEM(v.shape, v.dtype) for v in (dialogue, padding, position_set)]
         + [vm(gain_one.shape, F32)] * 2
         + [[vm(v.shape, BF) for v in weights]]
-        + [[vm((blocks, d_rows, 2 * n), BF) for blocks, n in zip(BLOCKS, sizes)]]
+        + [[vm((ATTENTION_BLOCKS if g <= O else ZN, d_rows, n), BF) for g, n in enumerate(lanes)]]
         + [[vm(v, BF) for v in own]]
-        + [[vm((width, 2 * n), BF) for n in sizes]]
-        + [[vm((ZN, 4, d_rows, 2 * n), BF) for n in sizes]]
-        + [[vm((2, ZN, d_rows, 2 * n), BF) for n in sizes]]
+        + [[vm((width, n), BF) for n in lanes]]
+        + [[vm((ZN, 4, d_rows, n), BF) for n in lanes]]
+        + [[vm((2, ZN, d_rows, n), BF) for n in lanes]]
         + [[vm(v, BF) for v in own]] * 3
         + [vm((2, 16, width), BF)]
         + [vm(pair_rows, BF), vm(block_rows, BF), vm(block_rows, BF), vm(pair_rows, BF)] + [vm((2,) + block_rows, F32)]
         + [vm(four, BF)] * 5
         + [[vm((pair_group, qb), BF)] * 3, [vm((pair_group, 2 * qb), BF)] * 3, vm((pair_group, 2 * qb), BF)]
         + [vm((pair_group // LANES, qb // HDIM, LANES, LANES), F32)]
-        + [vm((group, fb), F32)] * 2
-        + [vm((group, 2 * fb), BF)] * 3
-        + [vm((2, 4, 8, LANES), F32), vm((ZN, 8, width), F32), vm((8, 8, width), F32), vm((8, width), F32)]
+        + [[vm((group, n), F32) for n in (part, LANES)]] * 3
+        + [vm((group, 2 * part), BF)] * 3
+        + [[vm((group, 2 * LANES), BF)] * 2, [vm((group, LANES), BF)] * 2]
+        + [vm((2, 4, 8, LANES), F32), vm((ZN, 8, width // 2), F32), vm((8, 8, width // 2), F32), vm((8, width // 2), F32)]
         + [vm((2,) + frames.shape, BF)]
         + [vm((rows, width), F32)] * 4 + [vm((3, rows, LANES), F32)]
-        + [dma((7 + count,)), dma((2 + count,))]
+        + [dma((7 + len(weights),)), dma((2 + count,))]
         + [dma((count,)), dma((count, 3)), dma((count, 4)), dma((count,))]
         + [dma((4, 2)), dma((2, 8, CUTS)), dma((2, 4, CUTS))]
         + [dma((4,)), dma((2, 4, CUTS)), dma((2, 2, CUTS)), dma((4,)), dma((2, 4, CUTS)), dma((2, 4, CUTS)), dma((2, CUTS))]
@@ -863,11 +1077,10 @@
         + [dma((2,))] * 6
     )
     any_place = pl.BlockSpec(memory_space=pl.ANY)
-    spec = pl.BlockSpec(memory_space=pltpu.VMEM)
     packed = pl.pallas_call(
         layer_kernel,
-        out_shape=[[shape(v, BF) for v in own], shape((2,) + frames.shape, BF), shape((8, width), F32)],
-        in_specs=[any_place] * 7 + [[any_place] * count],
+        out_shape=[[shape(v, BF) for v in own], shape((2,) + frames.shape, BF), shape((8, width // 2), F32)],
+        in_specs=[any_place] * 7 + [[any_place] * len(weights)],
         out_specs=[[any_place] * count, any_place, any_place],
         scratch_shapes=scratch,
         compiler_params=pltpu.CompilerParams(
@@ -877,15 +1090,22 @@
         name="layer",
     )(frames, cot, dialogue, padding, position_set, gain_one, gain_two, list(weights))
     grads = [shape(v.shape, F32) for v in weights]
-    return pl.pallas_call(
+    gain = shape((2, d_rows), F32)
+    mixed, frames_grad, grads, first_gain, second_gain = pl.pallas_call(
         output_kernel,
-        out_shape=[shape(frames.shape, BF)] * 2 + grads + [shape((2, d_rows), F32)] * 2,
-        in_specs=[[spec] * count, spec, spec],
-        out_specs=[spec] * 11,
+        out_shape=[shape(frames.shape, BF), shape(frames.shape, BF), grads, gain, gain],
+        in_specs=[[any_place] * count, any_place, any_place],
+        out_specs=[any_place, any_place, [any_place] * len(grads), any_place, any_place],
+        scratch_shapes=[
+            [vm(v, BF) for v in own], vm((2,) + frames.shape, BF), vm((8, width // 2), F32),
+            [vm(v.shape, F32) for v in weights], vm(gain.shape, F32), vm(gain.shape, F32),
+            dma((count + 2,)), dma((len(grads) + 4,)),
+        ],
         compiler_params=pltpu.CompilerParams(vmem_limit_bytes=63 * 2**20),
         cost_estimate=pl.CostEstimate(flops=10**6, bytes_accessed=10**7, transcendentals=0),
         name="outputs",
     )(*packed)
+    return mixed, frames_grad, *grads, first_gain, second_gain
 
 
 def per_device(

time: 161 us -> 156 us (0.969)
  Pallas kernels: 160 us -> 155 us
    pallas_call x1, Pallas kernels: 157 us -> 151 us  [run_layer(): pl.pallas_call(layer_kernel, out_shape=[[shape(v, BF) for v in own], shap...]
where the time goes in v5:
time: 156 us; the launch traced here: 155 us
  Pallas kernels  155 us (99%)
    pallas_call x1, Pallas kernels, run_layer(): pl.pallas_call(layer_kernel, out_shape=[[shape(v, BF) for v in own], shap...  151 us
    pallas_call x1, Pallas kernels, run_layer(): pl.pallas_call(output_kernel, out_shape=[shape(frames.shape, BF), shape(f...  3.3 us

profile of v5, /device:TPU:0, one launch (start us, length us, event | category | flops | bytes accessed | tf_op | source)
XLA Modules:
  0.0 155.4 jit_solution(14849150924016326351)
XLA Ops:
  0.6 151.3 %layer.1 = (bf16[4,64,512]{2,1,0:T(8,128)(2,1)}, bf16[4,64,512]{2,1,0:T(8,128)(2,1)}, bf16[4,64,512]{2,1,0:T(8,128)(2,1)}, bf16[4,64,512]{2,1,0:T(8,128)(2,1)}, ...) custom-call(bf16[8,16,1024]{2,1,0:T(8,128)(2,1)} %frames_in.1, ...), custom_call_target="tpu_custom_call" | custom-call | flops 10000000000 | bytes 10000000 | tf_op jit(solution)/shard_map/layer/pallas_call | solution.py:1080
  152.0 3.3 %outputs.1 = (bf16[8,16,1024]{2,1,0:T(8,128)(2,1)}, bf16[8,16,1024]{2,1,0:T(8,128)(2,1)}, f32[2,64,512]{2,1,0:T(8,128)}, f32[2,64,512]{2,1,0:T(8,128)}, f32[2,64...) custom-call(bf16[4,64,512]{2,1,0:T(8,128)(2,1)} %get-tuple-element.3, ...), custom_call_target="tpu_custom_call" | custom-call | flops 1000000 | bytes 10000000 | tf_op jit(solution)/shard_map/outputs/pallas_call | solution.py:1094

commit v6 on v5

--- a/solution.py
+++ b/solution.py
@@ -696,256 +696,256 @@
         outputs[len(st) + 1].start()
 
     counts_start()
+    spread(Q, 1)
+    spread(Q, 2)
+    stage_rest()
     spread(K, 1)
+    spread(K, 3)
+    multicast(Q, 3)
+    counts_step()
+    spread(O, 3)
+    multicast(Q, 0)
+    multicast(K, 0)
+    multicast(DA, 0)
+    spread(K, 2)
+    spread(V, 1)
+    pair_start(0, n1)
+    spread(V, 2)
+    multicast(V, 0)
+    forward(Q, 0)
+    spread(O, 1)
+    multicast(O, 1)
+    spread(B2, 3)
+    forward(DA, 0)
+    multicast(B1, 0)
+    seed_here()
+    multicast(K, 1)
     spread(Q, 3)
-    spread(Q, 2)
-    spread(K, 3)
-    spread(V, 2)
-    pair_start(0, n1)
-    stage_rest()
-    spread(Q, 1)
-    multicast(V, 0)
-    multicast(Q, 0)
-    spread(B2, 3)
     spread(O, 2)
-    spread(O, 1)
-    spread(V, 1)
-    spread(B1, 1)
-    counts_step()
-    multicast(O, 0)
-    multicast(Q, 1)
+    forward(Q, 3)
+    spread(V, 3)
+    forward(V, 0)
+    forward(O, 1)
+    pair_step(0, n1)
+    gather_start(1, sd)
+    multicast(K, 3)
+    multicast(K, 2)
+    spread(UA, 3)
     multicast(Q, 2)
     multicast(V, 2)
-    spread(K, 2)
+    forward(K, 3)
+    spread(B2, 1)
+    multicast(Q, 1)
+    multicast(O, 0)
+    multicast(O, 2)
+    forward(K, 0)
+    spread(B2, 2)
+    spread(GA, 1)
+    spread(DA, 3)
+    forward(K, 2)
+    multicast(O, 3)
+    multicast(B2, 0)
+    forward(V, 2)
+    spread(B1, 3)
+    multicast(V, 3)
+    forward(K, 1)
     spread(DA, 1)
-    multicast(K, 0)
+    forward(Q, 2)
+    forward(Q, 1)
+    multicast(V, 1)
+    weights_here(Q)
+    pair_end(0, n1)
+    spread(B1, 2)
+    forward(O, 2)
+    spread(UA, 1)
+    gather_step(1, sd, 1)
+    forward(B1, 0)
+    project_heads(Q)
+    forward(O, 3)
+    multicast(UA, 1)
+    weights_here(K)
+    forward(O, 0)
+    forward(V, 3)
+    forward(V, 1)
+    project_heads(K)
+    weights_here(V)
+    project_heads(V)
+    spread(GA, 3)
+    attend()
+    spread(GA, 2)
+    spread(B1, 1)
+    weights_here(O)
+    multicast(B2, 2)
+    multicast(DA, 1)
+    multicast(UA, 0)
+    scatter_put(0, dot(att2[...], w[O][...], NT))
+    multicast(GA, 0)
+    pair_scatter_send(0)
+    pair_scatter_step(0)
+    forward(B2, 0)
+    multicast(B2, 3)
+    forward(UA, 1)
+    multicast(B1, 1)
     multicast(B2, 1)
-    forward(V, 2)
-    forward(K, 0)
-    multicast(Q, 3)
-    forward(Q, 0)
-    multicast(K, 1)
-    multicast(O, 3)
-    spread(V, 3)
-    multicast(B2, 0)
-    forward(Q, 3)
-    forward(Q, 2)
-    multicast(O, 2)
-    pair_step(0, n1)
-    multicast(V, 3)
-    forward(V, 0)
-    forward(Q, 1)
-    spread(O, 3)
-    spread(UA, 1)
-    seed_here()
-    multicast(DA, 3)
-    forward(K, 1)
-    multicast(K, 2)
-    spread(DA, 3)
-    multicast(V, 1)
-    forward(B2, 1)
-    gather_start(1, sd)
-    multicast(K, 3)
-    multicast(O, 1)
-    weights_here(Q)
-    forward(DA, 3)
-    spread(GA, 3)
-    forward(O, 0)
-    spread(UA, 2)
-    forward(V, 1)
-    spread(B2, 2)
-    multicast(B1, 3)
-    pair_end(0, n1)
-    spread(GA, 1)
-    multicast(UA, 0)
-    spread(B1, 3)
-    forward(V, 3)
-    multicast(B1, 0)
-    gather_step(1, sd, 1)
-    spread(UA, 3)
-    multicast(DA, 1)
-    spread(B2, 1)
-    multicast(DA, 0)
-    forward(O, 3)
-    forward(O, 2)
-    weights_here(V)
-    forward(B2, 0)
-    multicast(GA, 0)
-    forward(K, 3)
-    forward(K, 2)
-    project_heads(Q)
-    weights_here(K)
-    forward(O, 1)
-    project_heads(K)
-    weights_here(O)
-    project_heads(V)
-    attend()
-    scatter_put(0, dot(att2[...], w[O][...], NT))
-    pair_scatter_send(0)
-    multicast(B2, 2)
-    multicast(GA, 3)
-    spread(GA, 2)
-    pair_scatter_step(0)
-    multicast(GA, 1)
-    multicast(UA, 3)
-    multicast(B1, 1)
-    forward(B1, 0)
     spread(DA, 2)
+    multicast(B1, 2)
     gather_step(1, sd, 2)
     attention = pair_scatter_end(0)
-    forward(DA, 0)
+    forward(B1, 1)
     second_norm(attention)
+    multicast(UA, 3)
+    multicast(DA, 3)
     gather_start(2, n2)
+    spread(UA, 2)
     multicast(GA, 2)
+    forward(B2, 3)
+    multicast(GA, 1)
+    forward(DA, 1)
     gather_step(1, sd, 3)
-    multicast(B2, 3)
-    multicast(UA, 1)
-    spread(B1, 2)
-    forward(GA, 1)
+    multicast(B1, 3)
+    forward(UA, 0)
+    multicast(GA, 3)
+    multicast(DA, 2)
+    gather_step(2, n2, 1)
+    forward(GA, 2)
+    forward(B1, 2)
     multicast(UA, 2)
-    forward(UA, 0)
-    forward(B1, 1)
+    forward(B2, 1)
     forward(B2, 2)
-    forward(B2, 3)
-    gather_step(2, n2, 1)
-    forward(UA, 3)
-    forward(GA, 3)
-    multicast(DA, 2)
-    forward(DA, 1)
-    weights_here(B2)
-    forward(UA, 1)
-    forward(GA, 2)
-    multicast(B1, 2)
-    forward(UA, 2)
     forward(B1, 3)
     gather_step(2, n2, 2)
+    gather_end(1, sd)
+    forward(DA, 3)
     forward(DA, 2)
     forward(GA, 0)
-    gather_end(1, sd)
-    forward(B1, 2)
+    forward(GA, 3)
     gather_step(2, n2, 3)
+    forward(UA, 2)
+    weights_here(B2)
     weights_here(B1)
+    forward(GA, 1)
+    weights_here(DA)
+    active_dot()
+    forward(UA, 3)
+    active_dot_tail()
     weights_here(GA)
-    active_dot_tail()
-    weights_here(DA)
     weights_here(UA)
-    active_dot()
     gather_end(2, n2)
+    gate_up_rows()
     gate_up_tail()
-    gate_up_rows()
+    active_tail()
+    active_back_tail()
     active_rows()
-    active_tail()
     active_back()
-    active_back_tail()
     scatter_put(1, feed_back())
     scatter_add(1, feed_back_tail())
     scatter_send(1, 0)
     scatter_send(1, 1)
-    weight_grad(GA, flat(n2), gate_grad[...])
+    scatter_send(1, 2)
+    weight_grad(DA, flat(sd), act2[...])
     scatter_put(2, feed_out())
-    reduce_across(GA)
-    scatter_send(1, 2)
-    scatter_step(1, 0)
+    reduce_across(DA)
     scatter_send(1, 3)
     scatter_step(1, 1)
+    scatter_step(1, 0)
+    tail_grad(1)
     scatter_send(2, 0)
+    scatter_step(1, 2)
+    scatter_step(1, 3)
+    scatter_step(1, 4)
+    scatter_step(1, 5)
+    reduce_across(B2)
+    scatter_send(2, 2)
+    reduce_column(DA, 2)
+    reduce_column(DA, 1)
+    tail_grad(0)
     weight_grad(UA, flat(n2), up_grad[...])
-    scatter_step(1, 5)
+    scatter_step(1, 7)
+    reduce_across(B1)
+    scatter_step(1, 6)
+    reduce_across(UA)
+    scatter_step(2, 0)
+    reduce_column(B2, 2)
+    scatter_step(2, 1)
+    normed_two_grad = scatter_end(1)
+    scatter_send(2, 1)
+    second_norm_back(normed_two_grad)
+    reduce_column(B1, 2)
+    pair_start(3, hl)
+    weight_grad(GA, flat(n2), gate_grad[...])
+    reduce_column(UA, 2)
+    scatter_step(2, 2)
+    reduce_column(B1, 3)
+    reduce_column(UA, 3)
+    reduce_across(GA)
+    pair_step(3, hl)
+    scatter_step(2, 4)
+    reduce_column(GA, 2)
+    reduce_column(B2, 3)
     scatter_send(2, 3)
-    scatter_step(1, 4)
-    scatter_step(1, 3)
-    scatter_step(1, 2)
-    reduce_column(GA, 2)
-    reduce_across(UA)
-    scatter_step(1, 6)
-    scatter_step(1, 7)
-    tail_grad(1)
-    weight_grad(DA, flat(sd), act2[...])
-    reduce_column(UA, 2)
-    scatter_send(2, 1)
-    reduce_across(DA)
-    scatter_step(2, 1)
-    scatter_step(2, 0)
-    normed_two_grad = scatter_end(1)
-    second_norm_back(normed_two_grad)
-    pair_start(3, hl)
+    scatter_step(2, 5)
+    reduce_column(UA, 1)
+    reduce_column(B1, 1)
+    scatter_step(2, 7)
+    pair_end(3, hl)
+    weight_grad(O, flat(hl), att2[...])
     reduce_column(GA, 1)
+    attend_back()
     reduce_column(GA, 3)
-    reduce_column(DA, 2)
-    scatter_send(2, 2)
-    tail_grad(0)
-    reduce_across(B1)
-    reduce_column(UA, 1)
-    reduce_across(B2)
-    pair_step(3, hl)
-    reduce_column(B1, 2)
+    scatter_step(2, 6)
+    reduce_across(O)
+    scatter_put(3, heads_back())
+    weight_grad(V, flat(n1), heads_grad[V][...])
+    reduce_column(B1, 0)
+    pair_scatter_send(3)
+    reduce_column(O, 2)
+    reduce_column(DA, 3)
+    reduce_column(UA, 0)
+    reduce_across(V)
     scatter_step(2, 3)
-    scatter_step(2, 5)
-    scatter_step(2, 4)
-    reduce_column(B1, 3)
-    scatter_step(2, 7)
-    reduce_column(B1, 0)
-    reduce_column(UA, 3)
-    pair_end(3, hl)
-    reduce_column(B2, 2)
-    reduce_column(DA, 3)
-    scatter_step(2, 2)
-    weight_grad(O, flat(hl), att2[...])
-    reduce_column(B2, 3)
-    reduce_column(B1, 1)
-    reduce_across(O)
-    attend_back()
-    weight_grad(V, flat(n1), heads_grad[V][...])
+    pair_scatter_step(3)
+    weight_grad(Q, flat(n1), heads_grad[Q][...])
+    reduce_column(O, 1)
+    reduce_column(O, 3)
+    reduce_column(V, 2)
+    reduce_across(Q)
+    reduce_column(Q, 2)
+    reduce_column(V, 3)
+    reduce_column(B2, 1)
+    reduce_column(O, 0)
+    normed_one_grad = pair_scatter_end(3)
     weight_grad(K, flat(n1), heads_grad[K][...])
-    scatter_step(2, 6)
-    reduce_column(O, 2)
-    scatter_put(3, heads_back())
-    reduce_across(V)
-    reduce_column(O, 3)
-    reduce_column(O, 1)
-    pair_scatter_send(3)
+    first_norm_back(normed_one_grad)
+    reduce_column(B2, 0)
+    reduce_column(GA, 0)
+    reduce_column(Q, 1)
+    gains_start()
     output_rows(scatter_end(2))
-    reduce_column(V, 2)
-    weight_grad(Q, flat(n1), heads_grad[Q][...])
     reduce_across(K)
-    pair_scatter_step(3)
+    reduce_column(K, 2)
+    reduce_column(V, 0)
+    reduce_column(Q, 0)
+    reduce_column(DA, 0)
+    reduce_end(UA)
+    reduce_end(B1)
+    reduce_column(V, 1)
     half_send(0)
-    reduce_column(DA, 1)
-    reduce_column(B2, 1)
-    reduce_column(DA, 0)
-    reduce_column(V, 1)
-    reduce_column(GA, 0)
-    normed_one_grad = pair_scatter_end(3)
-    first_norm_back(normed_one_grad)
-    reduce_column(K, 2)
-    reduce_column(V, 3)
-    reduce_column(B2, 0)
+    reduce_column(Q, 3)
+    reduce_end(O)
+    reduce_end(GA)
     reduce_column(K, 3)
-    reduce_across(Q)
-    reduce_column(UA, 0)
-    gains_start()
-    reduce_end(UA)
+    half_send(1)
+    reduce_column(K, 1)
+    reduce_end(B2)
+    gains_step()
+    reduce_column(K, 0)
+    half_end(0)
+    half_end(1)
+    reduce_end(Q)
+    gains_end()
     reduce_end(DA)
-    half_end(0)
-    reduce_end(GA)
-    reduce_column(V, 0)
-    reduce_end(B1)
-    reduce_column(K, 1)
-    half_send(1)
-    reduce_column(O, 0)
-    reduce_column(Q, 2)
-    reduce_column(Q, 3)
     reduce_end(V)
-    reduce_column(Q, 1)
-    reduce_column(Q, 0)
-    reduce_column(K, 0)
-    half_end(1)
-    reduce_end(B2)
-    reduce_end(O)
-    gains_step()
-    gains_end()
     reduce_end(K)
-    reduce_end(Q)
     outputs[len(st)].start()
     for g in range(len(st)):
         if g == B2:

time: 156 us -> 151 us (0.968)
  Pallas kernels: 155 us -> 150 us
    pallas_call x1, Pallas kernels: 151 us -> 146 us  [run_layer(): pl.pallas_call(layer_kernel, out_shape=[[shape(v, BF) for v in own], shap...]
where the time goes in v6:
time: 151 us
  Pallas kernels  150 us (99%)
    pallas_call x1, Pallas kernels, run_layer(): pl.pallas_call(layer_kernel, out_shape=[[shape(v, BF) for v in own], shap...  146 us
    pallas_call x1, Pallas kernels, run_layer(): pl.pallas_call(output_kernel, out_shape=[shape(frames.shape, BF), shape(f...  3.3 us

profile of v6, /device:TPU:0, one launch (start us, length us, event | category | flops | bytes accessed | tf_op | source)
XLA Modules:
  0.0 150.6 jit_solution(1443552728463690570)
XLA Ops:
  0.6 146.5 %layer.1 = (bf16[4,64,512]{2,1,0:T(8,128)(2,1)}, bf16[4,64,512]{2,1,0:T(8,128)(2,1)}, bf16[4,64,512]{2,1,0:T(8,128)(2,1)}, bf16[4,64,512]{2,1,0:T(8,128)(2,1)}, ...) custom-call(bf16[8,16,1024]{2,1,0:T(8,128)(2,1)} %frames_in.1, ...), custom_call_target="tpu_custom_call" | custom-call | flops 10000000000 | bytes 10000000 | tf_op jit(solution)/shard_map/layer/pallas_call | solution.py:1080
  147.1 3.3 %outputs.1 = (bf16[8,16,1024]{2,1,0:T(8,128)(2,1)}, bf16[8,16,1024]{2,1,0:T(8,128)(2,1)}, f32[2,64,512]{2,1,0:T(8,128)}, f32[2,64,512]{2,1,0:T(8,128)}, f32[2,64...) custom-call(bf16[4,64,512]{2,1,0:T(8,128)(2,1)} %get-tuple-element.3, ...), custom_call_target="tpu_custom_call" | custom-call | flops 1000000 | bytes 10000000 | tf_op jit(solution)/shard_map/outputs/pallas_call | solution.py:1094

commit v7 on v6

--- a/solution.py
+++ b/solution.py
@@ -10,7 +10,7 @@
 INNER = 16
 ZN = 4
 LANES = 128
-CUTS = 2
+CUTS = 4
 MESH = pl.DeviceIdType.MESH
 BF = jnp.bfloat16
 F32 = jnp.float32

time: 151 us -> 150 us (level)
  no operation moved by 1% of the time
where the time goes in v7:
time: 150 us
  Pallas kernels  149 us (99%)
    pallas_call x1, Pallas kernels, run_layer(): pl.pallas_call(layer_kernel, out_shape=[[shape(v, BF) for v in own], shap...  146 us
    pallas_call x1, Pallas kernels, run_layer(): pl.pallas_call(output_kernel, out_shape=[shape(frames.shape, BF), shape(f...  3.3 us

profile of v7, /device:TPU:0, one launch (start us, length us, event | category | flops | bytes accessed | tf_op | source)
XLA Modules:
  0.0 149.7 jit_solution(3592732929062786559)
XLA Ops:
  0.6 145.6 %layer.1 = (bf16[4,64,512]{2,1,0:T(8,128)(2,1)}, bf16[4,64,512]{2,1,0:T(8,128)(2,1)}, bf16[4,64,512]{2,1,0:T(8,128)(2,1)}, bf16[4,64,512]{2,1,0:T(8,128)(2,1)}, ...) custom-call(bf16[8,16,1024]{2,1,0:T(8,128)(2,1)} %frames_in.1, ...), custom_call_target="tpu_custom_call" | custom-call | flops 10000000000 | bytes 10000000 | tf_op jit(solution)/shard_map/layer/pallas_call | solution.py:1080
  146.2 3.3 %outputs.1 = (bf16[8,16,1024]{2,1,0:T(8,128)(2,1)}, bf16[8,16,1024]{2,1,0:T(8,128)(2,1)}, f32[2,64,512]{2,1,0:T(8,128)}, f32[2,64,512]{2,1,0:T(8,128)}, f32[2,64...) custom-call(bf16[4,64,512]{2,1,0:T(8,128)(2,1)} %get-tuple-element.3, ...), custom_call_target="tpu_custom_call" | custom-call | flops 1000000 | bytes 10000000 | tf_op jit(solution)/shard_map/outputs/pallas_call | solution.py:1094
